TPU v7x, 256 devices: a whole 4x4x8 slice. The times are simulated.
256 devices in a mesh: dp: 32 (over y_lo, z, core), fsdp: 8 (over y_hi, x).
Axes of the slice: x: 4, y: 4 (y_hi: 2, y_lo: 2; y = y_hi * 2 + y_lo), z: 8, core: 2. Of those that a mesh axis runs over, the one named last changes fastest.
Arguments:
- section_input: bfloat16 [32768, 8192], P(('dp', 'fsdp')), may hold values from -24 to 24
- c_weight: bfloat16 [8192, 512], P('fsdp'), may hold values from -0.0625 to 0.0625
- scan_input: bfloat16 [32768, 8192], P(('dp', 'fsdp')), may hold values from -6 to 6
- b_factors: bfloat16 [32768, 512], P(('dp', 'fsdp')), may hold values from -0.5 to 0.5
- step_size: float32 [128, 32768], P(None, ('dp', 'fsdp')), may hold values from 0.5 to 8
- decay_rate: float32 [128], replicated, may hold values from 0.002 to 0.06
- skip_gain: float32 [128], replicated, may hold values from 0.5 to 1.5
- out_grad: bfloat16 [32768, 8192], P(('dp', 'fsdp')), may hold values from -18 to 18
- doc_index: int32 [32768], P(('dp', 'fsdp')), may hold values from 0 to 15, as said below
- kept_rows: int32 [32, 8], P(None, 'fsdp'), may hold values from 16 to 64, as said below
- send_counts: int32 [32, 8, 32], P(None, 'fsdp'), may hold values from 0 to 2, as said below
Outputs:
- input_grad: bfloat16 [32768, 8192], P(('dp', 'fsdp'))
- scan_grad: bfloat16 [32768, 8192], P(('dp', 'fsdp'))
- readout_weight_gradient: float32 [8192, 512], P(('dp', 'fsdp'))
Inputs may be any that keep to these rules, and one draw needn't show every extreme that they name: `kept_rows`: rows kept by each device; 64 on every device whose send_counts row is not all zero. send_counts[a, f, b] rows go from dp index a to dp index b in fsdp column f; zero on the diagonal; a device that sends receives nothing; in each column one device sends exactly 2 to every device that receives, and one device receives exactly 32 rows in all, which no device exceeds; kept_rows plus the sends of a device never pass 128. `doc_index`: starts at 0 on each device and never falls within one device's 128 rows; rows of one device with equal numbers form one document.
All inputs are finite; a program needn't handle non-finite values. Where the computation divides by a largest or mean magnitude, that divisor is 1e-20 or more.
Results may differ from a plain program's by a relative error of at most 0.019.
Values may be sent and summed in bfloat16 or wider, within the bound.
No kernel may reach another device: no remote copies, remote signals or barrier semaphores. Data moves between devices by JAX's collectives and lax.ppermute only.
A program may use at most 128 MiB of HBM per device.

v0:
```python
import jax
import jax.numpy as jnp
from jax import lax
from jax.sharding import PartitionSpec as P

GROUPS = 4
STATE = 128


peak_eps = 1e-06


def scan_block(
    c_proj, b_factors, scan_input, step_size, decay_rate, skip_gain, out_grad, doc_index, live_len
):
    row_count = scan_input.shape[0]
    head_count = step_size.shape[0]
    head_width = scan_input.shape[1] // head_count
    position = jnp.arange(row_count, dtype=jnp.int32)
    live_rows = position < live_len
    grad_live = jnp.where(live_rows[:, None], out_grad, jnp.zeros_like(out_grad))
    same_doc = (doc_index[:, None] == doc_index[None, :]) & (position[None, :] <= position[:, None])
    same_doc = same_doc & live_rows[:, None] & live_rows[None, :]
    totals = jnp.cumsum(step_size * decay_rate[:, None], axis=1)
    gap_sums = totals[:, None, :] - totals[:, :, None]
    decays = jnp.exp(jnp.where(same_doc[None, :, :], gap_sums, jnp.float32(-1e30)))
    grad_heads = grad_live.reshape(row_count, head_count, head_width)
    x_heads = scan_input.reshape(row_count, head_count, head_width)
    inner_dots = jnp.einsum("thp,shp->hts", grad_heads, x_heads, preferred_element_type=jnp.float32)
    mixing = (decays * step_size[:, None, :] * inner_dots).reshape(
        GROUPS, head_count // GROUPS, row_count, row_count
    )
    mixing = mixing.sum(axis=1).astype(jnp.bfloat16)
    b_groups = b_factors.reshape(row_count, GROUPS, STATE)
    c_grad = jnp.einsum("gts,sgn->tgn", mixing, b_groups, preferred_element_type=jnp.float32)
    c_grad = c_grad.reshape(row_count, GROUPS * STATE).astype(jnp.bfloat16)
    c_groups = c_proj.reshape(row_count, GROUPS, STATE)
    affinity = jnp.einsum("tgn,sgn->gts", c_groups, b_groups, preferred_element_type=jnp.float32)
    kernel = (
        decays * jnp.repeat(affinity, head_count // GROUPS, axis=0) * step_size[:, None, :]
    ).astype(jnp.bfloat16)
    scan_grad = jnp.einsum("hts,thp->shp", kernel, grad_heads, preferred_element_type=jnp.float32)
    scan_grad = scan_grad + skip_gain[None, :, None] * grad_heads.astype(jnp.float32)
    return (c_grad, scan_grad.reshape(row_count, head_count * head_width).astype(jnp.bfloat16))


def weight_term(work_in, work_c):

    def grad_term(start, count):
        return jnp.einsum("tk,tn->kn", work_in, work_c, preferred_element_type=jnp.float32)

    return grad_term


def shards(
    section_input,
    c_weight,
    scan_input,
    b_factors,
    step_size,
    decay_rate,
    skip_gain,
    out_grad,
    doc_index,
    kept_rows,
    send_counts,
):
    dp_count = lax.axis_size("dp")
    fsdp_count = lax.axis_size("fsdp")
    dp_index = lax.axis_index("dp")
    full_rows = c_weight.shape[0] * fsdp_count
    weights = lax.all_gather(c_weight, "fsdp", axis=0, tiled=True)
    counts = send_counts[:, 0, :]
    my_sends = lax.dynamic_index_in_dim(counts, dp_index, 0, keepdims=False)
    my_kept = lax.dynamic_index_in_dim(kept_rows[:, 0], dp_index, 0, keepdims=False)
    live_len = my_kept + jnp.sum(my_sends)
    c_proj = jnp.dot(section_input, weights, preferred_element_type=jnp.float32).astype(
        jnp.bfloat16
    )
    c_grad, scan_grad = scan_block(
        c_proj,
        b_factors,
        scan_input,
        step_size,
        decay_rate,
        skip_gain,
        out_grad,
        doc_index,
        live_len,
    )
    row_grad = jnp.einsum("tn,kn->tk", c_grad, weights, preferred_element_type=jnp.float32)
    row_top = jnp.max(jnp.abs(row_grad))
    row_peak = lax.pmax(row_top, ("dp", "fsdp"))
    input_grad = (row_grad / (row_peak + peak_eps)).astype(jnp.bfloat16)
    grad_term = weight_term(section_input, c_grad)
    grad_shard = lax.psum_scatter(
        grad_term(
            jnp.int32(0), full_rows // (dp_count * fsdp_count) * lax.axis_size(("dp", "fsdp"))
        ),
        ("dp", "fsdp"),
        scatter_dimension=0,
        tiled=True,
    )
    weight_top = lax.pmax(jnp.max(jnp.abs(grad_shard)), ("dp", "fsdp"))
    readout_weight_gradient = grad_shard / (weight_top + peak_eps)
    return (input_grad, scan_grad, readout_weight_gradient)


def solution(mesh):
    placed = (
        P(("dp", "fsdp"), None),
        P("fsdp", None),
        P(("dp", "fsdp"), None),
        P(("dp", "fsdp"), None),
        P(None, ("dp", "fsdp")),
        P(),
        P(),
        P(("dp", "fsdp"), None),
        P(("dp", "fsdp")),
        P(None, "fsdp"),
        P(None, "fsdp", None),
    )
    return jax.shard_map(
        shards,
        mesh=mesh,
        in_specs=placed,
        out_specs=(P(("dp", "fsdp"), None), P(("dp", "fsdp"), None), P(("dp", "fsdp"), None)),
        check_vma=False,
    )
```

profile of v0, /device:TPU:5, one launch (start us, length us, event | category | flops | bytes accessed | tf_op | source)
XLA Modules:
  0.0 1486.9 jit_solution(13474624884625919562)
XLA Ops:
  8.0 0.0 copy-start
  8.0 0.0 all-gather.2.cloned.1.call-start
  8.1 0.7 all-gather.2.cloned.1.call-update
  8.7 0.0 reduce-scatter.4.cloned.1.call-start
  8.8 1.3 dynamic-slice_reduce_fusion
  10.1 1.2 constant_dynamic-slice_fusion
  11.3 0.9 broadcast_multiply_fusion
  12.3 0.1 copy.34
  12.4 0.2 reduce_window_sum.11
  12.5 0.1 copy.35
  13.9 3.1 broadcast_select_fusion
  17.1 4.1 copy.37
  21.2 4.1 copy.38
  25.2 0.1 fusion.14
  25.4 5.3 bitcast_reduce_fusion
  30.7 0.2 convolution_convert_fusion
  30.9 8.0 convolution_bitcast_fusion
  39.0 17.5 %copy.44 = f32[8192,512]{1,0:T(8,128)} copy(f32[8192,512]{0,1:T(8,128)} %convolution_bitcast_fusion) | data formatting | bytes 33554432
  56.5 0.0 reduce-scatter.4.cloned.1.call-update
  56.5 76.8 %all-gather.2.cloned.1.call-done = bf16[8192,512]{1,0:T(8,128)(2,1)} async-done(((bf16[1024,512]{1,0:T(8,128)(2,1)}), bf16[8192,512]{1,0:T(8,128)(2,1)}) %all-gather.2.cloned.1.call-update) | async-done | bytes 8388624 | tf_op jit(solution)/shard_map/all_gather | solution.py:72
  133.2 4.7 fusion.3
  137.9 0.2 fusion.4
  138.1 2.6 fusion.1
  140.8 2.5 fusion.2
  143.3 4.1 copy.42
  147.4 8.8 abs_reduce_fusion
  156.2 1189.3 %reduce-scatter.4.cloned.1.call-done = f32[32,512]{1,0:T(8,128)} async-done(((f32[8192,512]{1,0:T(8,128)}), f32[32,512]{1,0:T(8,128)}) %reduce-scatter.4.cloned.1.call-update) | async-done | bytes 65552
  1345.5 1.0 copy.45
  1346.5 0.7 abs_reduce_fusion.1
  1347.2 126.4 %all-reduce = (f32[]{:T(128)}, f32[]{:T(128)}) all-reduce(f32[]{:T(128)} %get-tuple-element.14, f32[]{:T(128)} %abs_reduce_fusion.1), channel_id=1, replica_groups=mesh['dp'=32,'fsdp'=8] {'dp','fsdp'}, use_global_device_ids=true, to_apply=%region_4.5 | all-reduce | flops 2 | bytes 16 | tf_op jit(solution)/shard_map/pmax | solution.py:93
  1474.9 0.7 copy.43
  1475.6 3.8 divide_convert_fusion
  (13 shorter events, 0.1 us)
Async XLA Ops:
  8.0 22.9 %copy-start = (bf16[128,8192]{1,0:T(8,128)(2,1)S(1)}, bf16[128,8192]{1,0:T(8,128)(2,1)}, u32[]{:S(2)}) copy-start(bf16[128,8192]{1,0:T(8,128)(2,1)} %param.11) | copy-start | bytes 6291460
  8.0 125.2 %all-gather.2.cloned.1.call-start = ((), (), s32[]{:S(2)}) async-start(), calls=%async_computation.1 | async-start | bytes 9437184 | tf_op jit(solution)/shard_map/all_gather | solution.py:72
  8.7 1336.8 %reduce-scatter.4.cloned.1.call-start = ((), (), s32[]{:S(2)}) async-start(), calls=%async_computation.2 | async-start | bytes 16842752
  17.1 8.2 copy-start.4
  17.1 8.3 copy-start.3
  25.4 5.3 copy-start.2
  137.9 2.9 copy-start.1
  137.9 2.9 copy-start.5
Sparse Core Ops, SparseCore 0:
  11.5 121.7 all-gather.1
Sparse Core Ops, SparseCore 1:
  56.6 1288.9 reduce-scatter.3
where the time goes:
time: 1490 us
  waiting for transfers between devices  1270 us (85%)
  blocking collectives  126 us (8%)
  local copies, waits for them, and re-layouts  32.9 us (2%)
  matrix products  29.8 us (2%)
  between operations  18.3 us (1%)
    unnamed x3, waiting for transfers between devices  1190 us
    pmax x1, blocking collectives, shards(): row_peak = lax.pmax(row_top, ('dp', 'fsdp'))  126 us
    all_gather x1, waiting for transfers between devices, shards(): weights = lax.all_gather(c_weight, 'fsdp', axis=0, tiled=True)  76.8 us
  transfers between devices with their start and end apart: 2, of which 2 were waited for; matrix products, arithmetic and copies ran while one was open for 5% of the time, Pallas kernels for 0%

commit v1 on v0

v1 whole, which is shorter than its diff:
```python
import jax
import jax.numpy as jnp
from jax import lax
from jax.experimental import pallas as pl
from jax.experimental.pallas import tpu as pltpu
from jax.sharding import PartitionSpec as P

GROUPS = 4
STATE = 128
HEADS = 128
HDIM = 64
HPG = HEADS // GROUPS
ROWS = 128
LIVE = 96
D = 8192
NARROW = GROUPS * STATE
MEMBERS = 8
CHUNK = D // MEMBERS
LOG2E = 1.4426950408889634
ALL = ("dp", "fsdp")
peak_eps = 1e-06
F32 = jnp.float32
BF16 = jnp.bfloat16


def joint(y_hi, x, y_lo, z, core):
    return (y_lo * 16 + z * 2 + core) * 8 + y_hi * 4 + x


def ring_pairs(dx, flip):
    return [
        (joint(h, x, l, z, c), joint(h ^ flip, (x + dx) % 4, l ^ flip, z, c))
        for h in (0, 1)
        for x in range(4)
        for l in (0, 1)
        for z in range(8)
        for c in (0, 1)
    ]


STEPS = [(0, 0), (1, 0), (3, 0), (2, 0), (0, 1), (1, 1), (3, 1), (2, 1)]
CORE_SWAP = [(i, i ^ 1) for i in range(32)]
SAME_CORE = [[l * 16 + z * 2 + c for l in (0, 1) for z in range(8)] for c in (0, 1)]


def move(value, step):
    return lax.ppermute(value, ALL, ring_pairs(*step))


def pack_kernel(f_ref, s_ref, *out_refs):
    lane = lax.broadcasted_iota(jnp.int32, (LIVE, 128), 1) // 32
    for m, out_ref in enumerate(out_refs):
        f = f_ref[m]
        high, low = f // 4, f % 4

        def tile(o, _):
            acc = None
            for j in range(4):
                start = pl.multiple_of((o * 4 + j) * 256 + high * 128, 128)
                piece = s_ref[:, pl.ds(start, 128)].astype(F32)
                piece = pltpu.roll(piece, (j - low + 4) % 4 * 32, 1)
                acc = piece if acc is None else jnp.where(lane == j, piece, acc)
            out_ref[:, pl.ds(pl.multiple_of(o * 128, 128), 128)] = acc.astype(BF16)
            return 0

        lax.fori_loop(0, CHUNK // 128, tile, 0)


def pack(dests, section_input):
    return pl.pallas_call(
        pack_kernel,
        grid=(1,),
        out_shape=[jax.ShapeDtypeStruct((LIVE, CHUNK), BF16)] * MEMBERS,
        in_specs=[
            pl.BlockSpec(memory_space=pltpu.SMEM),
            pl.BlockSpec((LIVE, D), lambda i: (0, 0)),
        ],
        out_specs=[pl.BlockSpec((LIVE, CHUNK), lambda i: (0, 0))] * MEMBERS,
        compiler_params=pltpu.CompilerParams(vmem_limit_bytes=32 * 2**20),
        cost_estimate=pl.CostEstimate(flops=0, bytes_accessed=4 * LIVE * D, transcendentals=0),
        name="pack",
    )(dests, section_input)


def live_count(me_ref, kept_ref, sends_ref):
    dp = me_ref[0]
    total = kept_ref[dp, 0]
    for b in range(32):
        total = total + sends_ref[dp, b]
    return total


def head_tables(q, rate_ref, step_ref, rate_scr):
    rate_scr[...] = jnp.transpose(jnp.broadcast_to(rate_ref[...], (HEADS, HEADS)))
    steps = step_ref[...]
    totals = steps * rate_scr[pl.ds(pl.multiple_of(q * HPG, HPG), HPG), :]
    lane = lax.broadcasted_iota(jnp.int32, totals.shape, 1)
    reach = 1
    while reach < ROWS:
        totals = totals + jnp.where(lane >= reach, pltpu.roll(totals, reach, 1), 0.0)
        reach *= 2
    totals = totals * LOG2E
    return totals, totals + jnp.log(steps) * LOG2E


def turned(table):
    filler = jnp.zeros((ROWS - HPG, ROWS), F32)
    return jnp.transpose(jnp.concatenate([table, filler], axis=0))


def doc_tables(doc_ref):
    along = jnp.broadcast_to(doc_ref[...].astype(F32), (ROWS, ROWS))
    return along, jnp.transpose(along)


def c_grad_kernel(
    me_ref, kept_ref, sends_ref, rate_ref, doc_ref, step_ref, g_ref, x_ref, b_ref, full_ref, out_ref, rate_scr
):
    q = pl.program_id(0)
    live = live_count(me_ref, kept_ref, sends_ref)
    totals, source = head_tables(q, rate_ref, step_ref, rate_scr)
    totals_col = turned(totals)
    along, down = doc_tables(doc_ref)
    t = lax.broadcasted_iota(jnp.int32, (LIVE, ROWS), 0)
    s = lax.broadcasted_iota(jnp.int32, (LIVE, ROWS), 1)
    keep = (along[:LIVE] == down[:LIVE]) & (s <= t) & (t < live) & (s < live)
    bias = jnp.where(keep, 0.0, -1e30).astype(F32)
    half = lax.broadcasted_iota(jnp.int32, (ROWS, 128), 1) < HDIM
    mixing = jnp.zeros((LIVE, ROWS), F32)
    for p in range(HPG // 2):
        lanes = slice(p * 128, p * 128 + 128)
        x_pair = x_ref[:, lanes]
        zero = jnp.zeros_like(x_pair)
        both = jnp.concatenate([jnp.where(half, x_pair, zero), jnp.where(half, zero, x_pair)], axis=0)
        inner = lax.dot_general(
            g_ref[:, lanes], both, (((1,), (1,)), ((), ())), preferred_element_type=F32
        )
        for k in range(2):
            h = 2 * p + k
            gap = (source[h : h + 1, :] - totals_col[:LIVE, h : h + 1]) + bias
            mixing = mixing + jnp.exp2(gap) * inner[:, k * 128 : k * 128 + 128]
    c_grad = jnp.dot(mixing.astype(BF16), b_ref[...], preferred_element_type=F32).astype(BF16)
    full_ref[:LIVE, :] = c_grad
    full_ref[LIVE:, :] = jnp.zeros((ROWS - LIVE, STATE), BF16)
    out_ref[...] = c_grad


def smem():
    return pl.BlockSpec(memory_space=pltpu.SMEM)


def row_spec():
    return pl.BlockSpec((1, 128), lambda q: (0, 0))


def c_grad_call(me, kept, sends, rate, docs, steps, out_grad, scan_input, b_factors):
    wide = HPG * HDIM
    return pl.pallas_call(
        c_grad_kernel,
        grid=(GROUPS,),
        out_shape=[
            jax.ShapeDtypeStruct((ROWS, NARROW), BF16),
            jax.ShapeDtypeStruct((LIVE, NARROW), BF16),
        ],
        in_specs=[
            smem(),
            smem(),
            smem(),
            row_spec(),
            row_spec(),
            pl.BlockSpec((HPG, ROWS), lambda q: (q, 0)),
            pl.BlockSpec((LIVE, wide), lambda q: (0, q)),
            pl.BlockSpec((ROWS, wide), lambda q: (0, q)),
            pl.BlockSpec((ROWS, STATE), lambda q: (0, q)),
        ],
        out_specs=[
            pl.BlockSpec((ROWS, STATE), lambda q: (0, q)),
            pl.BlockSpec((LIVE, STATE), lambda q: (0, q)),
        ],
        scratch_shapes=[pltpu.VMEM((HEADS, HEADS), F32)],
        compiler_params=pltpu.CompilerParams(vmem_limit_bytes=32 * 2**20),
        cost_estimate=pl.CostEstimate(
            flops=4 * LIVE * ROWS * D, bytes_accessed=4 * ROWS * D, transcendentals=HEADS * LIVE * ROWS
        ),
        name="c_grad",
    )(me, kept, sends, rate, docs, steps, out_grad, scan_input, b_factors)


def scan_grad_kernel(
    me_ref, kept_ref, sends_ref, skip_ref, rate_ref, doc_ref, step_ref, g_ref, c_ref, b_ref, out_ref, rate_scr
):
    q = pl.program_id(0)
    live = live_count(me_ref, kept_ref, sends_ref)
    totals, source = head_tables(q, rate_ref, step_ref, rate_scr)
    source_col = turned(source)
    along, down = doc_tables(doc_ref)
    s = lax.broadcasted_iota(jnp.int32, (LIVE, ROWS), 0)
    t = lax.broadcasted_iota(jnp.int32, (LIVE, ROWS), 1)
    keep = (along[:LIVE] == down[:LIVE]) & (s <= t) & (t < live) & (s < live)
    bias = jnp.where(keep, 0.0, -1e30).astype(F32)
    half = lax.broadcasted_iota(jnp.int32, (ROWS, 128), 1) < HDIM
    affinity = lax.dot_general(
        b_ref[:LIVE, :], c_ref[...], (((1,), (1,)), ((), ())), preferred_element_type=F32
    )
    alive = s < live
    for p in range(HPG // 2):
        lanes = slice(p * 128, p * 128 + 128)
        g_pair = g_ref[:, lanes]
        zero = jnp.zeros_like(g_pair)
        both = jnp.concatenate([jnp.where(half, g_pair, zero), jnp.where(half, zero, g_pair)], axis=0)
        kernels = []
        for k in range(2):
            h = 2 * p + k
            gap = (source_col[:LIVE, h : h + 1] - totals[h : h + 1, :]) + bias
            kernels.append((jnp.exp2(gap) * affinity).astype(BF16))
        grads = jnp.dot(jnp.concatenate(kernels, axis=1), both, preferred_element_type=F32)
        first = q * HPG + 2 * p
        gain = jnp.where(half[:LIVE], skip_ref[first], skip_ref[first + 1])
        grads = grads + jnp.where(alive, gain * g_pair[:LIVE].astype(F32), 0.0)
        out_ref[:LIVE, lanes] = grads.astype(BF16)
    out_ref[LIVE:, :] = jnp.zeros((ROWS - LIVE, HPG * HDIM), BF16)


def scan_grad_call(me, kept, sends, skip, rate, docs, steps, out_grad, c_proj, b_factors):
    wide = HPG * HDIM
    return pl.pallas_call(
        scan_grad_kernel,
        grid=(GROUPS,),
        out_shape=jax.ShapeDtypeStruct((ROWS, D), BF16),
        in_specs=[
            smem(),
            smem(),
            smem(),
            smem(),
            row_spec(),
            row_spec(),
            pl.BlockSpec((HPG, ROWS), lambda q: (q, 0)),
            pl.BlockSpec((ROWS, wide), lambda q: (0, q)),
            pl.BlockSpec((ROWS, STATE), lambda q: (0, q)),
            pl.BlockSpec((ROWS, STATE), lambda q: (0, q)),
        ],
        out_specs=pl.BlockSpec((ROWS, wide), lambda q: (0, q)),
        scratch_shapes=[pltpu.VMEM((HEADS, HEADS), F32)],
        compiler_params=pltpu.CompilerParams(vmem_limit_bytes=32 * 2**20),
        cost_estimate=pl.CostEstimate(
            flops=4 * LIVE * ROWS * D, bytes_accessed=4 * ROWS * D, transcendentals=HEADS * LIVE * ROWS
        ),
        name="scan_grad",
    )(me, kept, sends, skip, rate, docs, steps, out_grad, c_proj, b_factors)


def weight_kernel(me_ref, *refs):
    s_refs, c_refs = refs[:MEMBERS], refs[MEMBERS : 2 * MEMBERS]
    keep_ref, send_ref, s_all, c_all = refs[2 * MEMBERS :]
    for m in range(MEMBERS):
        s_all[m * LIVE : (m + 1) * LIVE, :] = s_refs[m][...]
        c_all[m * LIVE : (m + 1) * LIVE, :] = c_refs[m][...]
    first_core = me_ref[1] == 0
    wide = 256
    for i in range(CHUNK // wide):
        part = lax.dot_general(
            s_all[:, i * wide : (i + 1) * wide],
            c_all[...],
            (((0,), (0,)), ((), ())),
            preferred_element_type=F32,
        )
        for j in range(wide // 64):
            low, high = part[j * 64 : j * 64 + 32], part[j * 64 + 32 : j * 64 + 64]
            keep_ref[i * (wide // 64) + j] = jnp.where(first_core, low, high)
            send_ref[i * (wide // 64) + j] = jnp.where(first_core, high, low).astype(send_ref.dtype)


def weight_call(me, pieces, grads):
    vmem = pl.BlockSpec(memory_space=pltpu.VMEM)
    return pl.pallas_call(
        weight_kernel,
        out_shape=[
            jax.ShapeDtypeStruct((16, 32, NARROW), F32),
            jax.ShapeDtypeStruct((16, 32, NARROW), F32),
        ],
        in_specs=[smem()] + [vmem] * (2 * MEMBERS),
        out_specs=[vmem, vmem],
        scratch_shapes=[
            pltpu.VMEM((MEMBERS * LIVE, CHUNK), BF16),
            pltpu.VMEM((MEMBERS * LIVE, NARROW), BF16),
        ],
        compiler_params=pltpu.CompilerParams(vmem_limit_bytes=32 * 2**20),
        cost_estimate=pl.CostEstimate(
            flops=2 * MEMBERS * LIVE * CHUNK * NARROW, bytes_accessed=7 * 2**20, transcendentals=0
        ),
        name="weight_part",
    )(me, *pieces, *grads)


def shards(
    section_input,
    c_weight,
    scan_input,
    b_factors,
    step_size,
    decay_rate,
    skip_gain,
    out_grad,
    doc_index,
    kept_rows,
    send_counts,
):
    dp_index = lax.axis_index("dp").astype(jnp.int32)
    f_index = lax.axis_index("fsdp").astype(jnp.int32)
    me = jnp.stack([dp_index, dp_index % 2])
    x, y_hi = f_index % 4, f_index // 4
    dests = jnp.stack([(y_hi ^ flip) * 4 + (x + dx) % 4 for dx, flip in STEPS])
    kept = kept_rows.reshape(32, 1)
    sends = send_counts.reshape(32, 32)
    rate, docs = decay_rate.reshape(1, HEADS), doc_index.reshape(1, ROWS)

    weights = lax.all_gather(c_weight, "fsdp", axis=0, tiled=True)

    packed = pack(dests, section_input)
    pieces = [packed[0]] + [move(packed[m], STEPS[m]) for m in range(1, MEMBERS)]

    c_full, c_live = c_grad_call(me, kept, sends, rate, docs, step_size, out_grad, scan_input, b_factors)
    grads = [c_live] + [move(c_live, STEPS[m]) for m in range(1, MEMBERS)]

    mine, theirs = weight_call(me, pieces, grads)
    mine = (mine + lax.ppermute(theirs, "dp", CORE_SWAP)).astype(BF16)
    mine = lax.all_to_all(mine, "dp", 0, 0, axis_index_groups=SAME_CORE)
    weight_sum = jnp.sum(mine.astype(F32), axis=0)

    c_proj = jnp.dot(section_input, weights, preferred_element_type=F32).astype(BF16)
    scan_grad = scan_grad_call(
        me, kept, sends, skip_gain, rate, docs, step_size, out_grad, c_proj, b_factors
    )
    row_grad = lax.dot_general(c_full, weights, (((1,), (1,)), ((), ())), preferred_element_type=F32)

    tops = jnp.where(
        lax.broadcasted_iota(jnp.int32, (256, 1, 128), 2) < 64,
        jnp.max(jnp.abs(row_grad)),
        jnp.max(jnp.abs(weight_sum)),
    )
    tops = jnp.max(lax.all_to_all(tops, ALL, 0, 0), axis=(0, 1))
    input_grad = (row_grad / (tops[0] + peak_eps)).astype(BF16)
    readout_weight_gradient = weight_sum / (tops[64] + peak_eps)
    return (input_grad, scan_grad, readout_weight_gradient)


def solution(mesh):
    rows = P(ALL, None)
    placed = (
        rows,
        P("fsdp", None),
        rows,
        rows,
        P(None, ALL),
        P(),
        P(),
        rows,
        P(ALL),
        P(None, "fsdp"),
        P(None, "fsdp", None),
    )
    return jax.shard_map(
        shards, mesh=mesh, in_specs=placed, out_specs=(rows, rows, rows), check_vma=False
    )
```

time: 1490 us -> 201 us (0.13)
  waiting for transfers between devices: 1270 us -> 20 us
  blocking collectives: 126 us -> 66.8 us
  starting transfers between devices: 0.08 us -> 44 us
  Pallas kernels: 0 us -> 23.8 us
  local copies, waits for them, and re-layouts: 32.9 us -> 9.13 us
  matrix products: 29.8 us -> 13.7 us
    unnamed x3 -> x1, waiting for transfers between devices: 1190 us -> 0.68 us
    pmax x1 -> x0, blocking collectives: 126 us -> none  [shards(): row_peak = lax.pmax(row_top, ('dp', 'fsdp'))]
    all_gather x1, waiting for transfers between devices: 76.8 us -> 0.01 us  [shards(): weights = lax.all_gather(c_weight, 'fsdp', axis=0, tiled=True)]
    all_to_all x0 -> x1, blocking collectives: none -> 66.8 us  [shards(): mine = lax.all_to_all(mine, 'dp', 0, 0, axis_index_groups=SAME_CORE)]
    ppermute x0 -> x15, starting transfers between devices: none -> 32.3 us  [the longest x14 25 us: move(): return lax.ppermute(value, ALL, ring_pairs(*step))]
    pallas_call x0 -> x4, Pallas kernels: none -> 23.8 us  [the longest x1 8.03 us: scan_grad_call(): pl.pallas_call(scan_grad_kernel, grid=(GROUPS,), out_shape=jax.ShapeDtype...]
    unnamed x17 -> x31, local copies, waits for them, and re-layouts: 27.4 us -> 7.74 us
    ppermute x0 -> x15, waiting for transfers between devices: none -> 19.3 us  [the longest x14 17 us: move(): return lax.ppermute(value, ALL, ring_pairs(*step))]
  transfers between devices with their start and end apart: 2 -> 17, of which waited for: 2 -> 8; matrix products, arithmetic and copies ran while one was open for 5% -> 3% of each run, Pallas kernels for 0% -> 12%
where the time goes in v1:
time: 201 us; the launch traced here: 200 us
  blocking collectives  66.8 us (33%)
  starting transfers between devices  44 us (22%)
  Pallas kernels  23.8 us (12%)
  waiting for transfers between devices  20 us (10%)
  between operations  15.5 us (8%)
  matrix products  13.7 us (7%)
  local copies, waits for them, and re-layouts  9.13 us (5%)
  other arithmetic  6.81 us (3%)
    all_to_all x1, blocking collectives, shards(): mine = lax.all_to_all(mine, 'dp', 0, 0, axis_index_groups=SAME_CORE)  66.8 us
    ppermute x14, starting transfers between devices, move(): return lax.ppermute(value, ALL, ring_pairs(*step))  25 us
    ppermute x14, waiting for transfers between devices, move(): return lax.ppermute(value, ALL, ring_pairs(*step))  17 us
    all_to_all x1, starting transfers between devices, shards(): tops = jnp.max(lax.all_to_all(tops, ALL, 0, 0), axis=(0, 1))  11.6 us
    dot_general x1, matrix products, shards(): lax.dot_general(c_full, weights, (((1,), (1,)), ((), ())), preferred_elem...  8.87 us
    pallas_call x1, Pallas kernels, scan_grad_call(): pl.pallas_call(scan_grad_kernel, grid=(GROUPS,), out_shape=jax.ShapeDtype...  8.03 us
    unnamed x31, local copies, waits for them, and re-layouts  7.74 us
    pallas_call x1, Pallas kernels, c_grad_call(): pl.pallas_call(c_grad_kernel, grid=(GROUPS,), out_shape=[jax.ShapeDtypeSt...  7.41 us
  transfers between devices with their start and end apart: 17, of which 8 were waited for; matrix products, arithmetic and copies ran while one was open for 3% of the time, Pallas kernels for 12%

profile of v1, /device:TPU:5, one launch (start us, length us, event | category | flops | bytes accessed | tf_op | source)
XLA Modules:
  0.0 199.7 jit_solution(4890376945072150450)
XLA Ops:
  8.7 1.6 copy-done.1
  10.3 1.6 copy-done.3
  11.9 0.9 copy-done.4
  12.8 0.8 copy-done.6
  15.7 7.4 %c_grad.1 = (bf16[128,512]{1,0:T(8,128)(2,1)S(1)}, bf16[96,512]{1,0:T(8,128)(2,1)S(1)}) custom-call(s32[2]{0:T(128)S(1)} %pad_add_fusion.me_ref, s32[32,1]{1,0:T(8,128)S(1)} %copy.18.kept_ref, s32[32,32]{1,0:T(8,128)S(1)} %bitcast.20, f32[1,128]{1,0:T(1,128)S(1)} %bitcast.22, s32[1,128]{1,0:T(1,128)S(1)} %bitcast.24, f32[128,128]{1,0:T(8,128)S(1)} %copy-done.6, ...), custom_call_target="tpu_custom_call" | custom-call | flops 402653184 | bytes 4194304 | tf_op jit(solution)/shard_map/c_grad/pallas_call | solution.py:158
  23.1 2.8 %collective-permute-start.13 = (bf16[96,512]{1,0:T(8,128)(2,1)S(1)}, bf16[96,512]{1,0:T(8,128)(2,1)S(1)}, u32[]{:S(2)}, u32[]{:S(2)}) collective-permute-start(bf16[96,512]{1,0:T(8,128)(2,1)S(1)} %get-tuple-element.24.refs_8_), channel_id=1, source_target_pairs={{0,134},{8,142},{16,150},{24,158},{32,166},{40,174},{48,182},{56,1... | collective-permute-start | bytes 294920 | tf_op jit(solution)/shard_map/ppermute | solution.py:47
  25.9 1.5 collective-permute-start.12
  27.4 2.0 %collective-permute-start.11 = (bf16[96,512]{1,0:T(8,128)(2,1)S(1)}, bf16[96,512]{1,0:T(8,128)(2,1)S(1)}, u32[]{:S(2)}, u32[]{:S(2)}) collective-permute-start(bf16[96,512]{1,0:T(8,128)(2,1)S(1)} %get-tuple-element.24.refs_8_), channel_id=1, source_target_pairs={{0,133},{8,141},{16,149},{24,157},{32,165},{40,173},{48,181},{56,1... | collective-permute-start | bytes 294920 | tf_op jit(solution)/shard_map/ppermute | solution.py:47
  30.2 6.8 %pack.1 = (bf16[96,1024]{1,0:T(8,128)(2,1)S(1)}, bf16[96,1024]{1,0:T(8,128)(2,1)S(1)}, bf16[96,1024]{1,0:T(8,128)(2,1)S(1)}, bf16[96,1024]{1,0:T(8,128)(2,1)S(1)...) custom-call(s32[8]{0:T(128)S(1)} %stack.47.f_ref, ...), custom_call_target="tpu_custom_call" | custom-call | bytes 3145728 | tf_op jit(solution)/shard_map/pack/pallas_call | solution.py:70
  37.1 2.4 %collective-permute-start = (bf16[96,1024]{1,0:T(8,128)(2,1)S(1)}, bf16[96,1024]{1,0:T(8,128)(2,1)S(1)}, u32[]{:S(2)}, u32[]{:S(2)}) collective-permute-start(bf16[96,1024]{1,0:T(8,128)(2,1)S(1)} %get-tuple-element.17), channel_id=1, source_target_pairs={{0,1},{8,9},{16,17},{24,25},{32,33},{40,41},{48,49},{56,57},{64,65... | collective-permute-start | bytes 589832 | tf_op jit(solution)/shard_map/ppermute | solution.py:47
  39.5 2.4 %collective-permute-start.9 = (bf16[96,512]{1,0:T(8,128)(2,1)S(1)}, bf16[96,512]{1,0:T(8,128)(2,1)S(1)}, u32[]{:S(2)}, u32[]{:S(2)}) collective-permute-start(bf16[96,512]{1,0:T(8,128)(2,1)S(1)} %get-tuple-element.24.refs_8_), channel_id=1, source_target_pairs={{0,2},{8,10},{16,18},{24,26},{32,34},{40,42},{48,50},{56,58},{64,6... | collective-permute-start | bytes 294920 | tf_op jit(solution)/shard_map/ppermute | solution.py:47
  42.2 7.0 %collective-permute-done.10.refs_12_ = bf16[96,512]{1,0:T(8,128)(2,1)S(1)} collective-permute-done((bf16[96,512]{1,0:T(8,128)(2,1)S(1)}, bf16[96,512]{1,0:T(8,128)(2,1)S(1)}, u32[]{:S(2)}, u32[]{:S(2)}) %collective-permute-start.10) | collective-permute-done | bytes 98336 | tf_op jit(solution)/shard_map/ppermute | solution.py:47
  49.2 1.1 collective-permute-start.7
  50.5 1.3 collective-permute-start.2
  51.8 1.6 collective-permute-done.8.refs_10_
  53.4 2.2 %collective-permute-start.3 = (bf16[96,1024]{1,0:T(8,128)(2,1)S(1)}, bf16[96,1024]{1,0:T(8,128)(2,1)S(1)}, u32[]{:S(2)}, u32[]{:S(2)}) collective-permute-start(bf16[96,1024]{1,0:T(8,128)(2,1)S(1)} %get-tuple-element.20), channel_id=1, source_target_pairs={{0,132},{8,140},{16,148},{24,156},{32,164},{40,172},{48,180},{56,1... | collective-permute-start | bytes 589832 | tf_op jit(solution)/shard_map/ppermute | solution.py:47
  55.6 1.0 collective-permute-done.7.refs_9_
  56.7 2.8 %collective-permute-start.4 = (bf16[96,1024]{1,0:T(8,128)(2,1)S(1)}, bf16[96,1024]{1,0:T(8,128)(2,1)S(1)}, u32[]{:S(2)}, u32[]{:S(2)}) collective-permute-start(bf16[96,1024]{1,0:T(8,128)(2,1)S(1)} %get-tuple-element.21), channel_id=1, source_target_pairs={{0,133},{8,141},{16,149},{24,157},{32,165},{40,173},{48,181},{56,1... | collective-permute-start | bytes 589832 | tf_op jit(solution)/shard_map/ppermute | solution.py:47
  60.3 4.7 %collective-permute-start.6 = (bf16[96,1024]{1,0:T(8,128)(2,1)S(1)}, bf16[96,1024]{1,0:T(8,128)(2,1)S(1)}, u32[]{:S(2)}, u32[]{:S(2)}) collective-permute-start(bf16[96,1024]{1,0:T(8,128)(2,1)S(1)} %get-tuple-element.23), channel_id=1, source_target_pairs={{0,134},{8,142},{16,150},{24,158},{32,166},{40,174},{48,182},{56,1... | collective-permute-start | bytes 589832 | tf_op jit(solution)/shard_map/ppermute | solution.py:47
  65.0 2.2 %collective-permute-done.4.refs_5_ = bf16[96,1024]{1,0:T(8,128)(2,1)S(1)} collective-permute-done((bf16[96,1024]{1,0:T(8,128)(2,1)S(1)}, bf16[96,1024]{1,0:T(8,128)(2,1)S(1)}, u32[]{:S(2)}, u32[]{:S(2)}) %collective-permute-start.4) | collective-permute-done | bytes 196640 | tf_op jit(solution)/shard_map/ppermute | solution.py:47
  67.2 1.5 collective-permute-done.5.refs_6_
  68.8 3.3 %collective-permute-done.6.refs_7_ = bf16[96,1024]{1,0:T(8,128)(2,1)S(1)} collective-permute-done((bf16[96,1024]{1,0:T(8,128)(2,1)S(1)}, bf16[96,1024]{1,0:T(8,128)(2,1)S(1)}, u32[]{:S(2)}, u32[]{:S(2)}) %collective-permute-start.6) | collective-permute-done | bytes 196640 | tf_op jit(solution)/shard_map/ppermute | solution.py:47
  72.0 1.6 weight_part.1
  73.6 7.3 %collective-permute-start.14 = (f32[16,32,512]{2,1,0:T(8,128)S(1)}, f32[16,32,512]{2,1,0:T(8,128)S(1)}, u32[]{:S(2)}, u32[]{:S(2)}) collective-permute-start(f32[16,32,512]{2,1,0:T(8,128)S(1)} %get-tuple-element.26), channel_id=1, source_target_pairs={{0,8},{8,0},{16,24},{24,16},{32,40},{40,32},{48,56},{56,48},{64,72... | collective-permute-start | bytes 3145736 | tf_op jit(solution)/shard_map/ppermute | solution.py:326
  80.9 2.3 %collective-permute-done.14 = f32[16,32,512]{2,1,0:T(8,128)S(1)} collective-permute-done((f32[16,32,512]{2,1,0:T(8,128)S(1)}, f32[16,32,512]{2,1,0:T(8,128)S(1)}, u32[]{:S(2)}, u32[]{:S(2)}) %collective-permute-start.14) | collective-permute-done | bytes 1048608 | tf_op jit(solution)/shard_map/ppermute | solution.py:326
  83.5 66.8 %all_to_all.10 = bf16[16,32,512]{2,1,0:T(8,128)(2,1)S(1)} all-to-all(bf16[16,32,512]{2,1,0:T(8,128)(2,1)S(1)} %add_convert_fusion), channel_id=1, replica_groups={{0,16,32,48,64,80,96,112,128,144,160,176,192,208,224,240},{8,24,40,56,7..., dimensions={0} | all-to-all | bytes 1048576 | tf_op jit(solution)/shard_map/all_to_all | solution.py:327
  150.9 8.9 %abs_reduce_fusion = (f32[]{:T(128)}, f32[128,8192]{1,0:T(8,128)}) fusion(bf16[128,512]{1,0:T(8,128)(2,1)S(1)} %get-tuple-element.15, bf16[8192,512]{1,0:T(8,128)(2,1)} %all-gather.2.cloned.1.call-done), kind=kOutput, calls=%fused_computation.1 | convolution fusion | flops 1075838976 | bytes 12713988 | tf_op jit(solution)/shard_map/dot_general | solution.py:334
  159.8 1.3 compare_select_fusion
  161.8 11.6 %all-to-all-start.1 = ((f32[256,1,128]{2,1,0:T(1,128)}), f32[256,1,128]{2,1,0:T(1,128)S(1)}, u32[]{:S(2)}, u32[]{:S(2)}) async-start(f32[256,1,128]{2,1,0:T(1,128)} %iota.7), calls=%async_computation.1 | async-start | bytes 262144 | tf_op jit(solution)/shard_map/all_to_all | solution.py:341
  173.5 4.8 %convolution_convert_fusion.c_ref = bf16[128,512]{1,0:T(8,128)(2,1)S(1)} fusion(bf16[128,8192]{1,0:T(8,128)(2,1)S(1)} %copy-done, bf16[8192,512]{1,0:T(8,128)(2,1)} %all-gather.2.cloned.1.call-done), kind=kOutput, calls=%fused_computation.2 | convolution fusion | flops 1073807360 | bytes 10616832 | tf_op jit(solution)/shard_map/dot_general | solution.py:330
  178.4 8.0 %scan_grad.1 = bf16[128,8192]{1,0:T(8,128)(2,1)} custom-call(s32[2]{0:T(128)S(1)} %pad_add_fusion.me_ref, s32[32,1]{1,0:T(8,128)S(1)} %copy.18.kept_ref, s32[32,32]{1,0:T(8,128)S(1)} %bitcast.21, f32[128]{0:T(128)S(1)} %copy-done.14, f32[1,128]{1,0:T(1,128)S(1)} %bitcast.23, s32[1,128]{1,0:T(1,128)S(1)} %bitcast.25, f32[128,128]{1,0:T(8,128)S(1)} %copy-done.7, ...), custom_call_target="tpu_custom_call" | custom-call | flops 402653184 | bytes 4194304 | tf_op jit(solution)/shard_map/scan_grad/pallas_call | solution.py:226
  189.0 3.8 %divide_convert_fusion = bf16[128,8192]{1,0:T(8,128)(2,1)} fusion(f32[128,8192]{1,0:T(8,128)} %get-tuple-element.30, f32[]{:T(128)} %bitcast.14), kind=kLoop, calls=%fused_computation | loop fusion | flops 2097152 | bytes 6291460 | tf_op jit(solution)/shard_map/convert_element_type | solution.py:342
  (52 shorter events, 8.6 us)
Async XLA Ops:
  7.2 23.1 %copy-start = (bf16[128,8192]{1,0:T(8,128)(2,1)S(1)}, bf16[128,8192]{1,0:T(8,128)(2,1)}, u32[]{:S(2)}) copy-start(bf16[128,8192]{1,0:T(8,128)(2,1)} %s_ref.1) | copy-start | bytes 6291460
  7.2 143.8 %all-gather.2.cloned.1.call-start = ((), (), s32[]{:S(2)}) async-start(), calls=%async_computation.2 | async-start | bytes 9437184 | tf_op jit(solution)/shard_map/all_gather | solution.py:317
  8.7 1.6 copy-start.1
  10.3 1.6 copy-start.3
  11.9 0.9 copy-start.4
  12.8 0.8 copy-start.6
  13.7 0.7 copy-start.8
  14.4 0.7 copy-start.10
  15.0 0.7 copy-start.12
  23.1 16.4 %collective-permute-start.13 = (bf16[96,512]{1,0:T(8,128)(2,1)S(1)}, bf16[96,512]{1,0:T(8,128)(2,1)S(1)}, u32[]{:S(2)}, u32[]{:S(2)}) collective-permute-start(bf16[96,512]{1,0:T(8,128)(2,1)S(1)} %get-tuple-element.24.refs_8_), channel_id=1, source_target_pairs={{0,134},{8,142},{16,150},{24,158},{32,166},{40,174},{48,182},{56,1... | collective-permute-start | bytes 294920 | tf_op jit(solution)/shard_map/ppermute | solution.py:47
  25.9 13.6 %collective-permute-start.12 = (bf16[96,512]{1,0:T(8,128)(2,1)S(1)}, bf16[96,512]{1,0:T(8,128)(2,1)S(1)}, u32[]{:S(2)}, u32[]{:S(2)}) collective-permute-start(bf16[96,512]{1,0:T(8,128)(2,1)S(1)} %get-tuple-element.24.refs_8_), channel_id=1, source_target_pairs={{0,135},{8,143},{16,151},{24,159},{32,167},{40,175},{48,183},{56,1... | collective-permute-start | bytes 294920 | tf_op jit(solution)/shard_map/ppermute | solution.py:47
  27.4 14.5 %collective-permute-start.11 = (bf16[96,512]{1,0:T(8,128)(2,1)S(1)}, bf16[96,512]{1,0:T(8,128)(2,1)S(1)}, u32[]{:S(2)}, u32[]{:S(2)}) collective-permute-start(bf16[96,512]{1,0:T(8,128)(2,1)S(1)} %get-tuple-element.24.refs_8_), channel_id=1, source_target_pairs={{0,133},{8,141},{16,149},{24,157},{32,165},{40,173},{48,181},{56,1... | collective-permute-start | bytes 294920 | tf_op jit(solution)/shard_map/ppermute | solution.py:47
  29.4 19.7 %collective-permute-start.10 = (bf16[96,512]{1,0:T(8,128)(2,1)S(1)}, bf16[96,512]{1,0:T(8,128)(2,1)S(1)}, u32[]{:S(2)}, u32[]{:S(2)}) collective-permute-start(bf16[96,512]{1,0:T(8,128)(2,1)S(1)} %get-tuple-element.24.refs_8_), channel_id=1, source_target_pairs={{0,132},{8,140},{16,148},{24,156},{32,164},{40,172},{48,180},{56,1... | collective-permute-start | bytes 294920 | tf_op jit(solution)/shard_map/ppermute | solution.py:47
  37.1 22.4 %collective-permute-start = (bf16[96,1024]{1,0:T(8,128)(2,1)S(1)}, bf16[96,1024]{1,0:T(8,128)(2,1)S(1)}, u32[]{:S(2)}, u32[]{:S(2)}) collective-permute-start(bf16[96,1024]{1,0:T(8,128)(2,1)S(1)} %get-tuple-element.17), channel_id=1, source_target_pairs={{0,1},{8,9},{16,17},{24,25},{32,33},{40,41},{48,49},{56,57},{64,65... | collective-permute-start | bytes 589832 | tf_op jit(solution)/shard_map/ppermute | solution.py:47
  39.5 20.8 %collective-permute-start.1 = (bf16[96,1024]{1,0:T(8,128)(2,1)S(1)}, bf16[96,1024]{1,0:T(8,128)(2,1)S(1)}, u32[]{:S(2)}, u32[]{:S(2)}) collective-permute-start(bf16[96,1024]{1,0:T(8,128)(2,1)S(1)} %get-tuple-element.18), channel_id=1, source_target_pairs={{0,3},{8,11},{16,19},{24,27},{32,35},{40,43},{48,51},{56,59},{64,6... | collective-permute-start | bytes 589832 | tf_op jit(solution)/shard_map/ppermute | solution.py:47
  39.5 11.0 %collective-permute-start.9 = (bf16[96,512]{1,0:T(8,128)(2,1)S(1)}, bf16[96,512]{1,0:T(8,128)(2,1)S(1)}, u32[]{:S(2)}, u32[]{:S(2)}) collective-permute-start(bf16[96,512]{1,0:T(8,128)(2,1)S(1)} %get-tuple-element.24.refs_8_), channel_id=1, source_target_pairs={{0,2},{8,10},{16,18},{24,26},{32,34},{40,42},{48,50},{56,58},{64,6... | collective-permute-start | bytes 294920 | tf_op jit(solution)/shard_map/ppermute | solution.py:47
  41.9 11.5 %collective-permute-start.8 = (bf16[96,512]{1,0:T(8,128)(2,1)S(1)}, bf16[96,512]{1,0:T(8,128)(2,1)S(1)}, u32[]{:S(2)}, u32[]{:S(2)}) collective-permute-start(bf16[96,512]{1,0:T(8,128)(2,1)S(1)} %get-tuple-element.24.refs_8_), channel_id=1, source_target_pairs={{0,3},{8,11},{16,19},{24,27},{32,35},{40,43},{48,51},{56,59},{64,6... | collective-permute-start | bytes 294920 | tf_op jit(solution)/shard_map/ppermute | solution.py:47
  49.2 7.5 %collective-permute-start.7 = (bf16[96,512]{1,0:T(8,128)(2,1)S(1)}, bf16[96,512]{1,0:T(8,128)(2,1)S(1)}, u32[]{:S(2)}, u32[]{:S(2)}) collective-permute-start(bf16[96,512]{1,0:T(8,128)(2,1)S(1)} %get-tuple-element.24.refs_8_), channel_id=1, source_target_pairs={{0,1},{8,9},{16,17},{24,25},{32,33},{40,41},{48,49},{56,57},{64,65... | collective-permute-start | bytes 294920 | tf_op jit(solution)/shard_map/ppermute | solution.py:47
  50.5 14.5 %collective-permute-start.2 = (bf16[96,1024]{1,0:T(8,128)(2,1)S(1)}, bf16[96,1024]{1,0:T(8,128)(2,1)S(1)}, u32[]{:S(2)}, u32[]{:S(2)}) collective-permute-start(bf16[96,1024]{1,0:T(8,128)(2,1)S(1)} %get-tuple-element.19), channel_id=1, source_target_pairs={{0,2},{8,10},{16,18},{24,26},{32,34},{40,42},{48,50},{56,58},{64,6... | collective-permute-start | bytes 589832 | tf_op jit(solution)/shard_map/ppermute | solution.py:47
  53.4 11.6 %collective-permute-start.3 = (bf16[96,1024]{1,0:T(8,128)(2,1)S(1)}, bf16[96,1024]{1,0:T(8,128)(2,1)S(1)}, u32[]{:S(2)}, u32[]{:S(2)}) collective-permute-start(bf16[96,1024]{1,0:T(8,128)(2,1)S(1)} %get-tuple-element.20), channel_id=1, source_target_pairs={{0,132},{8,140},{16,148},{24,156},{32,164},{40,172},{48,180},{56,1... | collective-permute-start | bytes 589832 | tf_op jit(solution)/shard_map/ppermute | solution.py:47
  56.7 10.5 %collective-permute-start.4 = (bf16[96,1024]{1,0:T(8,128)(2,1)S(1)}, bf16[96,1024]{1,0:T(8,128)(2,1)S(1)}, u32[]{:S(2)}, u32[]{:S(2)}) collective-permute-start(bf16[96,1024]{1,0:T(8,128)(2,1)S(1)} %get-tuple-element.21), channel_id=1, source_target_pairs={{0,133},{8,141},{16,149},{24,157},{32,165},{40,173},{48,181},{56,1... | collective-permute-start | bytes 589832 | tf_op jit(solution)/shard_map/ppermute | solution.py:47
  59.5 9.2 %collective-permute-start.5 = (bf16[96,1024]{1,0:T(8,128)(2,1)S(1)}, bf16[96,1024]{1,0:T(8,128)(2,1)S(1)}, u32[]{:S(2)}, u32[]{:S(2)}) collective-permute-start(bf16[96,1024]{1,0:T(8,128)(2,1)S(1)} %get-tuple-element.22), channel_id=1, source_target_pairs={{0,135},{8,143},{16,151},{24,159},{32,167},{40,175},{48,183},{56,1... | collective-permute-start | bytes 589832 | tf_op jit(solution)/shard_map/ppermute | solution.py:47
  60.3 11.8 %collective-permute-start.6 = (bf16[96,1024]{1,0:T(8,128)(2,1)S(1)}, bf16[96,1024]{1,0:T(8,128)(2,1)S(1)}, u32[]{:S(2)}, u32[]{:S(2)}) collective-permute-start(bf16[96,1024]{1,0:T(8,128)(2,1)S(1)} %get-tuple-element.23), channel_id=1, source_target_pairs={{0,134},{8,142},{16,150},{24,158},{32,166},{40,174},{48,182},{56,1... | collective-permute-start | bytes 589832 | tf_op jit(solution)/shard_map/ppermute | solution.py:47
  73.6 9.6 %collective-permute-start.14 = (f32[16,32,512]{2,1,0:T(8,128)S(1)}, f32[16,32,512]{2,1,0:T(8,128)S(1)}, u32[]{:S(2)}, u32[]{:S(2)}) collective-permute-start(f32[16,32,512]{2,1,0:T(8,128)S(1)} %get-tuple-element.26), channel_id=1, source_target_pairs={{0,8},{8,0},{16,24},{24,16},{32,40},{40,32},{48,56},{56,48},{64,72... | collective-permute-start | bytes 3145736 | tf_op jit(solution)/shard_map/ppermute | solution.py:326
  161.8 24.6 %all-to-all-start.1 = ((f32[256,1,128]{2,1,0:T(1,128)}), f32[256,1,128]{2,1,0:T(1,128)S(1)}, u32[]{:S(2)}, u32[]{:S(2)}) async-start(f32[256,1,128]{2,1,0:T(1,128)} %iota.7), calls=%async_computation.1 | async-start | bytes 262144 | tf_op jit(solution)/shard_map/all_to_all | solution.py:341
  173.5 4.9 %copy-start.2 = (bf16[128,8192]{1,0:T(8,128)(2,1)S(1)}, bf16[128,8192]{1,0:T(8,128)(2,1)}, u32[]{:S(2)}) copy-start(bf16[128,8192]{1,0:T(8,128)(2,1)} %g_ref.3) | copy-start | bytes 6291460
  173.5 4.9 %copy-start.5 = (bf16[128,512]{1,0:T(8,128)(2,1)S(1)}, bf16[128,512]{1,0:T(8,128)(2,1)}, u32[]{:S(2)}) copy-start(bf16[128,512]{1,0:T(8,128)(2,1)} %b_ref.3) | copy-start | bytes 393220
  173.5 4.9 %copy-start.7 = (f32[128,128]{1,0:T(8,128)S(1)}, f32[128,128]{1,0:T(8,128)}, u32[]{:S(2)}) copy-start(f32[128,128]{1,0:T(8,128)} %step_ref.3) | copy-start | bytes 196612
  173.5 4.9 %copy-start.9 = (s32[32,1,32]{2,1,0:T(1,128)S(1)}, s32[32,1,32]{2,1,0:T(1,128)}, u32[]{:S(2)}) copy-start(s32[32,1,32]{2,1,0:T(1,128)} %param.21) | copy-start | bytes 12292
  173.5 4.9 %copy-start.11 = (f32[128]{0:T(128)S(1)}, f32[128]{0:T(128)}, u32[]{:S(2)}) copy-start(f32[128]{0:T(128)} %param.16) | copy-start | bytes 1540
  173.5 4.9 %copy-start.13 = (s32[128]{0:T(128)S(1)}, s32[128]{0:T(128)}, u32[]{:S(2)}) copy-start(s32[128]{0:T(128)} %param.19) | copy-start | bytes 1540
  173.5 4.9 %copy-start.14 = (f32[128]{0:T(128)S(1)}, f32[128]{0:T(128)}, u32[]{:S(2)}) copy-start(f32[128]{0:T(128)} %skip_ref.1) | copy-start | bytes 1540
Sparse Core Ops, SparseCore 0:
  10.6 129.5 all-gather.1

commit v2 on v1

v2 whole, which is shorter than its diff:
```python
import jax
import jax.numpy as jnp
from jax import lax
from jax.experimental import pallas as pl
from jax.experimental.pallas import tpu as pltpu
from jax.sharding import PartitionSpec as P

GROUPS = 4
STATE = 128
HEADS = 128
HDIM = 64
HPG = HEADS // GROUPS
ROWS = 128
LIVE = 96
D = 8192
NARROW = GROUPS * STATE
MEMBERS = 8
CHUNK = D // MEMBERS
BOTH = NARROW + CHUNK
VMEM_LIMIT = 60 * 2**20
LOG2E = 1.4426950408889634
ALL = ("dp", "fsdp")
peak_eps = 1e-06
F32 = jnp.float32
BF16 = jnp.bfloat16


def joint(y_hi, x, y_lo, z, core):
    return (y_lo * 16 + z * 2 + core) * 8 + y_hi * 4 + x


WIDE = [
    [joint(h, x, h ^ s, z, c) for h in (0, 1) for x in range(4)]
    for s in (0, 1)
    for z in range(8)
    for c in (0, 1)
]
def moved(dx, pair):
    return [
        (joint(h, x, l, z, c), joint(h ^ pair, (x + dx) % 4, l ^ pair, z, c))
        for h in (0, 1)
        for x in range(4)
        for l in (0, 1)
        for z in range(8)
        for c in (0, 1)
    ]


X_STEPS = (0, 1, 3, 2)
STEPS = [(dx, pair) for dx in X_STEPS for pair in (0, 1)]
CORE_SWAP = [(i, i ^ 1) for i in range(32)]
SAME_CORE = [[l * 16 + z * 2 + c for l in (0, 1) for z in range(8)] for c in (0, 1)]
HOME = [
    (joint(h, x, l, z, c), joint(z // 4, z % 4, h, 2 * x + l, c))
    for h in (0, 1)
    for x in range(4)
    for l in (0, 1)
    for z in range(8)
    for c in (0, 1)
]


def exchange(value, groups):
    return lax.all_to_all(value, ALL, 0, 0, axis_index_groups=groups)


def along_x(value):
    return [value] + [lax.ppermute(value, ALL, moved(dx, 0)) for dx in X_STEPS[1:]]


def to_pair(value):
    return lax.ppermute(value, ALL, moved(0, 1))


def to_core(value):
    return lax.ppermute(value, "dp", CORE_SWAP)


def coordinates():
    dp, f = lax.axis_index("dp"), lax.axis_index("fsdp")
    return dict(dp=dp, core=dp % 2, y_lo=dp // 16, x=f % 4, y_hi=f // 4)


def rows_at(sign):
    at = coordinates()
    return [(at["y_hi"] + pair) % 2 * 4 + (at["x"] + 4 + sign * dx) % 4 for dx, pair in STEPS]


def sources():
    behind = rows_at(-1)
    return [behind[2 * i : 2 * i + 2] for i in range(4)]


def params():
    return pltpu.CompilerParams(vmem_limit_bytes=VMEM_LIMIT)


def pack_kernel(s_ref, wide_ref):
    wide_ref[0] = s_ref[...]


def pack(section_input):
    return pl.pallas_call(
        pack_kernel,
        grid=(MEMBERS,),
        out_shape=jax.ShapeDtypeStruct((MEMBERS, LIVE, CHUNK), BF16),
        in_specs=[pl.BlockSpec((LIVE, CHUNK), lambda f: (0, f))],
        out_specs=pl.BlockSpec((1, LIVE, CHUNK), lambda f: (f, 0, 0)),
        compiler_params=params(),
        cost_estimate=pl.CostEstimate(flops=0, bytes_accessed=4 * LIVE * D, transcendentals=0),
        name="pack",
    )(section_input)


def live_count(kept_ref, sends_ref):
    own = lax.broadcasted_iota(jnp.int32, (32, 32), 0) == coordinates()["dp"]
    sent = jnp.sum(jnp.where(own, sends_ref[...].astype(F32), 0.0), axis=1, keepdims=True)
    held = jnp.where(own[:, :1], kept_ref[...].astype(F32), 0.0)
    return jnp.sum(sent + held, axis=0, keepdims=True)


def places(shape):
    rows = [lax.broadcasted_iota(jnp.int32, shape, k).astype(F32) for k in range(2)]
    return rows


def head_tables(q, rate_ref, step_ref, rate_scr):
    rate_scr[...] = jnp.transpose(jnp.broadcast_to(rate_ref[...], (HEADS, HEADS)))
    steps = step_ref[...]
    totals = steps * rate_scr[pl.ds(pl.multiple_of(q * HPG, HPG), HPG), :]
    lane = lax.broadcasted_iota(jnp.int32, totals.shape, 1)
    reach = 1
    while reach < ROWS:
        totals = totals + jnp.where(lane >= reach, pltpu.roll(totals, reach, 1), 0.0)
        reach *= 2
    totals = totals * LOG2E
    return totals, totals + jnp.log(steps) * LOG2E


def turned(table):
    filler = jnp.zeros((ROWS - HPG, ROWS), F32)
    return jnp.transpose(jnp.concatenate([table, filler], axis=0))


def doc_tables(doc_ref):
    along = jnp.broadcast_to(doc_ref[...].astype(F32), (ROWS, ROWS))
    return along, jnp.transpose(along)


def c_grad_kernel(
    kept_ref, sends_ref, rate_ref, doc_ref, step_ref, g_ref, x_ref, b_ref, out_ref, rate_scr
):
    q = pl.program_id(0)
    live = live_count(kept_ref, sends_ref)
    totals, source = head_tables(q, rate_ref, step_ref, rate_scr)
    totals_col = turned(totals)
    along, down = doc_tables(doc_ref)
    t, s = places((LIVE, ROWS))
    keep = (along[:LIVE] == down[:LIVE]) & (s <= t) & (t < live) & (s < live)
    bias = jnp.where(keep, 0.0, -1e30).astype(F32)
    half = lax.broadcasted_iota(jnp.int32, (ROWS, 128), 1) < HDIM
    mixing = jnp.zeros((LIVE, ROWS), F32)
    for p in range(HPG // 2):
        lanes = slice(p * 128, p * 128 + 128)
        x_pair = x_ref[:, lanes]
        zero = jnp.zeros_like(x_pair)
        both = jnp.concatenate([jnp.where(half, x_pair, zero), jnp.where(half, zero, x_pair)], axis=0)
        inner = lax.dot_general(
            g_ref[:, lanes], both, (((1,), (1,)), ((), ())), preferred_element_type=F32
        )
        for k in range(2):
            h = 2 * p + k
            gap = (source[h : h + 1, :] - totals_col[:LIVE, h : h + 1]) + bias
            mixing = mixing + jnp.exp2(gap) * inner[:, k * 128 : k * 128 + 128]
    c_grad = jnp.dot(mixing.astype(BF16), b_ref[...], preferred_element_type=F32).astype(BF16)
    out_ref[...] = c_grad


def smem():
    return pl.BlockSpec(memory_space=pltpu.SMEM)


def row_spec():
    return pl.BlockSpec((1, 128), lambda q: (0, 0))


def c_grad_call(kept, sends, rate, docs, steps, out_grad, scan_input, b_factors):
    wide = HPG * HDIM
    return pl.pallas_call(
        c_grad_kernel,
        grid=(GROUPS,),
        out_shape=jax.ShapeDtypeStruct((LIVE, NARROW), BF16),
        in_specs=[
            pl.BlockSpec((32, 1), lambda q: (0, 0)),
            pl.BlockSpec((32, 32), lambda q: (0, 0)),
            row_spec(),
            row_spec(),
            pl.BlockSpec((HPG, ROWS), lambda q: (q, 0)),
            pl.BlockSpec((LIVE, wide), lambda q: (0, q)),
            pl.BlockSpec((ROWS, wide), lambda q: (0, q)),
            pl.BlockSpec((ROWS, STATE), lambda q: (0, q)),
        ],
        out_specs=pl.BlockSpec((LIVE, STATE), lambda q: (0, q)),
        scratch_shapes=[pltpu.VMEM((HEADS, HEADS), F32)],
        compiler_params=params(),
        cost_estimate=pl.CostEstimate(
            flops=4 * LIVE * ROWS * D, bytes_accessed=4 * ROWS * D, transcendentals=HEADS * LIVE * ROWS
        ),
        name="c_grad",
    )(kept, sends, rate, docs, steps, out_grad, scan_input, b_factors)


def scan_grad_kernel(
    kept_ref, sends_ref, skip_ref, rate_ref, doc_ref, step_ref, g_ref, b_ref, *refs
):
    q = pl.program_id(0)
    proj_refs, (out_ref, rate_scr) = refs[:MEMBERS], refs[MEMBERS:]
    live = live_count(kept_ref, sends_ref)
    totals, source = head_tables(q, rate_ref, step_ref, rate_scr)
    source_col = turned(source)
    along, down = doc_tables(doc_ref)
    s, t = places((LIVE, ROWS))
    keep = (along[:LIVE] == down[:LIVE]) & (s <= t) & (t < live) & (s < live)
    bias = jnp.where(keep, 0.0, -1e30).astype(F32)
    half = lax.broadcasted_iota(jnp.int32, (ROWS, 128), 1) < HDIM
    c_proj = proj_refs[0][...].astype(F32)
    for proj_ref in proj_refs[1:]:
        c_proj = c_proj + proj_ref[...].astype(F32)
    c_proj = jnp.concatenate([c_proj.astype(BF16), jnp.zeros((ROWS - LIVE, STATE), BF16)], axis=0)
    affinity = lax.dot_general(
        b_ref[:LIVE, :], c_proj, (((1,), (1,)), ((), ())), preferred_element_type=F32
    )
    alive = s < live
    for p in range(HPG // 2):
        lanes = slice(p * 128, p * 128 + 128)
        g_pair = g_ref[:, lanes]
        zero = jnp.zeros_like(g_pair)
        both = jnp.concatenate([jnp.where(half, g_pair, zero), jnp.where(half, zero, g_pair)], axis=0)
        kernels = []
        for k in range(2):
            h = 2 * p + k
            gap = (source_col[:LIVE, h : h + 1] - totals[h : h + 1, :]) + bias
            kernels.append((jnp.exp2(gap) * affinity).astype(BF16))
        grads = jnp.dot(jnp.concatenate(kernels, axis=1), both, preferred_element_type=F32)
        first = q * HPG + 2 * p
        gain = jnp.where(half[:LIVE], skip_ref[first], skip_ref[first + 1])
        grads = grads + jnp.where(alive, gain * g_pair[:LIVE].astype(F32), 0.0)
        out_ref[:LIVE, lanes] = grads.astype(BF16)
    out_ref[LIVE:, :] = jnp.zeros((ROWS - LIVE, HPG * HDIM), BF16)


def scan_grad_call(kept, sends, skip, rate, docs, steps, out_grad, b_factors, shares):
    wide = HPG * HDIM
    return pl.pallas_call(
        scan_grad_kernel,
        grid=(GROUPS,),
        out_shape=jax.ShapeDtypeStruct((ROWS, D), BF16),
        in_specs=[
            pl.BlockSpec((32, 1), lambda q: (0, 0)),
            pl.BlockSpec((32, 32), lambda q: (0, 0)),
            smem(),
            row_spec(),
            row_spec(),
            pl.BlockSpec((HPG, ROWS), lambda q: (q, 0)),
            pl.BlockSpec((ROWS, wide), lambda q: (0, q)),
            pl.BlockSpec((ROWS, STATE), lambda q: (0, q)),
        ]
        + [pl.BlockSpec((LIVE, STATE), lambda q: (0, q))] * MEMBERS,
        out_specs=pl.BlockSpec((ROWS, wide), lambda q: (0, q)),
        scratch_shapes=[pltpu.VMEM((HEADS, HEADS), F32)],
        compiler_params=params(),
        cost_estimate=pl.CostEstimate(
            flops=4 * LIVE * ROWS * D, bytes_accessed=4 * ROWS * D, transcendentals=HEADS * LIVE * ROWS
        ),
        name="scan_grad",
    )(kept, sends, skip, rate, docs, steps, out_grad, b_factors, *shares)


def gather_grads(c_refs, grads):
    for c_ref, pair in zip(c_refs, sources()):
        for p in range(2):
            grads[pair[p]] = c_ref[p]


def weight_kernel(s_ref, *refs):
    c_refs, (keep_ref, send_ref, grads) = refs[:4], refs[4:]
    gather_grads(c_refs, grads)
    first_core = coordinates()["core"] == 0
    wide = 256
    rows = MEMBERS * LIVE
    for i in range(CHUNK // wide):
        part = lax.dot_general(
            s_ref[:, :, i * wide : (i + 1) * wide].reshape(rows, wide),
            grads[...].reshape(rows, NARROW),
            (((0,), (0,)), ((), ())),
            preferred_element_type=F32,
        ).reshape(8, 32, NARROW)
        place = slice(i // 2 * 8, i // 2 * 8 + 8)

        @pl.when(first_core == (i % 2 == 0))
        def _():
            keep_ref[place] = part

        @pl.when(first_core != (i % 2 == 0))
        def _():
            send_ref[place] = part


def weight_call(pieces, grads):
    vmem = pl.BlockSpec(memory_space=pltpu.VMEM)
    return pl.pallas_call(
        weight_kernel,
        out_shape=[jax.ShapeDtypeStruct((16, 32, NARROW), F32)] * 2,
        in_specs=[vmem] * 5,
        out_specs=[vmem, vmem],
        scratch_shapes=[pltpu.VMEM((MEMBERS, LIVE, NARROW), BF16)],
        compiler_params=params(),
        cost_estimate=pl.CostEstimate(
            flops=2 * MEMBERS * LIVE * CHUNK * NARROW, bytes_accessed=5 * 2**20, transcendentals=0
        ),
        name="weight_part",
    )(pieces, *grads)


def project_kernel(w_ref, s_ref, *refs):
    c_refs, refs = refs[:4], refs[4:]
    out_refs, (top_ref, grads, held) = refs[:MEMBERS], refs[MEMBERS:]
    gather_grads(c_refs, grads)
    rows = MEMBERS * LIVE
    wide = 256
    proj = jnp.dot(s_ref[...].reshape(rows, CHUNK), w_ref[...], preferred_element_type=F32)
    held[:, :, :NARROW] = proj.astype(BF16).reshape(MEMBERS, LIVE, NARROW)
    top = jnp.zeros((8, wide), F32)
    for i in range(CHUNK // wide):
        part = lax.dot_general(
            grads[...].reshape(rows, NARROW),
            w_ref[i * wide : (i + 1) * wide, :],
            (((1,), (1,)), ((), ())),
            preferred_element_type=F32,
        )
        held[:, :, NARROW + i * wide : NARROW + (i + 1) * wide] = part.astype(BF16).reshape(
            MEMBERS, LIVE, wide
        )
        top = jnp.maximum(top, jnp.max(jnp.abs(part).reshape(rows // 8, 8, wide), axis=0))
    for out_ref, f in zip(out_refs, rows_at(1)):
        out_ref[...] = held[f]
    top_ref[...] = jnp.broadcast_to(jnp.max(top), (1, 128))


def project_call(weights, pieces, grads):
    vmem = pl.BlockSpec(memory_space=pltpu.VMEM)
    out = pl.pallas_call(
        project_kernel,
        out_shape=[jax.ShapeDtypeStruct((LIVE, BOTH), BF16)] * MEMBERS
        + [jax.ShapeDtypeStruct((1, 128), F32)],
        in_specs=[vmem] * 6,
        out_specs=[vmem] * 9,
        scratch_shapes=[
            pltpu.VMEM((MEMBERS, LIVE, NARROW), BF16),
            pltpu.VMEM((MEMBERS, LIVE, BOTH), BF16),
        ],
        compiler_params=params(),
        cost_estimate=pl.CostEstimate(
            flops=4 * MEMBERS * LIVE * CHUNK * NARROW, bytes_accessed=6 * 2**20, transcendentals=0
        ),
        name="project",
    )(weights, pieces, *grads)
    return out[:MEMBERS], out[MEMBERS]


def peak_kernel(parts_ref, top_ref, sum_ref, tops_ref):
    total = parts_ref[0].astype(F32)
    for i in range(1, 16):
        total = total + parts_ref[i].astype(F32)
    sum_ref[...] = total
    lane = lax.broadcasted_iota(jnp.int32, (1, 128), 1)
    both = jnp.where(lane < 64, top_ref[...], jnp.max(jnp.abs(total)))
    tops_ref[...] = jnp.broadcast_to(both[None], (256, 1, 128))


def peak_call(parts, top):
    vmem = pl.BlockSpec(memory_space=pltpu.VMEM)
    return pl.pallas_call(
        peak_kernel,
        out_shape=[
            jax.ShapeDtypeStruct((32, NARROW), F32),
            jax.ShapeDtypeStruct((256, 1, 128), F32),
        ],
        in_specs=[vmem, vmem],
        out_specs=[vmem, vmem],
        compiler_params=params(),
        cost_estimate=pl.CostEstimate(flops=16 * 32 * NARROW, bytes_accessed=2**20, transcendentals=0),
        name="peaks",
    )(parts, top)


def finish_kernel(tops_ref, sum_ref, *refs):
    back_refs, (input_ref, weight_ref, held, sems) = refs[:MEMBERS], refs[MEMBERS:]
    tops = jnp.max(tops_ref[...], axis=0)
    scale = 1.0 / (tops[:, :1] + peak_eps)
    copies = []
    for i, (ref, f) in enumerate(zip(back_refs, rows_at(-1))):
        held[i, :LIVE] = (ref[:, NARROW:].astype(F32) * scale).astype(BF16)
        held[i, LIVE:] = jnp.zeros((ROWS - LIVE, CHUNK), BF16)
        columns = pl.ds(pl.multiple_of(f * CHUNK, CHUNK), CHUNK)
        copies.append(pltpu.make_async_copy(held.at[i], input_ref.at[:, columns], sems.at[i]))
        copies[-1].start()
    weight_ref[...] = sum_ref[...] / (tops[:, 64:65] + peak_eps)
    for copy in copies:
        copy.wait()


def finish_call(tops, back, weight_sum):
    vmem = pl.BlockSpec(memory_space=pltpu.VMEM)
    return pl.pallas_call(
        finish_kernel,
        out_shape=[
            jax.ShapeDtypeStruct((ROWS, D), BF16),
            jax.ShapeDtypeStruct((32, NARROW), F32),
        ],
        in_specs=[vmem] * 10,
        out_specs=[pl.BlockSpec(memory_space=pl.ANY), vmem],
        scratch_shapes=[
            pltpu.VMEM((MEMBERS, ROWS, CHUNK), BF16),
            pltpu.SemaphoreType.DMA((MEMBERS,)),
        ],
        compiler_params=params(),
        cost_estimate=pl.CostEstimate(flops=LIVE * D, bytes_accessed=4 * ROWS * D, transcendentals=0),
        name="finish",
    )(tops, weight_sum, *back)


def shards(
    section_input,
    c_weight,
    scan_input,
    b_factors,
    step_size,
    decay_rate,
    skip_gain,
    out_grad,
    doc_index,
    kept_rows,
    send_counts,
):
    kept = kept_rows.reshape(32, 1)
    sends = send_counts.reshape(32, 32)
    rate, docs = decay_rate.reshape(1, HEADS), doc_index.reshape(1, ROWS)

    pieces = exchange(pack(section_input), WIDE)

    c_own = c_grad_call(kept, sends, rate, docs, step_size, out_grad, scan_input, b_factors)
    grads = along_x(jnp.stack([c_own, to_pair(c_own)]))

    keep, send = weight_call(pieces, grads)
    parts = (keep + to_core(send)).astype(BF16)
    parts = lax.all_to_all(parts, "dp", 0, 0, axis_index_groups=SAME_CORE)

    both, top = project_call(c_weight, pieces, grads)
    both = [both[0]] + [lax.ppermute(value, ALL, moved(*step)) for value, step in zip(both[1:], STEPS[1:])]
    weight_sum, tops = peak_call(parts, top)
    tops = exchange(tops, None)
    weight_sum = lax.ppermute(weight_sum, ALL, HOME)
    scan_grad = scan_grad_call(
        kept, sends, skip_gain, rate, docs, step_size, out_grad, b_factors, both
    )
    input_grad, readout_weight_gradient = finish_call(tops, both, weight_sum)
    return (input_grad, scan_grad, readout_weight_gradient)


def solution(mesh):
    rows = P(ALL, None)
    placed = (
        rows,
        P("fsdp", None),
        rows,
        rows,
        P(None, ALL),
        P(),
        P(),
        rows,
        P(ALL),
        P(None, "fsdp"),
        P(None, "fsdp", None),
    )
    return jax.shard_map(
        shards, mesh=mesh, in_specs=placed, out_specs=(rows, rows, rows), check_vma=False
    )
```

time: 201 us -> 128 us (0.64)
  blocking collectives: 66.8 us -> 0 us
  between operations: 15.5 us -> 1 us
  Pallas kernels: 23.8 us -> 38 us
  matrix products: 13.7 us -> 0 us
  starting transfers between devices: 44 us -> 55.7 us
  waiting for transfers between devices: 20 us -> 24.2 us
  other arithmetic: 6.81 us -> 3.09 us
  local copies, waits for them, and re-layouts: 9.13 us -> 5.5 us
    all_to_all x1 -> x0, blocking collectives: 66.8 us -> none  [shards(): mine = lax.all_to_all(mine, 'dp', 0, 0, axis_index_groups=SAME_CORE)]
    all_to_all x1 -> x3, starting transfers between devices: 11.6 us -> 30.1 us  [the longest x2 21.8 us: exchange(): return lax.all_to_all(value, ALL, 0, 0, axis_index_groups=groups)]
    dot_general x2 -> x0, matrix products: 13.7 us -> none  [the longest x1 8.87 us: shards(): lax.dot_general(c_full, weights, (((1,), (1,)), ((), ())), preferred_elem...]
    pallas_call x2 -> x5, Pallas kernels: 14.3 us -> 24.6 us  [the longest x1 8.18 us: c_grad_call(): pl.pallas_call(c_grad_kernel, grid=(GROUPS,), out_shape=jax.ShapeDtypeStr...]
    ppermute x15 -> x13, starting transfers between devices: 32.3 us -> 25.6 us  [the longest x7 10.6 us: shards(): lax.ppermute(value, ALL, moved(*step))]
    ppermute x15 -> x13, waiting for transfers between devices: 19.3 us -> 24.2 us  [the longest x1 11.4 us: to_pair(): return lax.ppermute(value, ALL, moved(0, 1))]
    pallas_call x1, Pallas kernels: 1.56 us -> 4.76 us  [weight_call(): pl.pallas_call(weight_kernel, out_shape=[jax.ShapeDtypeStruct((16, 32, NA...]
    unnamed x31 -> x33, local copies, waits for them, and re-layouts: 7.74 us -> 5.5 us
  transfers between devices with their start and end apart: 17 -> 16, of which waited for: 8 -> 6; matrix products, arithmetic and copies ran while one was open for 3% -> 1% of each run, Pallas kernels for 12% -> 19%
where the time goes in v2:
time: 128 us; the launch traced here: 127 us
  starting transfers between devices  55.7 us (44%)
  Pallas kernels  38 us (30%)
  waiting for transfers between devices  24.2 us (19%)
  local copies, waits for them, and re-layouts  5.5 us (4%)
  other arithmetic  3.09 us (2%)
    all_to_all x2, starting transfers between devices, exchange(): return lax.all_to_all(value, ALL, 0, 0, axis_index_groups=groups)  21.8 us
    ppermute x1, waiting for transfers between devices, to_pair(): return lax.ppermute(value, ALL, moved(0, 1))  11.4 us
    ppermute x7, starting transfers between devices, shards(): lax.ppermute(value, ALL, moved(*step))  10.6 us
    pallas_call x1, Pallas kernels, scan_grad_call(): pl.pallas_call(scan_grad_kernel, grid=(GROUPS,), out_shape=jax.ShapeDtype...  8.6 us
    all_to_all x1, starting transfers between devices, shards(): parts = lax.all_to_all(parts, 'dp', 0, 0, axis_index_groups=SAME_CORE)  8.29 us
    pallas_call x1, Pallas kernels, c_grad_call(): pl.pallas_call(c_grad_kernel, grid=(GROUPS,), out_shape=jax.ShapeDtypeStr...  8.18 us
    ppermute x1, starting transfers between devices, shards(): weight_sum = lax.ppermute(weight_sum, ALL, HOME)  7.93 us
    ppermute x3, waiting for transfers between devices, along_x(): lax.ppermute(value, ALL, moved(dx, 0))  7.87 us
  transfers between devices with their start and end apart: 16, of which 6 were waited for; matrix products, arithmetic and copies ran while one was open for 1% of the time, Pallas kernels for 19%

profile of v2, /device:TPU:5, one launch (start us, length us, event | category | flops | bytes accessed | tf_op | source)
XLA Modules:
  0.0 127.4 jit_solution(12961013460864487189)
XLA Ops:
  0.6 5.4 %pack.1 = bf16[8,96,1024]{2,1,0:T(8,128)(2,1)} custom-call(bf16[128,8192]{1,0:T(8,128)(2,1)} %s_ref.1), custom_call_target="tpu_custom_call" | custom-call | bytes 3145728 | tf_op jit(solution)/shard_map/pack/pallas_call | solution.py:103
  6.1 6.8 %all-to-all-start = ((bf16[8,96,1024]{2,1,0:T(8,128)(2,1)}), bf16[8,96,1024]{2,1,0:T(8,128)(2,1)S(1)}, u32[]{:S(2)}, u32[]{:S(2)}) async-start(bf16[8,96,1024]{2,1,0:T(8,128)(2,1)} %pack.1), calls=%async_computation | async-start | bytes 3145728 | tf_op jit(solution)/shard_map/all_to_all | solution.py:64
  12.9 0.7 copy.14.kept_ref
  13.6 8.2 %c_grad.1 = bf16[96,512]{1,0:T(8,128)(2,1)} custom-call(s32[32,1]{1,0:T(8,128)} %copy.14.kept_ref, s32[32,32]{1,0:T(8,128)} %bitcast.7, f32[1,128]{1,0:T(1,128)} %bitcast.9, s32[1,128]{1,0:T(1,128)} %bitcast.11, f32[128,128]{1,0:T(8,128)} %step_ref.3, bf16[128,8192]{1,0:T(8,128)(2,1)} %g_ref.3, bf16[128,8192]{1,0:T(8,128)(2,1)} %x_ref.1, bf16[128,512]{1,0:T(8,128)(2,1)} %b_ref.3), custom_call_target="tpu_custom_call" | custom-call | flops 402653184 | bytes 4194304 | tf_op jit(solution)/shard_map/c_grad/pallas_call | solution.py:189
  21.8 2.4 %collective-permute-start = (bf16[96,512]{1,0:T(8,128)(2,1)}, bf16[96,512]{1,0:T(8,128)(2,1)S(1)}, u32[]{:S(2)}, u32[]{:S(2)}) collective-permute-start(bf16[96,512]{1,0:T(8,128)(2,1)} %c_grad.1), channel_id=1, source_target_pairs={{0,132},{8,140},{16,148},{24,156},{32,164},{40,172},{48,180},{56,1... | collective-permute-start | bytes 294920 | tf_op jit(solution)/shard_map/ppermute | solution.py:72
  24.1 11.4 %collective-permute-done = bf16[96,512]{1,0:T(8,128)(2,1)S(1)} collective-permute-done((bf16[96,512]{1,0:T(8,128)(2,1)}, bf16[96,512]{1,0:T(8,128)(2,1)S(1)}, u32[]{:S(2)}, u32[]{:S(2)}) %collective-permute-start) | collective-permute-done | bytes 98336 | tf_op jit(solution)/shard_map/ppermute | solution.py:72
  35.6 0.9 pad_maximum_fusion.refs_0_
  36.5 1.0 collective-permute-start.1
  38.1 1.8 %collective-permute-start.3 = (bf16[2,96,512]{2,1,0:T(8,128)(2,1)S(1)}, bf16[2,96,512]{2,1,0:T(8,128)(2,1)S(1)}, u32[]{:S(2)}, u32[]{:S(2)}) collective-permute-start(bf16[2,96,512]{2,1,0:T(8,128)(2,1)S(1)} %pad_maximum_fusion.refs_0_), channel_id=1, source_target_pairs={{0,2},{8,10},{16,18},{24,26},{32,34},{40,42},{48,50},{56,58},{64,6... | collective-permute-start | bytes 589832 | tf_op jit(solution)/shard_map/ppermute | solution.py:68
  39.8 2.8 %collective-permute-done.1.refs_1_ = bf16[2,96,512]{2,1,0:T(8,128)(2,1)S(1)} collective-permute-done((bf16[2,96,512]{2,1,0:T(8,128)(2,1)S(1)}, bf16[2,96,512]{2,1,0:T(8,128)(2,1)S(1)}, u32[]{:S(2)}, u32[]{:S(2)}) %collective-permute-start.1) | collective-permute-done | bytes 196640 | tf_op jit(solution)/shard_map/ppermute | solution.py:68
  43.1 4.5 %collective-permute-done.3.refs_3_ = bf16[2,96,512]{2,1,0:T(8,128)(2,1)S(1)} collective-permute-done((bf16[2,96,512]{2,1,0:T(8,128)(2,1)S(1)}, bf16[2,96,512]{2,1,0:T(8,128)(2,1)S(1)}, u32[]{:S(2)}, u32[]{:S(2)}) %collective-permute-start.3) | collective-permute-done | bytes 196640 | tf_op jit(solution)/shard_map/ppermute | solution.py:68
  48.4 1.1 copy-done.1
  49.5 4.8 %weight_part.1 = (f32[16,32,512]{2,1,0:T(8,128)}, f32[16,32,512]{2,1,0:T(8,128)}) custom-call(bf16[8,96,1024]{2,1,0:T(8,128)(2,1)} %copy-done.1, bf16[2,96,512]{2,1,0:T(8,128)(2,1)} %copy-done.10, bf16[2,96,512]{2,1,0:T(8,128)(2,1)} %copy-done.13, bf16[2,96,512]{2,1,0:T(8,128)(2,1)} %copy-done.14, bf16[2,96,512]{2,1,0:T(8,128)(2,1)} %copy-done.15), custom_call_target="tpu_custom_call" | custom-call | flops 805306368 | bytes 5242880 | tf_op jit(solution)/shard_map/weight_part/pallas_call | solution.py:311
  54.3 1.3 %collective-permute-start.4 = (f32[16,32,512]{2,1,0:T(8,128)}, f32[16,32,512]{2,1,0:T(8,128)S(1)}, u32[]{:S(2)}, u32[]{:S(2)}) collective-permute-start(f32[16,32,512]{2,1,0:T(8,128)} %get-tuple-element.19), channel_id=1, source_target_pairs={{0,8},{8,0},{16,24},{24,16},{32,40},{40,32},{48,56},{56,48},{64,72... | collective-permute-start | bytes 3145736 | tf_op jit(solution)/shard_map/ppermute | solution.py:76
  55.6 2.5 %collective-permute-done.4 = f32[16,32,512]{2,1,0:T(8,128)S(1)} collective-permute-done((f32[16,32,512]{2,1,0:T(8,128)}, f32[16,32,512]{2,1,0:T(8,128)S(1)}, u32[]{:S(2)}, u32[]{:S(2)}) %collective-permute-start.4) | collective-permute-done | bytes 1048608 | tf_op jit(solution)/shard_map/ppermute | solution.py:76
  58.1 2.2 %add_convert_fusion = bf16[16,32,512]{2,1,0:T(8,128)(2,1)} fusion(f32[16,32,512]{2,1,0:T(8,128)} %get-tuple-element.18, f32[16,32,512]{2,1,0:T(8,128)S(1)} %collective-permute-done.4), kind=kLoop, calls=%fused_computation | loop fusion | flops 524288 | bytes 2621440 | tf_op jit(solution)/shard_map/convert_element_type | solution.py:456
  60.3 8.3 %all-to-all-start.1 = ((bf16[16,32,512]{2,1,0:T(8,128)(2,1)}), bf16[16,32,512]{2,1,0:T(8,128)(2,1)S(1)}, u32[]{:S(2)}, u32[]{:S(2)}) async-start(bf16[16,32,512]{2,1,0:T(8,128)(2,1)} %add_convert_fusion), calls=%async_computation.1 | async-start | bytes 1048576 | tf_op jit(solution)/shard_map/all_to_all | solution.py:457
  68.6 5.2 %project.1 = (bf16[96,1536]{1,0:T(8,128)(2,1)}, bf16[96,1536]{1,0:T(8,128)(2,1)}, bf16[96,1536]{1,0:T(8,128)(2,1)}, bf16[96,1536]{1,0:T(8,128)(2,1)}, bf16[96,15...) custom-call(bf16[1024,512]{1,0:T(8,128)(2,1)} %w_ref.1, ...), custom_call_target="tpu_custom_call" | custom-call | flops 1610612736 | bytes 6291456 | tf_op jit(solution)/shard_map/project/pallas_call | solution.py:352
  73.8 1.3 %collective-permute-start.6 = (bf16[96,1536]{1,0:T(8,128)(2,1)}, bf16[96,1536]{1,0:T(8,128)(2,1)S(1)}, u32[]{:S(2)}, u32[]{:S(2)}) collective-permute-start(bf16[96,1536]{1,0:T(8,128)(2,1)} %get-tuple-element.24), channel_id=1, source_target_pairs={{0,132},{8,140},{16,148},{24,156},{32,164},{40,172},{48,180},{56,1... | collective-permute-start | bytes 884744 | tf_op jit(solution)/shard_map/ppermute | solution.py:460
  75.1 2.1 %collective-permute-start.7 = (bf16[96,1536]{1,0:T(8,128)(2,1)}, bf16[96,1536]{1,0:T(8,128)(2,1)S(1)}, u32[]{:S(2)}, u32[]{:S(2)}) collective-permute-start(bf16[96,1536]{1,0:T(8,128)(2,1)} %get-tuple-element.25), channel_id=1, source_target_pairs={{0,1},{8,9},{16,17},{24,25},{32,33},{40,41},{48,49},{56,57},{64,65... | collective-permute-start | bytes 884744 | tf_op jit(solution)/shard_map/ppermute | solution.py:460
  77.2 1.4 %collective-permute-start.8 = (bf16[96,1536]{1,0:T(8,128)(2,1)}, bf16[96,1536]{1,0:T(8,128)(2,1)S(1)}, u32[]{:S(2)}, u32[]{:S(2)}) collective-permute-start(bf16[96,1536]{1,0:T(8,128)(2,1)} %get-tuple-element.26), channel_id=1, source_target_pairs={{0,133},{8,141},{16,149},{24,157},{32,165},{40,173},{48,181},{56,1... | collective-permute-start | bytes 884744 | tf_op jit(solution)/shard_map/ppermute | solution.py:460
  78.5 1.2 collective-permute-start.9
  79.7 1.0 collective-permute-start.10
  80.7 2.4 %collective-permute-done.6.refs_1_ = bf16[96,1536]{1,0:T(8,128)(2,1)S(1)} collective-permute-done((bf16[96,1536]{1,0:T(8,128)(2,1)}, bf16[96,1536]{1,0:T(8,128)(2,1)S(1)}, u32[]{:S(2)}, u32[]{:S(2)}) %collective-permute-start.6) | collective-permute-done | bytes 294944 | tf_op jit(solution)/shard_map/ppermute | solution.py:460
  83.1 1.5 %collective-permute-start.11 = (bf16[96,1536]{1,0:T(8,128)(2,1)}, bf16[96,1536]{1,0:T(8,128)(2,1)S(1)}, u32[]{:S(2)}, u32[]{:S(2)}) collective-permute-start(bf16[96,1536]{1,0:T(8,128)(2,1)} %get-tuple-element.29), channel_id=1, source_target_pairs={{0,2},{8,10},{16,18},{24,26},{32,34},{40,42},{48,50},{56,58},{64,6... | collective-permute-start | bytes 884744 | tf_op jit(solution)/shard_map/ppermute | solution.py:460
  84.6 2.2 %collective-permute-start.12 = (bf16[96,1536]{1,0:T(8,128)(2,1)}, bf16[96,1536]{1,0:T(8,128)(2,1)S(1)}, u32[]{:S(2)}, u32[]{:S(2)}) collective-permute-start(bf16[96,1536]{1,0:T(8,128)(2,1)} %get-tuple-element.30), channel_id=1, source_target_pairs={{0,134},{8,142},{16,150},{24,158},{32,166},{40,174},{48,182},{56,1... | collective-permute-start | bytes 884744 | tf_op jit(solution)/shard_map/ppermute | solution.py:460
  86.8 0.8 copy-done
  87.6 2.0 %peaks.1 = (f32[32,512]{1,0:T(8,128)}, f32[256,1,128]{2,1,0:T(1,128)}) custom-call(bf16[16,32,512]{2,1,0:T(8,128)(2,1)} %copy-done, f32[1,128]{1,0:T(1,128)} %get-tuple-element.20.top_ref), custom_call_target="tpu_custom_call" | custom-call | flops 262144 | bytes 1048576 | tf_op jit(solution)/shard_map/peaks/pallas_call | solution.py:383
  89.5 15.0 %all-to-all-start.2 = ((f32[256,1,128]{2,1,0:T(1,128)}), f32[256,1,128]{2,1,0:T(1,128)S(1)}, u32[]{:S(2)}, u32[]{:S(2)}) async-start(f32[256,1,128]{2,1,0:T(1,128)} %get-tuple-element.21), calls=%async_computation.2 | async-start | bytes 262144 | tf_op jit(solution)/shard_map/all_to_all | solution.py:64
  104.5 7.9 %collective-permute-start.5 = (f32[32,512]{1,0:T(8,128)}, f32[32,512]{1,0:T(8,128)S(1)}, u32[]{:S(2)}, u32[]{:S(2)}) collective-permute-start(f32[32,512]{1,0:T(8,128)} %get-tuple-element.22), channel_id=1, source_target_pairs={{0,0},{8,8},{16,1},{24,9},{32,2},{40,10},{48,3},{56,11},{64,4},{72... | collective-permute-start | bytes 196616 | tf_op jit(solution)/shard_map/ppermute | solution.py:463
  113.5 8.6 %scan_grad.1 = bf16[128,8192]{1,0:T(8,128)(2,1)} custom-call(s32[32,1]{1,0:T(8,128)} %copy.14.kept_ref, s32[32,32]{1,0:T(8,128)} %bitcast.8, f32[128]{0:T(128)} %skip_ref.1, f32[1,128]{1,0:T(1,128)} %bitcast.10, s32[1,128]{1,0:T(1,128)} %bitcast.12, f32[128,128]{1,0:T(8,128)} %step_ref.3, bf16[128,8192]{1,0:T(8,128)(2,1)} %g_ref.3, bf16[128,512]{1,0:T(8,128)(2,1)} %b_ref.3, ...), custom_call_target="tpu_custom_call" | custom-call | flops 402653184 | bytes 4194304 | tf_op jit(solution)/shard_map/scan_grad/pallas_call | solution.py:254
  123.4 3.9 %finish.1 = (bf16[128,8192]{1,0:T(8,128)(2,1)}, f32[32,512]{1,0:T(8,128)}) custom-call(f32[256,1,128]{2,1,0:T(1,128)} %copy-done.9, f32[32,512]{1,0:T(8,128)} %copy-done.11, bf16[96,1536]{1,0:T(8,128)(2,1)} %get-tuple-element.23.refs_0_, bf16[96,1536]{1,0:T(8,128)(2,1)} %copy-done.2, bf16[96,1536]{1,0:T(8,128)(2,1)} %copy-done.3, ...), custom_call_target="tpu_custom_call" | custom-call | flops 786432 | bytes 4194304 | tf_op jit(solution)/shard_map/finish/pallas_call | solution.py:415
  (42 shorter events, 4.0 us)
Async XLA Ops:
  6.0 6.8 %copy-start.12 = (s32[32,1]{0,1:T(1,128)S(1)}, s32[32,1]{0,1:T(1,128)}, u32[]{:S(2)}) copy-start(s32[32,1]{0,1:T(1,128)} %param.20) | copy-start | bytes 388
  6.1 41.6 %all-to-all-start = ((bf16[8,96,1024]{2,1,0:T(8,128)(2,1)}), bf16[8,96,1024]{2,1,0:T(8,128)(2,1)S(1)}, u32[]{:S(2)}, u32[]{:S(2)}) async-start(bf16[8,96,1024]{2,1,0:T(8,128)(2,1)} %pack.1), calls=%async_computation | async-start | bytes 3145728 | tf_op jit(solution)/shard_map/all_to_all | solution.py:64
  21.8 13.8 %collective-permute-start = (bf16[96,512]{1,0:T(8,128)(2,1)}, bf16[96,512]{1,0:T(8,128)(2,1)S(1)}, u32[]{:S(2)}, u32[]{:S(2)}) collective-permute-start(bf16[96,512]{1,0:T(8,128)(2,1)} %c_grad.1), channel_id=1, source_target_pairs={{0,132},{8,140},{16,148},{24,156},{32,164},{40,172},{48,180},{56,1... | collective-permute-start | bytes 294920 | tf_op jit(solution)/shard_map/ppermute | solution.py:72
  36.5 11.2 %copy-start.10 = (bf16[2,96,512]{2,1,0:T(8,128)(2,1)}, bf16[2,96,512]{2,1,0:T(8,128)(2,1)S(1)}, u32[]{:S(2)}) copy-start(bf16[2,96,512]{2,1,0:T(8,128)(2,1)S(1)} %pad_maximum_fusion.refs_0_) | copy-start | bytes 589828
  36.5 6.1 %collective-permute-start.1 = (bf16[2,96,512]{2,1,0:T(8,128)(2,1)S(1)}, bf16[2,96,512]{2,1,0:T(8,128)(2,1)S(1)}, u32[]{:S(2)}, u32[]{:S(2)}) collective-permute-start(bf16[2,96,512]{2,1,0:T(8,128)(2,1)S(1)} %pad_maximum_fusion.refs_0_), channel_id=1, source_target_pairs={{0,1},{8,9},{16,17},{24,25},{32,33},{40,41},{48,49},{56,57},{64,65... | collective-permute-start | bytes 589832 | tf_op jit(solution)/shard_map/ppermute | solution.py:68
  37.5 5.7 %collective-permute-start.2 = (bf16[2,96,512]{2,1,0:T(8,128)(2,1)S(1)}, bf16[2,96,512]{2,1,0:T(8,128)(2,1)S(1)}, u32[]{:S(2)}, u32[]{:S(2)}) collective-permute-start(bf16[2,96,512]{2,1,0:T(8,128)(2,1)S(1)} %pad_maximum_fusion.refs_0_), channel_id=1, source_target_pairs={{0,3},{8,11},{16,19},{24,27},{32,35},{40,43},{48,51},{56,59},{64,6... | collective-permute-start | bytes 589832 | tf_op jit(solution)/shard_map/ppermute | solution.py:68
  38.1 9.6 %collective-permute-start.3 = (bf16[2,96,512]{2,1,0:T(8,128)(2,1)S(1)}, bf16[2,96,512]{2,1,0:T(8,128)(2,1)S(1)}, u32[]{:S(2)}, u32[]{:S(2)}) collective-permute-start(bf16[2,96,512]{2,1,0:T(8,128)(2,1)S(1)} %pad_maximum_fusion.refs_0_), channel_id=1, source_target_pairs={{0,2},{8,10},{16,18},{24,26},{32,34},{40,42},{48,50},{56,58},{64,6... | collective-permute-start | bytes 589832 | tf_op jit(solution)/shard_map/ppermute | solution.py:68
  42.6 5.1 %copy-start.13 = (bf16[2,96,512]{2,1,0:T(8,128)(2,1)}, bf16[2,96,512]{2,1,0:T(8,128)(2,1)S(1)}, u32[]{:S(2)}) copy-start(bf16[2,96,512]{2,1,0:T(8,128)(2,1)S(1)} %collective-permute-done.1.refs_1_) | copy-start | bytes 589828
  43.1 4.6 %copy-start.14 = (bf16[2,96,512]{2,1,0:T(8,128)(2,1)}, bf16[2,96,512]{2,1,0:T(8,128)(2,1)S(1)}, u32[]{:S(2)}) copy-start(bf16[2,96,512]{2,1,0:T(8,128)(2,1)S(1)} %collective-permute-done.2.refs_2_) | copy-start | bytes 589828
  47.7 0.7 copy-start.15
  48.4 1.1 copy-start.1
  54.3 3.8 %collective-permute-start.4 = (f32[16,32,512]{2,1,0:T(8,128)}, f32[16,32,512]{2,1,0:T(8,128)S(1)}, u32[]{:S(2)}, u32[]{:S(2)}) collective-permute-start(f32[16,32,512]{2,1,0:T(8,128)} %get-tuple-element.19), channel_id=1, source_target_pairs={{0,8},{8,0},{16,24},{24,16},{32,40},{40,32},{48,56},{56,48},{64,72... | collective-permute-start | bytes 3145736 | tf_op jit(solution)/shard_map/ppermute | solution.py:76
  60.3 26.5 %all-to-all-start.1 = ((bf16[16,32,512]{2,1,0:T(8,128)(2,1)}), bf16[16,32,512]{2,1,0:T(8,128)(2,1)S(1)}, u32[]{:S(2)}, u32[]{:S(2)}) async-start(bf16[16,32,512]{2,1,0:T(8,128)(2,1)} %add_convert_fusion), calls=%async_computation.1 | async-start | bytes 1048576 | tf_op jit(solution)/shard_map/all_to_all | solution.py:457
  73.8 9.3 %collective-permute-start.6 = (bf16[96,1536]{1,0:T(8,128)(2,1)}, bf16[96,1536]{1,0:T(8,128)(2,1)S(1)}, u32[]{:S(2)}, u32[]{:S(2)}) collective-permute-start(bf16[96,1536]{1,0:T(8,128)(2,1)} %get-tuple-element.24), channel_id=1, source_target_pairs={{0,132},{8,140},{16,148},{24,156},{32,164},{40,172},{48,180},{56,1... | collective-permute-start | bytes 884744 | tf_op jit(solution)/shard_map/ppermute | solution.py:460
  75.1 9.5 %collective-permute-start.7 = (bf16[96,1536]{1,0:T(8,128)(2,1)}, bf16[96,1536]{1,0:T(8,128)(2,1)S(1)}, u32[]{:S(2)}, u32[]{:S(2)}) collective-permute-start(bf16[96,1536]{1,0:T(8,128)(2,1)} %get-tuple-element.25), channel_id=1, source_target_pairs={{0,1},{8,9},{16,17},{24,25},{32,33},{40,41},{48,49},{56,57},{64,65... | collective-permute-start | bytes 884744 | tf_op jit(solution)/shard_map/ppermute | solution.py:460
  77.2 27.3 %collective-permute-start.8 = (bf16[96,1536]{1,0:T(8,128)(2,1)}, bf16[96,1536]{1,0:T(8,128)(2,1)S(1)}, u32[]{:S(2)}, u32[]{:S(2)}) collective-permute-start(bf16[96,1536]{1,0:T(8,128)(2,1)} %get-tuple-element.26), channel_id=1, source_target_pairs={{0,133},{8,141},{16,149},{24,157},{32,165},{40,173},{48,181},{56,1... | collective-permute-start | bytes 884744 | tf_op jit(solution)/shard_map/ppermute | solution.py:460
  78.5 33.9 %collective-permute-start.9 = (bf16[96,1536]{1,0:T(8,128)(2,1)}, bf16[96,1536]{1,0:T(8,128)(2,1)S(1)}, u32[]{:S(2)}, u32[]{:S(2)}) collective-permute-start(bf16[96,1536]{1,0:T(8,128)(2,1)} %get-tuple-element.27), channel_id=1, source_target_pairs={{0,3},{8,11},{16,19},{24,27},{32,35},{40,43},{48,51},{56,59},{64,6... | collective-permute-start | bytes 884744 | tf_op jit(solution)/shard_map/ppermute | solution.py:460
  79.7 32.8 %collective-permute-start.10 = (bf16[96,1536]{1,0:T(8,128)(2,1)}, bf16[96,1536]{1,0:T(8,128)(2,1)S(1)}, u32[]{:S(2)}, u32[]{:S(2)}) collective-permute-start(bf16[96,1536]{1,0:T(8,128)(2,1)} %get-tuple-element.28), channel_id=1, source_target_pairs={{0,135},{8,143},{16,151},{24,159},{32,167},{40,175},{48,183},{56,1... | collective-permute-start | bytes 884744 | tf_op jit(solution)/shard_map/ppermute | solution.py:460
  83.1 29.4 %copy-start.2 = (bf16[96,1536]{1,0:T(8,128)(2,1)}, bf16[96,1536]{1,0:T(8,128)(2,1)S(1)}, u32[]{:S(2)}) copy-start(bf16[96,1536]{1,0:T(8,128)(2,1)S(1)} %collective-permute-done.6.refs_1_) | copy-start | bytes 884740
  83.1 29.4 %collective-permute-start.11 = (bf16[96,1536]{1,0:T(8,128)(2,1)}, bf16[96,1536]{1,0:T(8,128)(2,1)S(1)}, u32[]{:S(2)}, u32[]{:S(2)}) collective-permute-start(bf16[96,1536]{1,0:T(8,128)(2,1)} %get-tuple-element.29), channel_id=1, source_target_pairs={{0,2},{8,10},{16,18},{24,26},{32,34},{40,42},{48,50},{56,58},{64,6... | collective-permute-start | bytes 884744 | tf_op jit(solution)/shard_map/ppermute | solution.py:460
  84.6 28.0 %copy-start.3 = (bf16[96,1536]{1,0:T(8,128)(2,1)}, bf16[96,1536]{1,0:T(8,128)(2,1)S(1)}, u32[]{:S(2)}) copy-start(bf16[96,1536]{1,0:T(8,128)(2,1)S(1)} %collective-permute-done.7.refs_2_) | copy-start | bytes 884740
  84.6 27.9 %collective-permute-start.12 = (bf16[96,1536]{1,0:T(8,128)(2,1)}, bf16[96,1536]{1,0:T(8,128)(2,1)S(1)}, u32[]{:S(2)}, u32[]{:S(2)}) collective-permute-start(bf16[96,1536]{1,0:T(8,128)(2,1)} %get-tuple-element.30), channel_id=1, source_target_pairs={{0,134},{8,142},{16,150},{24,158},{32,166},{40,174},{48,182},{56,1... | collective-permute-start | bytes 884744 | tf_op jit(solution)/shard_map/ppermute | solution.py:460
  86.8 0.8 copy-start
  89.5 32.6 %all-to-all-start.2 = ((f32[256,1,128]{2,1,0:T(1,128)}), f32[256,1,128]{2,1,0:T(1,128)S(1)}, u32[]{:S(2)}, u32[]{:S(2)}) async-start(f32[256,1,128]{2,1,0:T(1,128)} %get-tuple-element.21), calls=%async_computation.2 | async-start | bytes 262144 | tf_op jit(solution)/shard_map/all_to_all | solution.py:64
  104.5 8.0 %copy-start.4 = (bf16[96,1536]{1,0:T(8,128)(2,1)}, bf16[96,1536]{1,0:T(8,128)(2,1)S(1)}, u32[]{:S(2)}) copy-start(bf16[96,1536]{1,0:T(8,128)(2,1)S(1)} %collective-permute-done.8.refs_3_) | copy-start | bytes 884740
  104.5 17.6 %collective-permute-start.5 = (f32[32,512]{1,0:T(8,128)}, f32[32,512]{1,0:T(8,128)S(1)}, u32[]{:S(2)}, u32[]{:S(2)}) collective-permute-start(f32[32,512]{1,0:T(8,128)} %get-tuple-element.22), channel_id=1, source_target_pairs={{0,0},{8,8},{16,1},{24,9},{32,2},{40,10},{48,3},{56,11},{64,4},{72... | collective-permute-start | bytes 196616 | tf_op jit(solution)/shard_map/ppermute | solution.py:463
  112.5 0.7 copy-start.5
  112.5 0.8 copy-start.6
  112.5 0.9 copy-start.7
  112.5 0.9 copy-start.8
  122.1 0.6 copy-start.11
  122.7 0.7 copy-start.9

commit v3 on v2

--- a/solution.py
+++ b/solution.py
@@ -91,21 +91,30 @@
     return [behind[2 * i : 2 * i + 2] for i in range(4)]
 
 
-def params():
-    return pltpu.CompilerParams(vmem_limit_bytes=VMEM_LIMIT)
-
-
-def pack_kernel(s_ref, wide_ref):
-    wide_ref[0] = s_ref[...]
+def params(limit=VMEM_LIMIT):
+    return pltpu.CompilerParams(vmem_limit_bytes=limit)
+
+
+def pack_kernel(s_ref, wide_ref, sems):
+    copies = [
+        pltpu.make_async_copy(
+            s_ref.at[pl.ds(0, LIVE), pl.ds(f * CHUNK, CHUNK)], wide_ref.at[f], sems.at[f]
+        )
+        for f in range(MEMBERS)
+    ]
+    for copy in copies:
+        copy.start()
+    for copy in copies:
+        copy.wait()
 
 
 def pack(section_input):
     return pl.pallas_call(
         pack_kernel,
-        grid=(MEMBERS,),
         out_shape=jax.ShapeDtypeStruct((MEMBERS, LIVE, CHUNK), BF16),
-        in_specs=[pl.BlockSpec((LIVE, CHUNK), lambda f: (0, f))],
-        out_specs=pl.BlockSpec((1, LIVE, CHUNK), lambda f: (f, 0, 0)),
+        in_specs=[pl.BlockSpec(memory_space=pl.ANY)],
+        out_specs=pl.BlockSpec(memory_space=pltpu.VMEM),
+        scratch_shapes=[pltpu.SemaphoreType.DMA((MEMBERS,))],
         compiler_params=params(),
         cost_estimate=pl.CostEstimate(flops=0, bytes_accessed=4 * LIVE * D, transcendentals=0),
         name="pack",
@@ -113,10 +122,13 @@
 
 
 def live_count(kept_ref, sends_ref):
-    own = lax.broadcasted_iota(jnp.int32, (32, 32), 0) == coordinates()["dp"]
-    sent = jnp.sum(jnp.where(own, sends_ref[...].astype(F32), 0.0), axis=1, keepdims=True)
-    held = jnp.where(own[:, :1], kept_ref[...].astype(F32), 0.0)
-    return jnp.sum(sent + held, axis=0, keepdims=True)
+    dp = coordinates()["dp"]
+    row, column = (lax.broadcasted_iota(jnp.int32, (32, 32), k) for k in range(2))
+    counts = jnp.where(row == dp, sends_ref[...], 0) + jnp.where(
+        (row == 0) & (column == dp), kept_ref[...], 0
+    )
+    counts = jnp.sum(counts.astype(F32), axis=0, keepdims=True)
+    return jnp.sum(counts, axis=1, keepdims=True)
 
 
 def places(shape):
@@ -124,10 +136,9 @@
     return rows
 
 
-def head_tables(q, rate_ref, step_ref, rate_scr):
-    rate_scr[...] = jnp.transpose(jnp.broadcast_to(rate_ref[...], (HEADS, HEADS)))
+def head_tables(rate_ref, step_ref):
     steps = step_ref[...]
-    totals = steps * rate_scr[pl.ds(pl.multiple_of(q * HPG, HPG), HPG), :]
+    totals = steps * jnp.transpose(jnp.broadcast_to(rate_ref[...], (HEADS, HEADS)))
     lane = lax.broadcasted_iota(jnp.int32, totals.shape, 1)
     reach = 1
     while reach < ROWS:
@@ -137,37 +148,48 @@
     return totals, totals + jnp.log(steps) * LOG2E
 
 
-def turned(table):
-    filler = jnp.zeros((ROWS - HPG, ROWS), F32)
-    return jnp.transpose(jnp.concatenate([table, filler], axis=0))
-
-
-def doc_tables(doc_ref):
+def keep_tables(along_ref, down_ref, along, down):
+    along_ref[...] = along
+    down = jnp.transpose(down)
+    for q in range(GROUPS):
+        down_ref[q] = pltpu.roll(down, HEADS - q * HPG, 1) if q else down
+
+
+def row_mask(live, doc_ref, target, source):
     along = jnp.broadcast_to(doc_ref[...].astype(F32), (ROWS, ROWS))
-    return along, jnp.transpose(along)
+    down = jnp.transpose(along)
+    keep = (along[:LIVE] == down[:LIVE]) & (source <= target) & (target < live) & (source < live)
+    return jnp.where(keep, 0.0, -1e30).astype(F32)
+
+
+def group_rows(q):
+    return pl.ds(pl.multiple_of(q * HPG, HPG), HPG)
 
 
 def c_grad_kernel(
-    kept_ref, sends_ref, rate_ref, doc_ref, step_ref, g_ref, x_ref, b_ref, out_ref, rate_scr
+    kept_ref, sends_ref, rate_ref, doc_ref, step_ref, g_ref, x_ref, b_ref, out_ref, source_scr, totals_scr, bias_scr
 ):
     q = pl.program_id(0)
-    live = live_count(kept_ref, sends_ref)
-    totals, source = head_tables(q, rate_ref, step_ref, rate_scr)
-    totals_col = turned(totals)
-    along, down = doc_tables(doc_ref)
-    t, s = places((LIVE, ROWS))
-    keep = (along[:LIVE] == down[:LIVE]) & (s <= t) & (t < live) & (s < live)
-    bias = jnp.where(keep, 0.0, -1e30).astype(F32)
-    half = lax.broadcasted_iota(jnp.int32, (ROWS, 128), 1) < HDIM
+
+    @pl.when(q == 0)
+    def _():
+        totals, source = head_tables(rate_ref, step_ref)
+        keep_tables(source_scr, totals_scr, source, totals)
+        t, s = places((LIVE, ROWS))
+        bias_scr[...] = row_mask(live_count(kept_ref, sends_ref), doc_ref, t, s)
+
+    bias = bias_scr[...]
+    source = source_scr[group_rows(q), :]
+    totals_col = totals_scr[q]
+    upper = lax.broadcasted_iota(jnp.int32, (128, ROWS), 0) < HDIM
     mixing = jnp.zeros((LIVE, ROWS), F32)
     for p in range(HPG // 2):
         lanes = slice(p * 128, p * 128 + 128)
         x_pair = x_ref[:, lanes]
         zero = jnp.zeros_like(x_pair)
-        both = jnp.concatenate([jnp.where(half, x_pair, zero), jnp.where(half, zero, x_pair)], axis=0)
-        inner = lax.dot_general(
-            g_ref[:, lanes], both, (((1,), (1,)), ((), ())), preferred_element_type=F32
-        )
+        x_turned = jnp.transpose(x_pair)
+        both = jnp.concatenate([jnp.where(upper, x_turned, zero), jnp.where(upper, zero, x_turned)], axis=1)
+        inner = jnp.dot(g_ref[:, lanes], both, preferred_element_type=F32)
         for k in range(2):
             h = 2 * p + k
             gap = (source[h : h + 1, :] - totals_col[:LIVE, h : h + 1]) + bias
@@ -191,17 +213,21 @@
         grid=(GROUPS,),
         out_shape=jax.ShapeDtypeStruct((LIVE, NARROW), BF16),
         in_specs=[
-            pl.BlockSpec((32, 1), lambda q: (0, 0)),
+            pl.BlockSpec((1, 32), lambda q: (0, 0)),
             pl.BlockSpec((32, 32), lambda q: (0, 0)),
             row_spec(),
             row_spec(),
-            pl.BlockSpec((HPG, ROWS), lambda q: (q, 0)),
+            pl.BlockSpec((HEADS, ROWS), lambda q: (0, 0)),
             pl.BlockSpec((LIVE, wide), lambda q: (0, q)),
             pl.BlockSpec((ROWS, wide), lambda q: (0, q)),
             pl.BlockSpec((ROWS, STATE), lambda q: (0, q)),
         ],
         out_specs=pl.BlockSpec((LIVE, STATE), lambda q: (0, q)),
-        scratch_shapes=[pltpu.VMEM((HEADS, HEADS), F32)],
+        scratch_shapes=[
+            pltpu.VMEM((HEADS, ROWS), F32),
+            pltpu.VMEM((GROUPS, ROWS, HEADS), F32),
+            pltpu.VMEM((LIVE, ROWS), F32),
+        ],
         compiler_params=params(),
         cost_estimate=pl.CostEstimate(
             flops=4 * LIVE * ROWS * D, bytes_accessed=4 * ROWS * D, transcendentals=HEADS * LIVE * ROWS
@@ -214,14 +240,27 @@
     kept_ref, sends_ref, skip_ref, rate_ref, doc_ref, step_ref, g_ref, b_ref, *refs
 ):
     q = pl.program_id(0)
-    proj_refs, (out_ref, rate_scr) = refs[:MEMBERS], refs[MEMBERS:]
-    live = live_count(kept_ref, sends_ref)
-    totals, source = head_tables(q, rate_ref, step_ref, rate_scr)
-    source_col = turned(source)
-    along, down = doc_tables(doc_ref)
-    s, t = places((LIVE, ROWS))
-    keep = (along[:LIVE] == down[:LIVE]) & (s <= t) & (t < live) & (s < live)
-    bias = jnp.where(keep, 0.0, -1e30).astype(F32)
+    proj_refs, both_refs, refs = refs[:MEMBERS], refs[MEMBERS : 2 * MEMBERS], refs[2 * MEMBERS :]
+    out_ref, back_ref, totals_scr, source_scr, bias_scr, live_scr, sems = refs
+    copies = [
+        pltpu.make_async_copy(ref.at[:, pl.ds(NARROW, CHUNK)], back_ref.at[f], sems.at[i])
+        for i, (ref, f) in enumerate(zip(both_refs, rows_at(-1)))
+    ]
+
+    @pl.when(q == 0)
+    def _():
+        for copy in copies:
+            copy.start()
+        totals, source = head_tables(rate_ref, step_ref)
+        keep_tables(totals_scr, source_scr, totals, source)
+        s, t = places((LIVE, ROWS))
+        live = live_count(kept_ref, sends_ref)
+        bias_scr[...] = row_mask(live, doc_ref, t, s)
+        live_scr[...] = jnp.where(s < live, 1.0, 0.0)
+
+    bias = bias_scr[...]
+    totals = totals_scr[group_rows(q), :]
+    source_col = source_scr[q]
     half = lax.broadcasted_iota(jnp.int32, (ROWS, 128), 1) < HDIM
     c_proj = proj_refs[0][...].astype(F32)
     for proj_ref in proj_refs[1:]:
@@ -230,7 +269,7 @@
     affinity = lax.dot_general(
         b_ref[:LIVE, :], c_proj, (((1,), (1,)), ((), ())), preferred_element_type=F32
     )
-    alive = s < live
+    alive = live_scr[...]
     for p in range(HPG // 2):
         lanes = slice(p * 128, p * 128 + 128)
         g_pair = g_ref[:, lanes]
@@ -243,10 +282,15 @@
             kernels.append((jnp.exp2(gap) * affinity).astype(BF16))
         grads = jnp.dot(jnp.concatenate(kernels, axis=1), both, preferred_element_type=F32)
         first = q * HPG + 2 * p
-        gain = jnp.where(half[:LIVE], skip_ref[first], skip_ref[first + 1])
-        grads = grads + jnp.where(alive, gain * g_pair[:LIVE].astype(F32), 0.0)
+        gain = jnp.where(half[:LIVE], skip_ref[first], skip_ref[first + 1]) * alive
+        grads = grads + gain * g_pair[:LIVE].astype(F32)
         out_ref[:LIVE, lanes] = grads.astype(BF16)
     out_ref[LIVE:, :] = jnp.zeros((ROWS - LIVE, HPG * HDIM), BF16)
+
+    @pl.when(q == GROUPS - 1)
+    def _():
+        for copy in copies:
+            copy.wait()
 
 
 def scan_grad_call(kept, sends, skip, rate, docs, steps, out_grad, b_factors, shares):
@@ -254,37 +298,45 @@
     return pl.pallas_call(
         scan_grad_kernel,
         grid=(GROUPS,),
-        out_shape=jax.ShapeDtypeStruct((ROWS, D), BF16),
+        out_shape=[
+            jax.ShapeDtypeStruct((ROWS, D), BF16),
+            jax.ShapeDtypeStruct((MEMBERS, LIVE, CHUNK), BF16),
+        ],
         in_specs=[
-            pl.BlockSpec((32, 1), lambda q: (0, 0)),
+            pl.BlockSpec((1, 32), lambda q: (0, 0)),
             pl.BlockSpec((32, 32), lambda q: (0, 0)),
             smem(),
             row_spec(),
             row_spec(),
-            pl.BlockSpec((HPG, ROWS), lambda q: (q, 0)),
+            pl.BlockSpec((HEADS, ROWS), lambda q: (0, 0)),
             pl.BlockSpec((ROWS, wide), lambda q: (0, q)),
             pl.BlockSpec((ROWS, STATE), lambda q: (0, q)),
         ]
-        + [pl.BlockSpec((LIVE, STATE), lambda q: (0, q))] * MEMBERS,
-        out_specs=pl.BlockSpec((ROWS, wide), lambda q: (0, q)),
-        scratch_shapes=[pltpu.VMEM((HEADS, HEADS), F32)],
+        + [pl.BlockSpec((LIVE, STATE), lambda q: (0, q))] * MEMBERS
+        + [pl.BlockSpec(memory_space=pl.ANY)] * MEMBERS,
+        out_specs=[
+            pl.BlockSpec((ROWS, wide), lambda q: (0, q)),
+            pl.BlockSpec((MEMBERS, LIVE, CHUNK), lambda q: (0, 0, 0)),
+        ],
+        scratch_shapes=[
+            pltpu.VMEM((HEADS, ROWS), F32),
+            pltpu.VMEM((GROUPS, ROWS, HEADS), F32),
+            pltpu.VMEM((LIVE, ROWS), F32),
+            pltpu.VMEM((LIVE, ROWS), F32),
+            pltpu.SemaphoreType.DMA((MEMBERS,)),
+        ],
         compiler_params=params(),
         cost_estimate=pl.CostEstimate(
             flops=4 * LIVE * ROWS * D, bytes_accessed=4 * ROWS * D, transcendentals=HEADS * LIVE * ROWS
         ),
         name="scan_grad",
-    )(kept, sends, skip, rate, docs, steps, out_grad, b_factors, *shares)
-
-
-def gather_grads(c_refs, grads):
-    for c_ref, pair in zip(c_refs, sources()):
-        for p in range(2):
-            grads[pair[p]] = c_ref[p]
+    )(kept, sends, skip, rate, docs, steps, out_grad, b_factors, *shares, *shares)
 
 
 def weight_kernel(s_ref, *refs):
-    c_refs, (keep_ref, send_ref, grads) = refs[:4], refs[4:]
-    gather_grads(c_refs, grads)
+    c_refs, (keep_ref, send_ref, grads) = refs[:MEMBERS], refs[MEMBERS:]
+    for c_ref, f in zip(c_refs, rows_at(-1)):
+        grads[f] = c_ref[...]
     first_core = coordinates()["core"] == 0
     wide = 256
     rows = MEMBERS * LIVE
@@ -303,18 +355,18 @@
 
         @pl.when(first_core != (i % 2 == 0))
         def _():
-            send_ref[place] = part
+            send_ref[place] = part.astype(BF16)
 
 
 def weight_call(pieces, grads):
     vmem = pl.BlockSpec(memory_space=pltpu.VMEM)
     return pl.pallas_call(
         weight_kernel,
-        out_shape=[jax.ShapeDtypeStruct((16, 32, NARROW), F32)] * 2,
-        in_specs=[vmem] * 5,
-        out_specs=[vmem, vmem],
-        scratch_shapes=[pltpu.VMEM((MEMBERS, LIVE, NARROW), BF16)],
-        compiler_params=params(),
+        out_shape=[jax.ShapeDtypeStruct((16, 32, NARROW), kind) for kind in (F32, BF16)]
+        + [jax.ShapeDtypeStruct((MEMBERS, LIVE, NARROW), BF16)],
+        in_specs=[vmem] * 9,
+        out_specs=[vmem] * 3,
+        compiler_params=params(24 * 2**20),
         cost_estimate=pl.CostEstimate(
             flops=2 * MEMBERS * LIVE * CHUNK * NARROW, bytes_accessed=5 * 2**20, transcendentals=0
         ),
@@ -322,10 +374,8 @@
     )(pieces, *grads)
 
 
-def project_kernel(w_ref, s_ref, *refs):
-    c_refs, refs = refs[:4], refs[4:]
-    out_refs, (top_ref, grads, held) = refs[:MEMBERS], refs[MEMBERS:]
-    gather_grads(c_refs, grads)
+def project_kernel(w_ref, s_ref, grads, *refs):
+    out_refs, (top_ref, held) = refs[:MEMBERS], refs[MEMBERS:]
     rows = MEMBERS * LIVE
     wide = 256
     proj = jnp.dot(s_ref[...].reshape(rows, CHUNK), w_ref[...], preferred_element_type=F32)
@@ -353,18 +403,17 @@
         project_kernel,
         out_shape=[jax.ShapeDtypeStruct((LIVE, BOTH), BF16)] * MEMBERS
         + [jax.ShapeDtypeStruct((1, 128), F32)],
-        in_specs=[vmem] * 6,
+        in_specs=[vmem] * 3,
         out_specs=[vmem] * 9,
         scratch_shapes=[
-            pltpu.VMEM((MEMBERS, LIVE, NARROW), BF16),
             pltpu.VMEM((MEMBERS, LIVE, BOTH), BF16),
         ],
-        compiler_params=params(),
+        compiler_params=params(24 * 2**20),
         cost_estimate=pl.CostEstimate(
             flops=4 * MEMBERS * LIVE * CHUNK * NARROW, bytes_accessed=6 * 2**20, transcendentals=0
         ),
         name="project",
-    )(weights, pieces, *grads)
+    )(weights, pieces, grads)
     return out[:MEMBERS], out[MEMBERS]
 
 
@@ -388,22 +437,21 @@
         ],
         in_specs=[vmem, vmem],
         out_specs=[vmem, vmem],
-        compiler_params=params(),
+        compiler_params=params(16 * 2**20),
         cost_estimate=pl.CostEstimate(flops=16 * 32 * NARROW, bytes_accessed=2**20, transcendentals=0),
         name="peaks",
     )(parts, top)
 
 
-def finish_kernel(tops_ref, sum_ref, *refs):
-    back_refs, (input_ref, weight_ref, held, sems) = refs[:MEMBERS], refs[MEMBERS:]
+def finish_kernel(tops_ref, sum_ref, back_ref, input_ref, weight_ref, held, sems):
     tops = jnp.max(tops_ref[...], axis=0)
     scale = 1.0 / (tops[:, :1] + peak_eps)
+    held[:, LIVE:, :] = jnp.zeros((MEMBERS, ROWS - LIVE, CHUNK), BF16)
     copies = []
-    for i, (ref, f) in enumerate(zip(back_refs, rows_at(-1))):
-        held[i, :LIVE] = (ref[:, NARROW:].astype(F32) * scale).astype(BF16)
-        held[i, LIVE:] = jnp.zeros((ROWS - LIVE, CHUNK), BF16)
-        columns = pl.ds(pl.multiple_of(f * CHUNK, CHUNK), CHUNK)
-        copies.append(pltpu.make_async_copy(held.at[i], input_ref.at[:, columns], sems.at[i]))
+    for f in range(MEMBERS):
+        held[f, :LIVE] = (back_ref[f].astype(F32) * scale).astype(BF16)
+        columns = pl.ds(f * CHUNK, CHUNK)
+        copies.append(pltpu.make_async_copy(held.at[f], input_ref.at[:, columns], sems.at[f]))
         copies[-1].start()
     weight_ref[...] = sum_ref[...] / (tops[:, 64:65] + peak_eps)
     for copy in copies:
@@ -418,16 +466,16 @@
             jax.ShapeDtypeStruct((ROWS, D), BF16),
             jax.ShapeDtypeStruct((32, NARROW), F32),
         ],
-        in_specs=[vmem] * 10,
+        in_specs=[vmem] * 3,
         out_specs=[pl.BlockSpec(memory_space=pl.ANY), vmem],
         scratch_shapes=[
             pltpu.VMEM((MEMBERS, ROWS, CHUNK), BF16),
             pltpu.SemaphoreType.DMA((MEMBERS,)),
         ],
-        compiler_params=params(),
+        compiler_params=params(16 * 2**20),
         cost_estimate=pl.CostEstimate(flops=LIVE * D, bytes_accessed=4 * ROWS * D, transcendentals=0),
         name="finish",
-    )(tops, weight_sum, *back)
+    )(tops, weight_sum, back)
 
 
 def shards(
@@ -443,17 +491,17 @@
     kept_rows,
     send_counts,
 ):
-    kept = kept_rows.reshape(32, 1)
+    kept = kept_rows.reshape(1, 32)
     sends = send_counts.reshape(32, 32)
     rate, docs = decay_rate.reshape(1, HEADS), doc_index.reshape(1, ROWS)
 
     pieces = exchange(pack(section_input), WIDE)
 
     c_own = c_grad_call(kept, sends, rate, docs, step_size, out_grad, scan_input, b_factors)
-    grads = along_x(jnp.stack([c_own, to_pair(c_own)]))
-
-    keep, send = weight_call(pieces, grads)
-    parts = (keep + to_core(send)).astype(BF16)
+    grads = [c_own] + [lax.ppermute(c_own, ALL, moved(*step)) for step in STEPS[1:]]
+
+    keep, send, grads = weight_call(pieces, grads)
+    parts = (keep + to_core(send).astype(F32)).astype(BF16)
     parts = lax.all_to_all(parts, "dp", 0, 0, axis_index_groups=SAME_CORE)
 
     both, top = project_call(c_weight, pieces, grads)
@@ -461,10 +509,10 @@
     weight_sum, tops = peak_call(parts, top)
     tops = exchange(tops, None)
     weight_sum = lax.ppermute(weight_sum, ALL, HOME)
-    scan_grad = scan_grad_call(
+    scan_grad, back = scan_grad_call(
         kept, sends, skip_gain, rate, docs, step_size, out_grad, b_factors, both
     )
-    input_grad, readout_weight_gradient = finish_call(tops, both, weight_sum)
+    input_grad, readout_weight_gradient = finish_call(tops, back, weight_sum)
     return (input_grad, scan_grad, readout_weight_gradient)
 
 

time: 128 us -> 115 us (0.90)
  the two profiles are of different devices: /device:TPU:5 before, /device:TPU:94 now
where the time goes in v3:
time: 115 us; the launch traced here: 114 us
  starting transfers between devices  63.5 us (55%)
  Pallas kernels  24.2 us (21%)
  waiting for transfers between devices  18.8 us (16%)
  local copies, waits for them, and re-layouts  5.71 us (5%)
    all_to_all x2, starting transfers between devices, exchange(): return lax.all_to_all(value, ALL, 0, 0, axis_index_groups=groups)  20.7 us
    ppermute x7, starting transfers between devices, shards(): lax.ppermute(c_own, ALL, moved(*step))  14.6 us
    ppermute x7, starting transfers between devices, shards(): lax.ppermute(value, ALL, moved(*step))  12.2 us
    ppermute x7, waiting for transfers between devices, shards(): lax.ppermute(c_own, ALL, moved(*step))  9.99 us
    all_to_all x1, starting transfers between devices, shards(): parts = lax.all_to_all(parts, 'dp', 0, 0, axis_index_groups=SAME_CORE)  9.04 us
    pallas_call x1, Pallas kernels, scan_grad_call(): pl.pallas_call(scan_grad_kernel, grid=(GROUPS,), out_shape=[jax.ShapeDtyp...  7.36 us
    ppermute x1, starting transfers between devices, shards(): weight_sum = lax.ppermute(weight_sum, ALL, HOME)  6.97 us
    ppermute x7, waiting for transfers between devices, shards(): lax.ppermute(value, ALL, moved(*step))  6.9 us
  transfers between devices with their start and end apart: 19, of which 6 were waited for; matrix products, arithmetic and copies ran while one was open for 0% of the time, Pallas kernels for 15%

profile of v3, /device:TPU:94, one launch (start us, length us, event | category | flops | bytes accessed | tf_op | source)
XLA Modules:
  0.0 114.2 jit_solution(13363876616593445087)
XLA Ops:
  0.6 2.7 %pack.1 = bf16[8,96,1024]{2,1,0:T(8,128)(2,1)} custom-call(bf16[128,8192]{1,0:T(8,128)(2,1)} %s_ref.1), custom_call_target="tpu_custom_call" | custom-call | bytes 3145728 | tf_op jit(solution)/shard_map/pack/pallas_call | solution.py:112
  3.3 6.9 %all-to-all-start = ((bf16[8,96,1024]{2,1,0:T(8,128)(2,1)}), bf16[8,96,1024]{2,1,0:T(8,128)(2,1)S(1)}, u32[]{:S(2)}, u32[]{:S(2)}) async-start(bf16[8,96,1024]{2,1,0:T(8,128)(2,1)} %pack.1), calls=%async_computation | async-start | bytes 3145728 | tf_op jit(solution)/shard_map/all_to_all | solution.py:64
  10.2 6.4 %c_grad.1.refs_0_ = bf16[96,512]{1,0:T(8,128)(2,1)} custom-call(s32[1,32]{1,0:T(1,128)} %bitcast.6, s32[32,32]{1,0:T(8,128)} %bitcast.4, f32[1,128]{1,0:T(1,128)} %bitcast.8, s32[1,128]{1,0:T(1,128)} %bitcast.10, f32[128,128]{1,0:T(8,128)} %step_ref.3, bf16[128,8192]{1,0:T(8,128)(2,1)} %g_ref.3, bf16[128,8192]{1,0:T(8,128)(2,1)} %x_ref.1, bf16[128,512]{1,0:T(8,128)(2,1)} %b_ref.3), custom_call_target="tpu_custom_call" | custom-call | flops 402653184 | bytes 4194304 | tf_op jit(solution)/shard_map/c_grad/pallas_call | solution.py:211
  16.6 1.5 %collective-permute-start.6 = (bf16[96,512]{1,0:T(8,128)(2,1)}, bf16[96,512]{1,0:T(8,128)(2,1)S(1)}, u32[]{:S(2)}, u32[]{:S(2)}) collective-permute-start(bf16[96,512]{1,0:T(8,128)(2,1)} %c_grad.1.refs_0_), channel_id=1, source_target_pairs={{0,134},{8,142},{16,150},{24,158},{32,166},{40,174},{48,182},{56,1... | collective-permute-start | bytes 294920 | tf_op jit(solution)/shard_map/ppermute | solution.py:501
  18.1 2.1 %collective-permute-start.5 = (bf16[96,512]{1,0:T(8,128)(2,1)}, bf16[96,512]{1,0:T(8,128)(2,1)S(1)}, u32[]{:S(2)}, u32[]{:S(2)}) collective-permute-start(bf16[96,512]{1,0:T(8,128)(2,1)} %c_grad.1.refs_0_), channel_id=1, source_target_pairs={{0,2},{8,10},{16,18},{24,26},{32,34},{40,42},{48,50},{56,58},{64,6... | collective-permute-start | bytes 294920 | tf_op jit(solution)/shard_map/ppermute | solution.py:501
  20.2 3.0 %collective-permute-start.4 = (bf16[96,512]{1,0:T(8,128)(2,1)}, bf16[96,512]{1,0:T(8,128)(2,1)S(1)}, u32[]{:S(2)}, u32[]{:S(2)}) collective-permute-start(bf16[96,512]{1,0:T(8,128)(2,1)} %c_grad.1.refs_0_), channel_id=1, source_target_pairs={{0,135},{8,143},{16,151},{24,159},{32,167},{40,175},{48,183},{56,1... | collective-permute-start | bytes 294920 | tf_op jit(solution)/shard_map/ppermute | solution.py:501
  23.7 2.7 %collective-permute-start.2 = (bf16[96,512]{1,0:T(8,128)(2,1)}, bf16[96,512]{1,0:T(8,128)(2,1)S(1)}, u32[]{:S(2)}, u32[]{:S(2)}) collective-permute-start(bf16[96,512]{1,0:T(8,128)(2,1)} %c_grad.1.refs_0_), channel_id=1, source_target_pairs={{0,133},{8,141},{16,149},{24,157},{32,165},{40,173},{48,181},{56,1... | collective-permute-start | bytes 294920 | tf_op jit(solution)/shard_map/ppermute | solution.py:501
  26.4 6.6 %collective-permute-done.6.refs_7_ = bf16[96,512]{1,0:T(8,128)(2,1)S(1)} collective-permute-done((bf16[96,512]{1,0:T(8,128)(2,1)}, bf16[96,512]{1,0:T(8,128)(2,1)S(1)}, u32[]{:S(2)}, u32[]{:S(2)}) %collective-permute-start.6) | collective-permute-done | bytes 98336 | tf_op jit(solution)/shard_map/ppermute | solution.py:501
  33.0 2.2 %collective-permute-start.1 = (bf16[96,512]{1,0:T(8,128)(2,1)}, bf16[96,512]{1,0:T(8,128)(2,1)S(1)}, u32[]{:S(2)}, u32[]{:S(2)}) collective-permute-start(bf16[96,512]{1,0:T(8,128)(2,1)} %c_grad.1.refs_0_), channel_id=1, source_target_pairs={{0,1},{8,9},{16,17},{24,25},{32,33},{40,41},{48,49},{56,57},{64,65... | collective-permute-start | bytes 294920 | tf_op jit(solution)/shard_map/ppermute | solution.py:501
  35.2 2.7 %collective-permute-start = (bf16[96,512]{1,0:T(8,128)(2,1)}, bf16[96,512]{1,0:T(8,128)(2,1)S(1)}, u32[]{:S(2)}, u32[]{:S(2)}) collective-permute-start(bf16[96,512]{1,0:T(8,128)(2,1)} %c_grad.1.refs_0_), channel_id=1, source_target_pairs={{0,132},{8,140},{16,148},{24,156},{32,164},{40,172},{48,180},{56,1... | collective-permute-start | bytes 294920 | tf_op jit(solution)/shard_map/ppermute | solution.py:501
  37.9 3.3 %collective-permute-done.refs_1_ = bf16[96,512]{1,0:T(8,128)(2,1)S(1)} collective-permute-done((bf16[96,512]{1,0:T(8,128)(2,1)}, bf16[96,512]{1,0:T(8,128)(2,1)S(1)}, u32[]{:S(2)}, u32[]{:S(2)}) %collective-permute-start) | collective-permute-done | bytes 98336 | tf_op jit(solution)/shard_map/ppermute | solution.py:501
  41.2 0.9 copy-done.2
  42.1 1.8 %weight_part.1 = (f32[16,32,512]{2,1,0:T(8,128)S(1)}, bf16[16,32,512]{2,1,0:T(8,128)(2,1)S(1)}, bf16[8,96,512]{2,1,0:T(8,128)(2,1)S(1)}) custom-call(bf16[8,96,1024]{2,1,0:T(8,128)(2,1)S(1)} %all-to-all-done.s_ref, bf16[96,512]{1,0:T(8,128)(2,1)S(1)} %copy-done.2, bf16[96,512]{1,0:T(8,128)(2,1)S(1)} %collective-permute-done.refs_1_, ...), custom_call_target="tpu_custom_call" | custom-call | flops 805306368 | bytes 5242880 | tf_op jit(solution)/shard_map/weight_part/pallas_call | solution.py:363
  44.8 1.9 %collective-permute-done.7 = bf16[16,32,512]{2,1,0:T(8,128)(2,1)S(1)} collective-permute-done((bf16[16,32,512]{2,1,0:T(8,128)(2,1)S(1)}, bf16[16,32,512]{2,1,0:T(8,128)(2,1)S(1)}, u32[]{:S(2)}, u32[]{:S(2)}) %collective-permute-start.7) | collective-permute-done | bytes 524320 | tf_op jit(solution)/shard_map/ppermute | solution.py:76
  46.7 1.0 add_convert_fusion
  47.6 9.0 %all-to-all-start.1 = ((bf16[16,32,512]{2,1,0:T(8,128)(2,1)}), bf16[16,32,512]{2,1,0:T(8,128)(2,1)S(1)}, u32[]{:S(2)}, u32[]{:S(2)}) async-start(bf16[16,32,512]{2,1,0:T(8,128)(2,1)} %add_convert_fusion), calls=%async_computation.1 | async-start | bytes 1048576 | tf_op jit(solution)/shard_map/all_to_all | solution.py:505
  56.7 1.1 copy-done.5
  57.8 2.9 %project.1 = (bf16[96,1536]{1,0:T(8,128)(2,1)S(1)}, bf16[96,1536]{1,0:T(8,128)(2,1)S(1)}, bf16[96,1536]{1,0:T(8,128)(2,1)S(1)}, bf16[96,1536]{1,0:T(8,128)(2,1)}...) custom-call(bf16[1024,512]{1,0:T(8,128)(2,1)S(1)} %copy-done.3, ...), custom_call_target="tpu_custom_call" | custom-call | flops 1610612736 | bytes 6291456 | tf_op jit(solution)/shard_map/project/pallas_call | solution.py:402
  61.4 1.8 %collective-permute-start.9 = (bf16[96,1536]{1,0:T(8,128)(2,1)S(1)}, bf16[96,1536]{1,0:T(8,128)(2,1)S(1)}, u32[]{:S(2)}, u32[]{:S(2)}) collective-permute-start(bf16[96,1536]{1,0:T(8,128)(2,1)S(1)} %get-tuple-element.28), channel_id=1, source_target_pairs={{0,132},{8,140},{16,148},{24,156},{32,164},{40,172},{48,180},{56,1... | collective-permute-start | bytes 884744 | tf_op jit(solution)/shard_map/ppermute | solution.py:508
  63.5 2.6 %collective-permute-start.11 = (bf16[96,1536]{1,0:T(8,128)(2,1)}, bf16[96,1536]{1,0:T(8,128)(2,1)S(1)}, u32[]{:S(2)}, u32[]{:S(2)}) collective-permute-start(bf16[96,1536]{1,0:T(8,128)(2,1)} %get-tuple-element.30), channel_id=1, source_target_pairs={{0,133},{8,141},{16,149},{24,157},{32,165},{40,173},{48,181},{56,1... | collective-permute-start | bytes 884744 | tf_op jit(solution)/shard_map/ppermute | solution.py:508
  66.1 2.0 %collective-permute-start.12 = (bf16[96,1536]{1,0:T(8,128)(2,1)}, bf16[96,1536]{1,0:T(8,128)(2,1)S(1)}, u32[]{:S(2)}, u32[]{:S(2)}) collective-permute-start(bf16[96,1536]{1,0:T(8,128)(2,1)} %get-tuple-element.31), channel_id=1, source_target_pairs={{0,3},{8,11},{16,19},{24,27},{32,35},{40,43},{48,51},{56,59},{64,6... | collective-permute-start | bytes 884744 | tf_op jit(solution)/shard_map/ppermute | solution.py:508
  68.1 1.2 %collective-permute-start.13 = (bf16[96,1536]{1,0:T(8,128)(2,1)}, bf16[96,1536]{1,0:T(8,128)(2,1)S(1)}, u32[]{:S(2)}, u32[]{:S(2)}) collective-permute-start(bf16[96,1536]{1,0:T(8,128)(2,1)} %get-tuple-element.32), channel_id=1, source_target_pairs={{0,135},{8,143},{16,151},{24,159},{32,167},{40,175},{48,183},{56,1... | collective-permute-start | bytes 884744 | tf_op jit(solution)/shard_map/ppermute | solution.py:508
  69.4 2.3 %collective-permute-done.9.refs_1_.refs_9_ = bf16[96,1536]{1,0:T(8,128)(2,1)S(1)} collective-permute-done((bf16[96,1536]{1,0:T(8,128)(2,1)S(1)}, bf16[96,1536]{1,0:T(8,128)(2,1)S(1)}, u32[]{:S(2)}, u32[]{:S(2)}) %collective-permute-start.9) | collective-permute-done | bytes 294944 | tf_op jit(solution)/shard_map/ppermute | solution.py:508
  71.7 0.9 collective-permute-start.14
  73.1 3.3 %collective-permute-start.15 = (bf16[96,1536]{1,0:T(8,128)(2,1)S(1)}, bf16[96,1536]{1,0:T(8,128)(2,1)S(1)}, u32[]{:S(2)}, u32[]{:S(2)}) collective-permute-start(bf16[96,1536]{1,0:T(8,128)(2,1)S(1)} %get-tuple-element.34), channel_id=1, source_target_pairs={{0,134},{8,142},{16,150},{24,158},{32,166},{40,174},{48,182},{56,1... | collective-permute-start | bytes 884744 | tf_op jit(solution)/shard_map/ppermute | solution.py:508
  76.4 0.9 peaks.1
  77.3 13.8 %all-to-all-start.2 = ((f32[256,1,128]{2,1,0:T(1,128)}), f32[256,1,128]{2,1,0:T(1,128)S(1)}, u32[]{:S(2)}, u32[]{:S(2)}) async-start(f32[256,1,128]{2,1,0:T(1,128)} %get-tuple-element.25), calls=%async_computation.2 | async-start | bytes 262144 | tf_op jit(solution)/shard_map/all_to_all | solution.py:64
  91.2 7.0 %collective-permute-start.8 = (f32[32,512]{1,0:T(8,128)S(1)}, f32[32,512]{1,0:T(8,128)S(1)}, u32[]{:S(2)}, u32[]{:S(2)}) collective-permute-start(f32[32,512]{1,0:T(8,128)S(1)} %get-tuple-element.26), channel_id=1, source_target_pairs={{0,0},{8,8},{16,1},{24,9},{32,2},{40,10},{48,3},{56,11},{64,4},{72... | collective-permute-start | bytes 196616 | tf_op jit(solution)/shard_map/ppermute | solution.py:511
  98.2 4.1 %collective-permute-done.15.refs_7_.refs_15_ = bf16[96,1536]{1,0:T(8,128)(2,1)S(1)} collective-permute-done((bf16[96,1536]{1,0:T(8,128)(2,1)S(1)}, bf16[96,1536]{1,0:T(8,128)(2,1)S(1)}, u32[]{:S(2)}, u32[]{:S(2)}) %collective-permute-start.15) | collective-permute-done | bytes 294944 | tf_op jit(solution)/shard_map/ppermute | solution.py:508
  103.0 7.4 %scan_grad.1 = (bf16[128,8192]{1,0:T(8,128)(2,1)}, bf16[8,96,1024]{2,1,0:T(8,128)(2,1)}) custom-call(s32[1,32]{1,0:T(1,128)} %bitcast.7, s32[32,32]{1,0:T(8,128)} %bitcast.5, f32[128]{0:T(128)} %skip_ref.1, f32[1,128]{1,0:T(1,128)} %bitcast.9, s32[1,128]{1,0:T(1,128)} %bitcast.11, f32[128,128]{1,0:T(8,128)} %step_ref.3, bf16[128,8192]{1,0:T(8,128)(2,1)} %g_ref.3, ...), custom_call_target="tpu_custom_call" | custom-call | flops 402653184 | bytes 4194304 | tf_op jit(solution)/shard_map/scan_grad/pallas_call | solution.py:298
  110.4 1.4 %copy-done = bf16[8,96,1024]{2,1,0:T(8,128)(2,1)S(1)} copy-done((bf16[8,96,1024]{2,1,0:T(8,128)(2,1)S(1)}, bf16[8,96,1024]{2,1,0:T(8,128)(2,1)}, u32[]{:S(2)}) %copy-start) | copy-done | bytes 1572888
  111.8 2.2 %finish.1 = (bf16[128,8192]{1,0:T(8,128)(2,1)}, f32[32,512]{1,0:T(8,128)}) custom-call(f32[256,1,128]{2,1,0:T(1,128)S(1)} %all-to-all-done.2.tops_ref, f32[32,512]{1,0:T(8,128)S(1)} %collective-permute-done.8.sum_ref, bf16[8,96,1024]{2,1,0:T(8,128)(2,1)S(1)} %copy-done), custom_call_target="tpu_custom_call" | custom-call | flops 786432 | bytes 4194304 | tf_op jit(solution)/shard_map/finish/pallas_call | solution.py:463
  (40 shorter events, 3.7 us)
Async XLA Ops:
  3.3 37.9 %all-to-all-start = ((bf16[8,96,1024]{2,1,0:T(8,128)(2,1)}), bf16[8,96,1024]{2,1,0:T(8,128)(2,1)S(1)}, u32[]{:S(2)}, u32[]{:S(2)}) async-start(bf16[8,96,1024]{2,1,0:T(8,128)(2,1)} %pack.1), calls=%async_computation | async-start | bytes 3145728 | tf_op jit(solution)/shard_map/all_to_all | solution.py:64
  16.6 16.4 %collective-permute-start.6 = (bf16[96,512]{1,0:T(8,128)(2,1)}, bf16[96,512]{1,0:T(8,128)(2,1)S(1)}, u32[]{:S(2)}, u32[]{:S(2)}) collective-permute-start(bf16[96,512]{1,0:T(8,128)(2,1)} %c_grad.1.refs_0_), channel_id=1, source_target_pairs={{0,134},{8,142},{16,150},{24,158},{32,166},{40,174},{48,182},{56,1... | collective-permute-start | bytes 294920 | tf_op jit(solution)/shard_map/ppermute | solution.py:501
  18.1 17.1 %collective-permute-start.5 = (bf16[96,512]{1,0:T(8,128)(2,1)}, bf16[96,512]{1,0:T(8,128)(2,1)S(1)}, u32[]{:S(2)}, u32[]{:S(2)}) collective-permute-start(bf16[96,512]{1,0:T(8,128)(2,1)} %c_grad.1.refs_0_), channel_id=1, source_target_pairs={{0,2},{8,10},{16,18},{24,26},{32,34},{40,42},{48,50},{56,58},{64,6... | collective-permute-start | bytes 294920 | tf_op jit(solution)/shard_map/ppermute | solution.py:501
  20.2 17.7 %collective-permute-start.4 = (bf16[96,512]{1,0:T(8,128)(2,1)}, bf16[96,512]{1,0:T(8,128)(2,1)S(1)}, u32[]{:S(2)}, u32[]{:S(2)}) collective-permute-start(bf16[96,512]{1,0:T(8,128)(2,1)} %c_grad.1.refs_0_), channel_id=1, source_target_pairs={{0,135},{8,143},{16,151},{24,159},{32,167},{40,175},{48,183},{56,1... | collective-permute-start | bytes 294920 | tf_op jit(solution)/shard_map/ppermute | solution.py:501
  23.1 14.7 %collective-permute-start.3 = (bf16[96,512]{1,0:T(8,128)(2,1)}, bf16[96,512]{1,0:T(8,128)(2,1)S(1)}, u32[]{:S(2)}, u32[]{:S(2)}) collective-permute-start(bf16[96,512]{1,0:T(8,128)(2,1)} %c_grad.1.refs_0_), channel_id=1, source_target_pairs={{0,3},{8,11},{16,19},{24,27},{32,35},{40,43},{48,51},{56,59},{64,6... | collective-permute-start | bytes 294920 | tf_op jit(solution)/shard_map/ppermute | solution.py:501
  23.7 14.2 %collective-permute-start.2 = (bf16[96,512]{1,0:T(8,128)(2,1)}, bf16[96,512]{1,0:T(8,128)(2,1)S(1)}, u32[]{:S(2)}, u32[]{:S(2)}) collective-permute-start(bf16[96,512]{1,0:T(8,128)(2,1)} %c_grad.1.refs_0_), channel_id=1, source_target_pairs={{0,133},{8,141},{16,149},{24,157},{32,165},{40,173},{48,181},{56,1... | collective-permute-start | bytes 294920 | tf_op jit(solution)/shard_map/ppermute | solution.py:501
  33.0 4.9 %collective-permute-start.1 = (bf16[96,512]{1,0:T(8,128)(2,1)}, bf16[96,512]{1,0:T(8,128)(2,1)S(1)}, u32[]{:S(2)}, u32[]{:S(2)}) collective-permute-start(bf16[96,512]{1,0:T(8,128)(2,1)} %c_grad.1.refs_0_), channel_id=1, source_target_pairs={{0,1},{8,9},{16,17},{24,25},{32,33},{40,41},{48,49},{56,57},{64,65... | collective-permute-start | bytes 294920 | tf_op jit(solution)/shard_map/ppermute | solution.py:501
  35.2 6.0 %collective-permute-start = (bf16[96,512]{1,0:T(8,128)(2,1)}, bf16[96,512]{1,0:T(8,128)(2,1)S(1)}, u32[]{:S(2)}, u32[]{:S(2)}) collective-permute-start(bf16[96,512]{1,0:T(8,128)(2,1)} %c_grad.1.refs_0_), channel_id=1, source_target_pairs={{0,132},{8,140},{16,148},{24,156},{32,164},{40,172},{48,180},{56,1... | collective-permute-start | bytes 294920 | tf_op jit(solution)/shard_map/ppermute | solution.py:501
  41.2 0.9 copy-start.2
  43.9 0.9 copy-start.4
  44.7 11.9 %copy-start.3 = (bf16[1024,512]{1,0:T(8,128)(2,1)S(1)}, bf16[1024,512]{1,0:T(8,128)(2,1)}, u32[]{:S(2)}) copy-start(bf16[1024,512]{1,0:T(8,128)(2,1)} %w_ref.1) | copy-start | bytes 3145732
  44.8 1.9 %collective-permute-start.7 = (bf16[16,32,512]{2,1,0:T(8,128)(2,1)S(1)}, bf16[16,32,512]{2,1,0:T(8,128)(2,1)S(1)}, u32[]{:S(2)}, u32[]{:S(2)}) collective-permute-start(bf16[16,32,512]{2,1,0:T(8,128)(2,1)S(1)} %get-tuple-element.22), channel_id=1, source_target_pairs={{0,8},{8,0},{16,24},{24,16},{32,40},{40,32},{48,56},{56,48},{64,72... | collective-permute-start | bytes 1572872 | tf_op jit(solution)/shard_map/ppermute | solution.py:76
  47.6 28.8 %all-to-all-start.1 = ((bf16[16,32,512]{2,1,0:T(8,128)(2,1)}), bf16[16,32,512]{2,1,0:T(8,128)(2,1)S(1)}, u32[]{:S(2)}, u32[]{:S(2)}) async-start(bf16[16,32,512]{2,1,0:T(8,128)(2,1)} %add_convert_fusion), calls=%async_computation.1 | async-start | bytes 1048576 | tf_op jit(solution)/shard_map/all_to_all | solution.py:505
  56.7 1.1 copy-start.5
  60.7 0.7 copy-start.1
  61.4 10.3 %collective-permute-start.9 = (bf16[96,1536]{1,0:T(8,128)(2,1)S(1)}, bf16[96,1536]{1,0:T(8,128)(2,1)S(1)}, u32[]{:S(2)}, u32[]{:S(2)}) collective-permute-start(bf16[96,1536]{1,0:T(8,128)(2,1)S(1)} %get-tuple-element.28), channel_id=1, source_target_pairs={{0,132},{8,140},{16,148},{24,156},{32,164},{40,172},{48,180},{56,1... | collective-permute-start | bytes 884744 | tf_op jit(solution)/shard_map/ppermute | solution.py:508
  63.2 9.9 %collective-permute-start.10 = (bf16[96,1536]{1,0:T(8,128)(2,1)S(1)}, bf16[96,1536]{1,0:T(8,128)(2,1)S(1)}, u32[]{:S(2)}, u32[]{:S(2)}) collective-permute-start(bf16[96,1536]{1,0:T(8,128)(2,1)S(1)} %get-tuple-element.29), channel_id=1, source_target_pairs={{0,1},{8,9},{16,17},{24,25},{32,33},{40,41},{48,49},{56,57},{64,65... | collective-permute-start | bytes 884744 | tf_op jit(solution)/shard_map/ppermute | solution.py:508
  63.5 27.7 %collective-permute-start.11 = (bf16[96,1536]{1,0:T(8,128)(2,1)}, bf16[96,1536]{1,0:T(8,128)(2,1)S(1)}, u32[]{:S(2)}, u32[]{:S(2)}) collective-permute-start(bf16[96,1536]{1,0:T(8,128)(2,1)} %get-tuple-element.30), channel_id=1, source_target_pairs={{0,133},{8,141},{16,149},{24,157},{32,165},{40,173},{48,181},{56,1... | collective-permute-start | bytes 884744 | tf_op jit(solution)/shard_map/ppermute | solution.py:508
  66.1 32.0 %collective-permute-start.12 = (bf16[96,1536]{1,0:T(8,128)(2,1)}, bf16[96,1536]{1,0:T(8,128)(2,1)S(1)}, u32[]{:S(2)}, u32[]{:S(2)}) collective-permute-start(bf16[96,1536]{1,0:T(8,128)(2,1)} %get-tuple-element.31), channel_id=1, source_target_pairs={{0,3},{8,11},{16,19},{24,27},{32,35},{40,43},{48,51},{56,59},{64,6... | collective-permute-start | bytes 884744 | tf_op jit(solution)/shard_map/ppermute | solution.py:508
  68.1 30.0 %collective-permute-start.13 = (bf16[96,1536]{1,0:T(8,128)(2,1)}, bf16[96,1536]{1,0:T(8,128)(2,1)S(1)}, u32[]{:S(2)}, u32[]{:S(2)}) collective-permute-start(bf16[96,1536]{1,0:T(8,128)(2,1)} %get-tuple-element.32), channel_id=1, source_target_pairs={{0,135},{8,143},{16,151},{24,159},{32,167},{40,175},{48,183},{56,1... | collective-permute-start | bytes 884744 | tf_op jit(solution)/shard_map/ppermute | solution.py:508
  71.7 30.6 %copy-start.6 = (bf16[96,1536]{1,0:T(8,128)(2,1)}, bf16[96,1536]{1,0:T(8,128)(2,1)S(1)}, u32[]{:S(2)}) copy-start(bf16[96,1536]{1,0:T(8,128)(2,1)S(1)} %collective-permute-done.9.refs_1_.refs_9_) | copy-start | bytes 884740
  71.7 26.5 %collective-permute-start.14 = (bf16[96,1536]{1,0:T(8,128)(2,1)}, bf16[96,1536]{1,0:T(8,128)(2,1)S(1)}, u32[]{:S(2)}, u32[]{:S(2)}) collective-permute-start(bf16[96,1536]{1,0:T(8,128)(2,1)} %get-tuple-element.33), channel_id=1, source_target_pairs={{0,2},{8,10},{16,18},{24,26},{32,34},{40,42},{48,50},{56,58},{64,6... | collective-permute-start | bytes 884744 | tf_op jit(solution)/shard_map/ppermute | solution.py:508
  73.1 29.1 %copy-start.7 = (bf16[96,1536]{1,0:T(8,128)(2,1)}, bf16[96,1536]{1,0:T(8,128)(2,1)S(1)}, u32[]{:S(2)}) copy-start(bf16[96,1536]{1,0:T(8,128)(2,1)S(1)} %collective-permute-done.10.refs_2_.refs_10_) | copy-start | bytes 884740
  73.1 29.1 %collective-permute-start.15 = (bf16[96,1536]{1,0:T(8,128)(2,1)S(1)}, bf16[96,1536]{1,0:T(8,128)(2,1)S(1)}, u32[]{:S(2)}, u32[]{:S(2)}) collective-permute-start(bf16[96,1536]{1,0:T(8,128)(2,1)S(1)} %get-tuple-element.34), channel_id=1, source_target_pairs={{0,134},{8,142},{16,150},{24,158},{32,166},{40,174},{48,182},{56,1... | collective-permute-start | bytes 884744 | tf_op jit(solution)/shard_map/ppermute | solution.py:508
  77.3 33.0 %all-to-all-start.2 = ((f32[256,1,128]{2,1,0:T(1,128)}), f32[256,1,128]{2,1,0:T(1,128)S(1)}, u32[]{:S(2)}, u32[]{:S(2)}) async-start(f32[256,1,128]{2,1,0:T(1,128)} %get-tuple-element.25), calls=%async_computation.2 | async-start | bytes 262144 | tf_op jit(solution)/shard_map/all_to_all | solution.py:64
  91.2 11.1 %copy-start.8 = (bf16[96,1536]{1,0:T(8,128)(2,1)}, bf16[96,1536]{1,0:T(8,128)(2,1)S(1)}, u32[]{:S(2)}) copy-start(bf16[96,1536]{1,0:T(8,128)(2,1)S(1)} %collective-permute-done.11.refs_3_.refs_11_) | copy-start | bytes 884740
  91.2 19.2 %collective-permute-start.8 = (f32[32,512]{1,0:T(8,128)S(1)}, f32[32,512]{1,0:T(8,128)S(1)}, u32[]{:S(2)}, u32[]{:S(2)}) collective-permute-start(f32[32,512]{1,0:T(8,128)S(1)} %get-tuple-element.26), channel_id=1, source_target_pairs={{0,0},{8,8},{16,1},{24,9},{32,2},{40,10},{48,3},{56,11},{64,4},{72... | collective-permute-start | bytes 196616 | tf_op jit(solution)/shard_map/ppermute | solution.py:511
  98.2 4.1 %copy-start.9 = (bf16[96,1536]{1,0:T(8,128)(2,1)}, bf16[96,1536]{1,0:T(8,128)(2,1)S(1)}, u32[]{:S(2)}) copy-start(bf16[96,1536]{1,0:T(8,128)(2,1)S(1)} %collective-permute-done.12.refs_4_.refs_12_) | copy-start | bytes 884740
  98.2 4.1 %copy-start.10 = (bf16[96,1536]{1,0:T(8,128)(2,1)}, bf16[96,1536]{1,0:T(8,128)(2,1)S(1)}, u32[]{:S(2)}) copy-start(bf16[96,1536]{1,0:T(8,128)(2,1)S(1)} %collective-permute-done.13.refs_5_.refs_13_) | copy-start | bytes 884740
  98.2 4.1 %copy-start.11 = (bf16[96,1536]{1,0:T(8,128)(2,1)}, bf16[96,1536]{1,0:T(8,128)(2,1)S(1)}, u32[]{:S(2)}) copy-start(bf16[96,1536]{1,0:T(8,128)(2,1)S(1)} %collective-permute-done.14.refs_6_.refs_14_) | copy-start | bytes 884740
  102.3 0.7 copy-start.12
  110.4 1.4 %copy-start = (bf16[8,96,1024]{2,1,0:T(8,128)(2,1)S(1)}, bf16[8,96,1024]{2,1,0:T(8,128)(2,1)}, u32[]{:S(2)}) copy-start(bf16[8,96,1024]{2,1,0:T(8,128)(2,1)} %get-tuple-element.35.back_ref) | copy-start | bytes 4718596

commit v4 on v3

--- a/solution.py
+++ b/solution.py
@@ -46,30 +46,30 @@
     ]
 
 
-X_STEPS = (0, 1, 3, 2)
-STEPS = [(dx, pair) for dx in X_STEPS for pair in (0, 1)]
+STEPS = [(0, 0), (2, 1), (2, 0), (1, 1), (3, 1), (0, 1), (1, 0), (3, 0)]
 CORE_SWAP = [(i, i ^ 1) for i in range(32)]
 SAME_CORE = [[l * 16 + z * 2 + c for l in (0, 1) for z in range(8)] for c in (0, 1)]
+AWAY = (3, 2, 0, 1)
+
+
+def summed_at(x, b, x_home):
+    away = AWAY[(x_home - x) % 4]
+    return (2 * x + 1 + away) % 8 if b else (2 * x - away) % 8
+
+
 HOME = [
-    (joint(h, x, l, z, c), joint(z // 4, z % 4, h, 2 * x + l, c))
+    (joint(h, x, k, summed_at(x, b, i), c), joint(k, i, h, 2 * x + b, c))
     for h in (0, 1)
     for x in range(4)
-    for l in (0, 1)
-    for z in range(8)
+    for k in (0, 1)
+    for i in range(4)
+    for b in (0, 1)
     for c in (0, 1)
 ]
 
 
 def exchange(value, groups):
     return lax.all_to_all(value, ALL, 0, 0, axis_index_groups=groups)
-
-
-def along_x(value):
-    return [value] + [lax.ppermute(value, ALL, moved(dx, 0)) for dx in X_STEPS[1:]]
-
-
-def to_pair(value):
-    return lax.ppermute(value, ALL, moved(0, 1))
 
 
 def to_core(value):
@@ -84,11 +84,6 @@
 def rows_at(sign):
     at = coordinates()
     return [(at["y_hi"] + pair) % 2 * 4 + (at["x"] + 4 + sign * dx) % 4 for dx, pair in STEPS]
-
-
-def sources():
-    behind = rows_at(-1)
-    return [behind[2 * i : 2 * i + 2] for i in range(4)]
 
 
 def params(limit=VMEM_LIMIT):
@@ -211,7 +206,7 @@
     return pl.pallas_call(
         c_grad_kernel,
         grid=(GROUPS,),
-        out_shape=jax.ShapeDtypeStruct((LIVE, NARROW), BF16),
+        out_shape=pltpu.VMEM((LIVE, NARROW), BF16),
         in_specs=[
             pl.BlockSpec((1, 32), lambda q: (0, 0)),
             pl.BlockSpec((32, 32), lambda q: (0, 0)),
@@ -240,17 +235,10 @@
     kept_ref, sends_ref, skip_ref, rate_ref, doc_ref, step_ref, g_ref, b_ref, *refs
 ):
     q = pl.program_id(0)
-    proj_refs, both_refs, refs = refs[:MEMBERS], refs[MEMBERS : 2 * MEMBERS], refs[2 * MEMBERS :]
-    out_ref, back_ref, totals_scr, source_scr, bias_scr, live_scr, sems = refs
-    copies = [
-        pltpu.make_async_copy(ref.at[:, pl.ds(NARROW, CHUNK)], back_ref.at[f], sems.at[i])
-        for i, (ref, f) in enumerate(zip(both_refs, rows_at(-1)))
-    ]
+    proj_refs, (out_ref, totals_scr, source_scr, bias_scr, live_scr) = refs[:MEMBERS], refs[MEMBERS:]
 
     @pl.when(q == 0)
     def _():
-        for copy in copies:
-            copy.start()
         totals, source = head_tables(rate_ref, step_ref)
         keep_tables(totals_scr, source_scr, totals, source)
         s, t = places((LIVE, ROWS))
@@ -287,21 +275,13 @@
         out_ref[:LIVE, lanes] = grads.astype(BF16)
     out_ref[LIVE:, :] = jnp.zeros((ROWS - LIVE, HPG * HDIM), BF16)
 
-    @pl.when(q == GROUPS - 1)
-    def _():
-        for copy in copies:
-            copy.wait()
-
 
 def scan_grad_call(kept, sends, skip, rate, docs, steps, out_grad, b_factors, shares):
     wide = HPG * HDIM
     return pl.pallas_call(
         scan_grad_kernel,
         grid=(GROUPS,),
-        out_shape=[
-            jax.ShapeDtypeStruct((ROWS, D), BF16),
-            jax.ShapeDtypeStruct((MEMBERS, LIVE, CHUNK), BF16),
-        ],
+        out_shape=jax.ShapeDtypeStruct((ROWS, D), BF16),
         in_specs=[
             pl.BlockSpec((1, 32), lambda q: (0, 0)),
             pl.BlockSpec((32, 32), lambda q: (0, 0)),
@@ -312,32 +292,35 @@
             pl.BlockSpec((ROWS, wide), lambda q: (0, q)),
             pl.BlockSpec((ROWS, STATE), lambda q: (0, q)),
         ]
-        + [pl.BlockSpec((LIVE, STATE), lambda q: (0, q))] * MEMBERS
-        + [pl.BlockSpec(memory_space=pl.ANY)] * MEMBERS,
-        out_specs=[
-            pl.BlockSpec((ROWS, wide), lambda q: (0, q)),
-            pl.BlockSpec((MEMBERS, LIVE, CHUNK), lambda q: (0, 0, 0)),
-        ],
+        + [pl.BlockSpec((LIVE, STATE), lambda q: (0, q))] * MEMBERS,
+        out_specs=pl.BlockSpec((ROWS, wide), lambda q: (0, q)),
         scratch_shapes=[
             pltpu.VMEM((HEADS, ROWS), F32),
             pltpu.VMEM((GROUPS, ROWS, HEADS), F32),
             pltpu.VMEM((LIVE, ROWS), F32),
             pltpu.VMEM((LIVE, ROWS), F32),
-            pltpu.SemaphoreType.DMA((MEMBERS,)),
         ],
         compiler_params=params(),
         cost_estimate=pl.CostEstimate(
             flops=4 * LIVE * ROWS * D, bytes_accessed=4 * ROWS * D, transcendentals=HEADS * LIVE * ROWS
         ),
         name="scan_grad",
-    )(kept, sends, skip, rate, docs, steps, out_grad, b_factors, *shares, *shares)
+    )(kept, sends, skip, rate, docs, steps, out_grad, b_factors, *shares)
 
 
 def weight_kernel(s_ref, *refs):
     c_refs, (keep_ref, send_ref, grads) = refs[:MEMBERS], refs[MEMBERS:]
     for c_ref, f in zip(c_refs, rows_at(-1)):
         grads[f] = c_ref[...]
-    first_core = coordinates()["core"] == 0
+    at = coordinates()
+    first_core = at["core"] == 0
+
+    def place(b, j):
+        step = (j % 4 + 4 - at["x"]) % 4
+        away = jnp.where(step == 0, AWAY[0], jnp.where(step == 1, AWAY[1], jnp.where(step == 2, AWAY[2], AWAY[3])))
+        z = 2 * at["x"] + 1 + away if b else 2 * at["x"] + 8 - away
+        return j // 4 * 8 + z % 8
+
     wide = 256
     rows = MEMBERS * LIVE
     for i in range(CHUNK // wide):
@@ -347,15 +330,17 @@
             (((0,), (0,)), ((), ())),
             preferred_element_type=F32,
         ).reshape(8, 32, NARROW)
-        place = slice(i // 2 * 8, i // 2 * 8 + 8)
-
-        @pl.when(first_core == (i % 2 == 0))
+        b, core = i // 2, i % 2
+
+        @pl.when(first_core == (core == 0))
         def _():
-            keep_ref[place] = part
-
-        @pl.when(first_core != (i % 2 == 0))
+            for j in range(8):
+                keep_ref[place(b, j)] = part[j]
+
+        @pl.when(first_core != (core == 0))
         def _():
-            send_ref[place] = part.astype(BF16)
+            for j in range(8):
+                send_ref[place(b, j)] = part[j].astype(BF16)
 
 
 def weight_call(pieces, grads):
@@ -401,7 +386,8 @@
     vmem = pl.BlockSpec(memory_space=pltpu.VMEM)
     out = pl.pallas_call(
         project_kernel,
-        out_shape=[jax.ShapeDtypeStruct((LIVE, BOTH), BF16)] * MEMBERS
+        out_shape=[pltpu.VMEM((LIVE, BOTH), BF16)]
+        + [pltpu.HBM((LIVE, BOTH), BF16)] * (MEMBERS - 1)
         + [jax.ShapeDtypeStruct((1, 128), F32)],
         in_specs=[vmem] * 3,
         out_specs=[vmem] * 9,
@@ -443,22 +429,23 @@
     )(parts, top)
 
 
-def finish_kernel(tops_ref, sum_ref, back_ref, input_ref, weight_ref, held, sems):
+def finish_kernel(tops_ref, sum_ref, *refs):
+    back_refs, (input_ref, weight_ref, held, sems) = refs[:MEMBERS], refs[MEMBERS:]
     tops = jnp.max(tops_ref[...], axis=0)
     scale = 1.0 / (tops[:, :1] + peak_eps)
     held[:, LIVE:, :] = jnp.zeros((MEMBERS, ROWS - LIVE, CHUNK), BF16)
     copies = []
-    for f in range(MEMBERS):
-        held[f, :LIVE] = (back_ref[f].astype(F32) * scale).astype(BF16)
-        columns = pl.ds(f * CHUNK, CHUNK)
-        copies.append(pltpu.make_async_copy(held.at[f], input_ref.at[:, columns], sems.at[f]))
+    for i, (ref, f) in enumerate(zip(back_refs, rows_at(-1))):
+        held[i, :LIVE] = (ref[:, NARROW:].astype(F32) * scale).astype(BF16)
+        columns = pl.ds(pl.multiple_of(f * CHUNK, CHUNK), CHUNK)
+        copies.append(pltpu.make_async_copy(held.at[i], input_ref.at[:, columns], sems.at[i]))
         copies[-1].start()
     weight_ref[...] = sum_ref[...] / (tops[:, 64:65] + peak_eps)
     for copy in copies:
         copy.wait()
 
 
-def finish_call(tops, back, weight_sum):
+def finish_call(tops, both, weight_sum):
     vmem = pl.BlockSpec(memory_space=pltpu.VMEM)
     return pl.pallas_call(
         finish_kernel,
@@ -466,7 +453,7 @@
             jax.ShapeDtypeStruct((ROWS, D), BF16),
             jax.ShapeDtypeStruct((32, NARROW), F32),
         ],
-        in_specs=[vmem] * 3,
+        in_specs=[vmem] * (2 + MEMBERS),
         out_specs=[pl.BlockSpec(memory_space=pl.ANY), vmem],
         scratch_shapes=[
             pltpu.VMEM((MEMBERS, ROWS, CHUNK), BF16),
@@ -475,7 +462,7 @@
         compiler_params=params(16 * 2**20),
         cost_estimate=pl.CostEstimate(flops=LIVE * D, bytes_accessed=4 * ROWS * D, transcendentals=0),
         name="finish",
-    )(tops, weight_sum, back)
+    )(tops, weight_sum, *both)
 
 
 def shards(
@@ -501,18 +488,21 @@
     grads = [c_own] + [lax.ppermute(c_own, ALL, moved(*step)) for step in STEPS[1:]]
 
     keep, send, grads = weight_call(pieces, grads)
-    parts = (keep + to_core(send).astype(F32)).astype(BF16)
+    both, top = project_call(c_weight, pieces, grads)
+    got = to_core(send)
+    got, top = lax.optimization_barrier((got, top))
+    parts = (keep + got.astype(F32)).astype(BF16)
     parts = lax.all_to_all(parts, "dp", 0, 0, axis_index_groups=SAME_CORE)
 
-    both, top = project_call(c_weight, pieces, grads)
     both = [both[0]] + [lax.ppermute(value, ALL, moved(*step)) for value, step in zip(both[1:], STEPS[1:])]
     weight_sum, tops = peak_call(parts, top)
     tops = exchange(tops, None)
     weight_sum = lax.ppermute(weight_sum, ALL, HOME)
-    scan_grad, back = scan_grad_call(
+    both = [pltpu.with_memory_space_constraint(value, pltpu.VMEM) for value in both]
+    scan_grad = scan_grad_call(
         kept, sends, skip_gain, rate, docs, step_size, out_grad, b_factors, both
     )
-    input_grad, readout_weight_gradient = finish_call(tops, back, weight_sum)
+    input_grad, readout_weight_gradient = finish_call(tops, both, weight_sum)
     return (input_grad, scan_grad, readout_weight_gradient)
 
 

time: 115 us -> 107 us (0.930)
  the two profiles are of different devices: /device:TPU:94 before, /device:TPU:5 now
where the time goes in v4:
time: 107 us; the launch traced here: 105 us
  starting transfers between devices  61.4 us (57%)
  Pallas kernels  23.1 us (22%)
  waiting for transfers between devices  18.2 us (17%)
    all_to_all x2, starting transfers between devices, exchange(): return lax.all_to_all(value, ALL, 0, 0, axis_index_groups=groups)  20.3 us
    ppermute x7, starting transfers between devices, shards(): lax.ppermute(c_own, ALL, moved(*step))  12.2 us
    ppermute x7, starting transfers between devices, shards(): lax.ppermute(value, ALL, moved(*step))  10.7 us
    ppermute x7, waiting for transfers between devices, shards(): lax.ppermute(c_own, ALL, moved(*step))  10 us
    all_to_all x1, starting transfers between devices, shards(): parts = lax.all_to_all(parts, 'dp', 0, 0, axis_index_groups=SAME_CORE)  8.29 us
    ppermute x7, waiting for transfers between devices, shards(): lax.ppermute(value, ALL, moved(*step))  8.17 us
    pallas_call x1, Pallas kernels, scan_grad_call(): pl.pallas_call(scan_grad_kernel, grid=(GROUPS,), out_shape=jax.ShapeDtype...  6.39 us
    pallas_call x1, Pallas kernels, c_grad_call(): pl.pallas_call(c_grad_kernel, grid=(GROUPS,), out_shape=pltpu.VMEM((LIVE,...  5.87 us
  transfers between devices with their start and end apart: 19, of which 6 were waited for; matrix products, arithmetic and copies ran while one was open for 0% of the time, Pallas kernels for 16%

profile of v4, /device:TPU:5, one launch (start us, length us, event | category | flops | bytes accessed | tf_op | source)
XLA Modules:
  0.0 104.6 jit_solution(14954333812103128778)
XLA Ops:
  0.6 2.7 %pack.1 = bf16[8,96,1024]{2,1,0:T(8,128)(2,1)} custom-call(bf16[128,8192]{1,0:T(8,128)(2,1)} %s_ref.1), custom_call_target="tpu_custom_call" | custom-call | bytes 3145728 | tf_op jit(solution)/shard_map/pack/pallas_call | solution.py:107
  3.3 6.7 %all-to-all-start = ((bf16[8,96,1024]{2,1,0:T(8,128)(2,1)}), bf16[8,96,1024]{2,1,0:T(8,128)(2,1)S(1)}, u32[]{:S(2)}, u32[]{:S(2)}) async-start(bf16[8,96,1024]{2,1,0:T(8,128)(2,1)} %pack.1), calls=%async_computation | async-start | bytes 3145728 | tf_op jit(solution)/shard_map/all_to_all | solution.py:72
  10.0 5.9 %c_grad.1.refs_0_ = bf16[96,512]{1,0:T(8,128)(2,1)S(1)} custom-call(s32[1,32]{1,0:T(1,128)} %bitcast.6, s32[32,32]{1,0:T(8,128)} %bitcast.4, f32[1,128]{1,0:T(1,128)} %bitcast.8, s32[1,128]{1,0:T(1,128)} %bitcast.10, f32[128,128]{1,0:T(8,128)} %step_ref.3, bf16[128,8192]{1,0:T(8,128)(2,1)} %g_ref.3, bf16[128,8192]{1,0:T(8,128)(2,1)} %x_ref.1, ...), custom_call_target="tpu_custom_call" | custom-call | flops 402653184 | bytes 4194304 | tf_op jit(solution)/shard_map/c_grad/pallas_call | solution.py:206
  15.9 0.4 collective-permute-start.6
  16.3 1.2 %collective-permute-start.5 = (bf16[96,512]{1,0:T(8,128)(2,1)S(1)}, bf16[96,512]{1,0:T(8,128)(2,1)S(1)}, u32[]{:S(2)}, u32[]{:S(2)}) collective-permute-start(bf16[96,512]{1,0:T(8,128)(2,1)S(1)} %c_grad.1.refs_0_), channel_id=1, source_target_pairs={{0,1},{8,9},{16,17},{24,25},{32,33},{40,41},{48,49},{56,57},{64,65... | collective-permute-start | bytes 294920 | tf_op jit(solution)/shard_map/ppermute | solution.py:488
  17.5 2.4 %collective-permute-start.4 = (bf16[96,512]{1,0:T(8,128)(2,1)S(1)}, bf16[96,512]{1,0:T(8,128)(2,1)S(1)}, u32[]{:S(2)}, u32[]{:S(2)}) collective-permute-start(bf16[96,512]{1,0:T(8,128)(2,1)S(1)} %c_grad.1.refs_0_), channel_id=1, source_target_pairs={{0,132},{8,140},{16,148},{24,156},{32,164},{40,172},{48,180},{56,1... | collective-permute-start | bytes 294920 | tf_op jit(solution)/shard_map/ppermute | solution.py:488
  19.9 0.3 collective-permute-start.3
  20.1 3.3 %collective-permute-start.2 = (bf16[96,512]{1,0:T(8,128)(2,1)S(1)}, bf16[96,512]{1,0:T(8,128)(2,1)S(1)}, u32[]{:S(2)}, u32[]{:S(2)}) collective-permute-start(bf16[96,512]{1,0:T(8,128)(2,1)S(1)} %c_grad.1.refs_0_), channel_id=1, source_target_pairs={{0,133},{8,141},{16,149},{24,157},{32,165},{40,173},{48,181},{56,1... | collective-permute-start | bytes 294920 | tf_op jit(solution)/shard_map/ppermute | solution.py:488
  23.4 6.4 %collective-permute-done.6.refs_7_ = bf16[96,512]{1,0:T(8,128)(2,1)S(1)} collective-permute-done((bf16[96,512]{1,0:T(8,128)(2,1)S(1)}, bf16[96,512]{1,0:T(8,128)(2,1)S(1)}, u32[]{:S(2)}, u32[]{:S(2)}) %collective-permute-start.6) | collective-permute-done | bytes 98336 | tf_op jit(solution)/shard_map/ppermute | solution.py:488
  29.9 0.7 collective-permute-start.1
  30.6 0.4 collective-permute-done.5.refs_6_
  31.0 3.9 %collective-permute-start = (bf16[96,512]{1,0:T(8,128)(2,1)S(1)}, bf16[96,512]{1,0:T(8,128)(2,1)S(1)}, u32[]{:S(2)}, u32[]{:S(2)}) collective-permute-start(bf16[96,512]{1,0:T(8,128)(2,1)S(1)} %c_grad.1.refs_0_), channel_id=1, source_target_pairs={{0,134},{8,142},{16,150},{24,158},{32,166},{40,174},{48,182},{56,1... | collective-permute-start | bytes 294920 | tf_op jit(solution)/shard_map/ppermute | solution.py:488
  35.0 1.8 %collective-permute-done.4.refs_5_ = bf16[96,512]{1,0:T(8,128)(2,1)S(1)} collective-permute-done((bf16[96,512]{1,0:T(8,128)(2,1)S(1)}, bf16[96,512]{1,0:T(8,128)(2,1)S(1)}, u32[]{:S(2)}, u32[]{:S(2)}) %collective-permute-start.4) | collective-permute-done | bytes 98336 | tf_op jit(solution)/shard_map/ppermute | solution.py:488
  36.8 1.3 %collective-permute-done.refs_1_ = bf16[96,512]{1,0:T(8,128)(2,1)S(1)} collective-permute-done((bf16[96,512]{1,0:T(8,128)(2,1)S(1)}, bf16[96,512]{1,0:T(8,128)(2,1)S(1)}, u32[]{:S(2)}, u32[]{:S(2)}) %collective-permute-start) | collective-permute-done | bytes 98336 | tf_op jit(solution)/shard_map/ppermute | solution.py:488
  38.1 1.9 %weight_part.1 = (f32[16,32,512]{2,1,0:T(8,128)S(1)}, bf16[16,32,512]{2,1,0:T(8,128)(2,1)S(1)}, bf16[8,96,512]{2,1,0:T(8,128)(2,1)S(1)}) custom-call(bf16[8,96,1024]{2,1,0:T(8,128)(2,1)S(1)} %all-to-all-done.s_ref, bf16[96,512]{1,0:T(8,128)(2,1)S(1)} %c_grad.1.refs_0_, bf16[96,512]{1,0:T(8,128)(2,1)S(1)} %collective-permute-done.refs_1_, ...), custom_call_target="tpu_custom_call" | custom-call | flops 805306368 | bytes 5242880 | tf_op jit(solution)/shard_map/weight_part/pallas_call | solution.py:348
  40.0 4.5 %collective-permute-start.7 = (bf16[16,32,512]{2,1,0:T(8,128)(2,1)S(1)}, bf16[16,32,512]{2,1,0:T(8,128)(2,1)S(1)}, u32[]{:S(2)}, u32[]{:S(2)}) collective-permute-start(bf16[16,32,512]{2,1,0:T(8,128)(2,1)S(1)} %get-tuple-element.22), channel_id=1, source_target_pairs={{0,8},{8,0},{16,24},{24,16},{32,40},{40,32},{48,56},{56,48},{64,72... | collective-permute-start | bytes 1572872 | tf_op jit(solution)/shard_map/ppermute | solution.py:76
  44.5 3.2 %project.1 = (bf16[96,1536]{1,0:T(8,128)(2,1)S(1)}, bf16[96,1536]{1,0:T(8,128)(2,1)}, bf16[96,1536]{1,0:T(8,128)(2,1)}, bf16[96,1536]{1,0:T(8,128)(2,1)}, bf16[9...) custom-call(bf16[1024,512]{1,0:T(8,128)(2,1)S(1)} %copy-done, ...), custom_call_target="tpu_custom_call" | custom-call | flops 1610612736 | bytes 6291456 | tf_op jit(solution)/shard_map/project/pallas_call | solution.py:387
  47.7 1.0 add_convert_fusion
  48.6 8.3 %all-to-all-start.1 = ((bf16[16,32,512]{2,1,0:T(8,128)(2,1)}), bf16[16,32,512]{2,1,0:T(8,128)(2,1)S(1)}, u32[]{:S(2)}, u32[]{:S(2)}) async-start(bf16[16,32,512]{2,1,0:T(8,128)(2,1)} %add_convert_fusion), calls=%async_computation.1 | async-start | bytes 1048576 | tf_op jit(solution)/shard_map/all_to_all | solution.py:495
  56.9 5.5 %collective-permute-start.9 = (bf16[96,1536]{1,0:T(8,128)(2,1)S(1)}, bf16[96,1536]{1,0:T(8,128)(2,1)S(1)}, u32[]{:S(2)}, u32[]{:S(2)}) collective-permute-start(bf16[96,1536]{1,0:T(8,128)(2,1)S(1)} %copy-done.3), channel_id=1, source_target_pairs={{0,134},{8,142},{16,150},{24,158},{32,166},{40,174},{48,182},{56,1... | collective-permute-start | bytes 884744 | tf_op jit(solution)/shard_map/ppermute | solution.py:497
  62.4 0.4 collective-permute-start.10
  62.8 0.4 collective-permute-start.11
  63.2 3.2 %collective-permute-start.12 = (bf16[96,1536]{1,0:T(8,128)(2,1)}, bf16[96,1536]{1,0:T(8,128)(2,1)S(1)}, u32[]{:S(2)}, u32[]{:S(2)}) collective-permute-start(bf16[96,1536]{1,0:T(8,128)(2,1)} %get-tuple-element.33), channel_id=1, source_target_pairs={{0,135},{8,143},{16,151},{24,159},{32,167},{40,175},{48,183},{56,1... | collective-permute-start | bytes 884744 | tf_op jit(solution)/shard_map/ppermute | solution.py:497
  66.4 0.3 collective-permute-start.13
  66.7 2.5 %collective-permute-done.9.refs_1_ = bf16[96,1536]{1,0:T(8,128)(2,1)S(1)} collective-permute-done((bf16[96,1536]{1,0:T(8,128)(2,1)S(1)}, bf16[96,1536]{1,0:T(8,128)(2,1)S(1)}, u32[]{:S(2)}, u32[]{:S(2)}) %collective-permute-start.9) | collective-permute-done | bytes 294944 | tf_op jit(solution)/shard_map/ppermute | solution.py:497
  69.2 0.8 collective-permute-start.14
  70.1 5.6 %collective-permute-done.10.refs_2_ = bf16[96,1536]{1,0:T(8,128)(2,1)S(1)} collective-permute-done((bf16[96,1536]{1,0:T(8,128)(2,1)S(1)}, bf16[96,1536]{1,0:T(8,128)(2,1)S(1)}, u32[]{:S(2)}, u32[]{:S(2)}) %collective-permute-start.10) | collective-permute-done | bytes 294944 | tf_op jit(solution)/shard_map/ppermute | solution.py:497
  75.8 0.9 peaks.1
  76.7 13.6 %all-to-all-start.2 = ((f32[256,1,128]{2,1,0:T(1,128)}), f32[256,1,128]{2,1,0:T(1,128)S(1)}, u32[]{:S(2)}, u32[]{:S(2)}) async-start(f32[256,1,128]{2,1,0:T(1,128)} %get-tuple-element.27), calls=%async_computation.2 | async-start | bytes 262144 | tf_op jit(solution)/shard_map/all_to_all | solution.py:72
  90.3 5.5 %collective-permute-start.8 = (f32[32,512]{1,0:T(8,128)S(1)}, f32[32,512]{1,0:T(8,128)S(1)}, u32[]{:S(2)}, u32[]{:S(2)}) collective-permute-start(f32[32,512]{1,0:T(8,128)S(1)} %get-tuple-element.28), channel_id=1, source_target_pairs={{80,0},{88,8},{64,16},{72,24},{96,1},{104,9},{48,17},{56,25},{0,2}... | collective-permute-start | bytes 196616 | tf_op jit(solution)/shard_map/ppermute | solution.py:500
  95.8 6.4 %scan_grad.1 = bf16[128,8192]{1,0:T(8,128)(2,1)} custom-call(s32[1,32]{1,0:T(1,128)} %bitcast.7, s32[32,32]{1,0:T(8,128)} %bitcast.5, f32[128]{0:T(128)} %skip_ref.1, f32[1,128]{1,0:T(1,128)} %bitcast.9, s32[1,128]{1,0:T(1,128)} %bitcast.11, f32[128,128]{1,0:T(8,128)} %step_ref.3, bf16[128,8192]{1,0:T(8,128)(2,1)} %g_ref.3, bf16[128,512]{1,0:T(8,128)(2,1)} %b_ref.3, ...), custom_call_target="tpu_custom_call" | custom-call | flops 402653184 | bytes 4194304 | tf_op jit(solution)/shard_map/scan_grad/pallas_call | solution.py:281
  102.2 2.2 %finish.1 = (bf16[128,8192]{1,0:T(8,128)(2,1)}, f32[32,512]{1,0:T(8,128)}) custom-call(f32[256,1,128]{2,1,0:T(1,128)S(1)} %all-to-all-done.2.tops_ref, f32[32,512]{1,0:T(8,128)S(1)} %collective-permute-done.8.sum_ref, bf16[96,1536]{1,0:T(8,128)(2,1)S(1)} %get-tuple-element.29.refs_0_, bf16[96,1536]{1,0:T(8,128)(2,1)S(1)} %collective-permute-done.9.refs_1_, ...), custom_call_target="tpu_custom_call" | custom-call | flops 786432 | bytes 4194304 | tf_op jit(solution)/shard_map/finish/pallas_call | solution.py:450
  (22 shorter events, 0.2 us)
Async XLA Ops:
  3.3 34.8 %all-to-all-start = ((bf16[8,96,1024]{2,1,0:T(8,128)(2,1)}), bf16[8,96,1024]{2,1,0:T(8,128)(2,1)S(1)}, u32[]{:S(2)}, u32[]{:S(2)}) async-start(bf16[8,96,1024]{2,1,0:T(8,128)(2,1)} %pack.1), calls=%async_computation | async-start | bytes 3145728 | tf_op jit(solution)/shard_map/all_to_all | solution.py:72
  15.9 28.6 %copy-start = (bf16[1024,512]{1,0:T(8,128)(2,1)S(1)}, bf16[1024,512]{1,0:T(8,128)(2,1)}, u32[]{:S(2)}) copy-start(bf16[1024,512]{1,0:T(8,128)(2,1)} %w_ref.1) | copy-start | bytes 3145732
  15.9 14.0 %collective-permute-start.6 = (bf16[96,512]{1,0:T(8,128)(2,1)S(1)}, bf16[96,512]{1,0:T(8,128)(2,1)S(1)}, u32[]{:S(2)}, u32[]{:S(2)}) collective-permute-start(bf16[96,512]{1,0:T(8,128)(2,1)S(1)} %c_grad.1.refs_0_), channel_id=1, source_target_pairs={{0,3},{8,11},{16,19},{24,27},{32,35},{40,43},{48,51},{56,59},{64,6... | collective-permute-start | bytes 294920 | tf_op jit(solution)/shard_map/ppermute | solution.py:488
  16.3 14.8 %collective-permute-start.5 = (bf16[96,512]{1,0:T(8,128)(2,1)S(1)}, bf16[96,512]{1,0:T(8,128)(2,1)S(1)}, u32[]{:S(2)}, u32[]{:S(2)}) collective-permute-start(bf16[96,512]{1,0:T(8,128)(2,1)S(1)} %c_grad.1.refs_0_), channel_id=1, source_target_pairs={{0,1},{8,9},{16,17},{24,25},{32,33},{40,41},{48,49},{56,57},{64,65... | collective-permute-start | bytes 294920 | tf_op jit(solution)/shard_map/ppermute | solution.py:488
  17.5 19.4 %collective-permute-start.4 = (bf16[96,512]{1,0:T(8,128)(2,1)S(1)}, bf16[96,512]{1,0:T(8,128)(2,1)S(1)}, u32[]{:S(2)}, u32[]{:S(2)}) collective-permute-start(bf16[96,512]{1,0:T(8,128)(2,1)S(1)} %c_grad.1.refs_0_), channel_id=1, source_target_pairs={{0,132},{8,140},{16,148},{24,156},{32,164},{40,172},{48,180},{56,1... | collective-permute-start | bytes 294920 | tf_op jit(solution)/shard_map/ppermute | solution.py:488
  19.9 17.0 %collective-permute-start.3 = (bf16[96,512]{1,0:T(8,128)(2,1)S(1)}, bf16[96,512]{1,0:T(8,128)(2,1)S(1)}, u32[]{:S(2)}, u32[]{:S(2)}) collective-permute-start(bf16[96,512]{1,0:T(8,128)(2,1)S(1)} %c_grad.1.refs_0_), channel_id=1, source_target_pairs={{0,135},{8,143},{16,151},{24,159},{32,167},{40,175},{48,183},{56,1... | collective-permute-start | bytes 294920 | tf_op jit(solution)/shard_map/ppermute | solution.py:488
  20.1 16.7 %collective-permute-start.2 = (bf16[96,512]{1,0:T(8,128)(2,1)S(1)}, bf16[96,512]{1,0:T(8,128)(2,1)S(1)}, u32[]{:S(2)}, u32[]{:S(2)}) collective-permute-start(bf16[96,512]{1,0:T(8,128)(2,1)S(1)} %c_grad.1.refs_0_), channel_id=1, source_target_pairs={{0,133},{8,141},{16,149},{24,157},{32,165},{40,173},{48,181},{56,1... | collective-permute-start | bytes 294920 | tf_op jit(solution)/shard_map/ppermute | solution.py:488
  29.9 6.9 %collective-permute-start.1 = (bf16[96,512]{1,0:T(8,128)(2,1)S(1)}, bf16[96,512]{1,0:T(8,128)(2,1)S(1)}, u32[]{:S(2)}, u32[]{:S(2)}) collective-permute-start(bf16[96,512]{1,0:T(8,128)(2,1)S(1)} %c_grad.1.refs_0_), channel_id=1, source_target_pairs={{0,2},{8,10},{16,18},{24,26},{32,34},{40,42},{48,50},{56,58},{64,6... | collective-permute-start | bytes 294920 | tf_op jit(solution)/shard_map/ppermute | solution.py:488
  31.0 7.1 %collective-permute-start = (bf16[96,512]{1,0:T(8,128)(2,1)S(1)}, bf16[96,512]{1,0:T(8,128)(2,1)S(1)}, u32[]{:S(2)}, u32[]{:S(2)}) collective-permute-start(bf16[96,512]{1,0:T(8,128)(2,1)S(1)} %c_grad.1.refs_0_), channel_id=1, source_target_pairs={{0,134},{8,142},{16,150},{24,158},{32,166},{40,174},{48,182},{56,1... | collective-permute-start | bytes 294920 | tf_op jit(solution)/shard_map/ppermute | solution.py:488
  40.0 7.7 %collective-permute-start.7 = (bf16[16,32,512]{2,1,0:T(8,128)(2,1)S(1)}, bf16[16,32,512]{2,1,0:T(8,128)(2,1)S(1)}, u32[]{:S(2)}, u32[]{:S(2)}) collective-permute-start(bf16[16,32,512]{2,1,0:T(8,128)(2,1)S(1)} %get-tuple-element.22), channel_id=1, source_target_pairs={{0,8},{8,0},{16,24},{24,16},{32,40},{40,32},{48,56},{56,48},{64,72... | collective-permute-start | bytes 1572872 | tf_op jit(solution)/shard_map/ppermute | solution.py:76
  47.7 9.3 %copy-start.3 = (bf16[96,1536]{1,0:T(8,128)(2,1)S(1)}, bf16[96,1536]{1,0:T(8,128)(2,1)}, u32[]{:S(2)}) copy-start(bf16[96,1536]{1,0:T(8,128)(2,1)} %get-tuple-element.30) | copy-start | bytes 884740
  47.7 14.8 %copy-start.2 = (bf16[96,1536]{1,0:T(8,128)(2,1)S(1)}, bf16[96,1536]{1,0:T(8,128)(2,1)}, u32[]{:S(2)}) copy-start(bf16[96,1536]{1,0:T(8,128)(2,1)} %get-tuple-element.31) | copy-start | bytes 884740
  47.7 28.0 %copy-start.1 = (bf16[96,1536]{1,0:T(8,128)(2,1)S(1)}, bf16[96,1536]{1,0:T(8,128)(2,1)}, u32[]{:S(2)}) copy-start(bf16[96,1536]{1,0:T(8,128)(2,1)} %get-tuple-element.36) | copy-start | bytes 884740
  48.6 27.2 %all-to-all-start.1 = ((bf16[16,32,512]{2,1,0:T(8,128)(2,1)}), bf16[16,32,512]{2,1,0:T(8,128)(2,1)S(1)}, u32[]{:S(2)}, u32[]{:S(2)}) async-start(bf16[16,32,512]{2,1,0:T(8,128)(2,1)} %add_convert_fusion), calls=%async_computation.1 | async-start | bytes 1048576 | tf_op jit(solution)/shard_map/all_to_all | solution.py:495
  56.9 12.3 %collective-permute-start.9 = (bf16[96,1536]{1,0:T(8,128)(2,1)S(1)}, bf16[96,1536]{1,0:T(8,128)(2,1)S(1)}, u32[]{:S(2)}, u32[]{:S(2)}) collective-permute-start(bf16[96,1536]{1,0:T(8,128)(2,1)S(1)} %copy-done.3), channel_id=1, source_target_pairs={{0,134},{8,142},{16,150},{24,158},{32,166},{40,174},{48,182},{56,1... | collective-permute-start | bytes 884744 | tf_op jit(solution)/shard_map/ppermute | solution.py:497
  62.4 13.3 %collective-permute-start.10 = (bf16[96,1536]{1,0:T(8,128)(2,1)S(1)}, bf16[96,1536]{1,0:T(8,128)(2,1)S(1)}, u32[]{:S(2)}, u32[]{:S(2)}) collective-permute-start(bf16[96,1536]{1,0:T(8,128)(2,1)S(1)} %copy-done.2), channel_id=1, source_target_pairs={{0,2},{8,10},{16,18},{24,26},{32,34},{40,42},{48,50},{56,58},{64,6... | collective-permute-start | bytes 884744 | tf_op jit(solution)/shard_map/ppermute | solution.py:497
  62.8 27.5 %collective-permute-start.11 = (bf16[96,1536]{1,0:T(8,128)(2,1)}, bf16[96,1536]{1,0:T(8,128)(2,1)S(1)}, u32[]{:S(2)}, u32[]{:S(2)}) collective-permute-start(bf16[96,1536]{1,0:T(8,128)(2,1)} %get-tuple-element.32), channel_id=1, source_target_pairs={{0,133},{8,141},{16,149},{24,157},{32,165},{40,173},{48,181},{56,1... | collective-permute-start | bytes 884744 | tf_op jit(solution)/shard_map/ppermute | solution.py:497
  63.2 32.6 %collective-permute-start.12 = (bf16[96,1536]{1,0:T(8,128)(2,1)}, bf16[96,1536]{1,0:T(8,128)(2,1)S(1)}, u32[]{:S(2)}, u32[]{:S(2)}) collective-permute-start(bf16[96,1536]{1,0:T(8,128)(2,1)} %get-tuple-element.33), channel_id=1, source_target_pairs={{0,135},{8,143},{16,151},{24,159},{32,167},{40,175},{48,183},{56,1... | collective-permute-start | bytes 884744 | tf_op jit(solution)/shard_map/ppermute | solution.py:497
  66.4 29.4 %collective-permute-start.13 = (bf16[96,1536]{1,0:T(8,128)(2,1)}, bf16[96,1536]{1,0:T(8,128)(2,1)S(1)}, u32[]{:S(2)}, u32[]{:S(2)}) collective-permute-start(bf16[96,1536]{1,0:T(8,128)(2,1)} %get-tuple-element.34), channel_id=1, source_target_pairs={{0,132},{8,140},{16,148},{24,156},{32,164},{40,172},{48,180},{56,1... | collective-permute-start | bytes 884744 | tf_op jit(solution)/shard_map/ppermute | solution.py:497
  69.2 26.6 %collective-permute-start.14 = (bf16[96,1536]{1,0:T(8,128)(2,1)}, bf16[96,1536]{1,0:T(8,128)(2,1)S(1)}, u32[]{:S(2)}, u32[]{:S(2)}) collective-permute-start(bf16[96,1536]{1,0:T(8,128)(2,1)} %get-tuple-element.35), channel_id=1, source_target_pairs={{0,1},{8,9},{16,17},{24,25},{32,33},{40,41},{48,49},{56,57},{64,65... | collective-permute-start | bytes 884744 | tf_op jit(solution)/shard_map/ppermute | solution.py:497
  75.7 20.1 %collective-permute-start.15 = (bf16[96,1536]{1,0:T(8,128)(2,1)S(1)}, bf16[96,1536]{1,0:T(8,128)(2,1)S(1)}, u32[]{:S(2)}, u32[]{:S(2)}) collective-permute-start(bf16[96,1536]{1,0:T(8,128)(2,1)S(1)} %copy-done.1), channel_id=1, source_target_pairs={{0,3},{8,11},{16,19},{24,27},{32,35},{40,43},{48,51},{56,59},{64,6... | collective-permute-start | bytes 884744 | tf_op jit(solution)/shard_map/ppermute | solution.py:497
  76.7 25.5 %all-to-all-start.2 = ((f32[256,1,128]{2,1,0:T(1,128)}), f32[256,1,128]{2,1,0:T(1,128)S(1)}, u32[]{:S(2)}, u32[]{:S(2)}) async-start(f32[256,1,128]{2,1,0:T(1,128)} %get-tuple-element.27), calls=%async_computation.2 | async-start | bytes 262144 | tf_op jit(solution)/shard_map/all_to_all | solution.py:72
  90.3 11.9 %collective-permute-start.8 = (f32[32,512]{1,0:T(8,128)S(1)}, f32[32,512]{1,0:T(8,128)S(1)}, u32[]{:S(2)}, u32[]{:S(2)}) collective-permute-start(f32[32,512]{1,0:T(8,128)S(1)} %get-tuple-element.28), channel_id=1, source_target_pairs={{80,0},{88,8},{64,16},{72,24},{96,1},{104,9},{48,17},{56,25},{0,2}... | collective-permute-start | bytes 196616 | tf_op jit(solution)/shard_map/ppermute | solution.py:500

commit v5 on v4

--- a/solution.py
+++ b/solution.py
@@ -231,23 +231,44 @@
     )(kept, sends, rate, docs, steps, out_grad, scan_input, b_factors)
 
 
-def scan_grad_kernel(
-    kept_ref, sends_ref, skip_ref, rate_ref, doc_ref, step_ref, g_ref, b_ref, *refs
-):
+def tables_kernel(kept_ref, sends_ref, rate_ref, doc_ref, step_ref, out_ref):
+    totals, source = head_tables(rate_ref, step_ref)
+    out_ref[0] = totals
+    out_ref[1] = jnp.transpose(source)
+    s, t = places((LIVE, ROWS))
+    live = live_count(kept_ref, sends_ref)
+    out_ref[2, :LIVE] = row_mask(live, doc_ref, t, s)
+    out_ref[2, LIVE:] = jnp.zeros((ROWS - LIVE, ROWS), F32)
+    out_ref[3, :LIVE] = jnp.where(s < live, 1.0, 0.0)
+    out_ref[3, LIVE:] = jnp.zeros((ROWS - LIVE, ROWS), F32)
+
+
+def tables_call(kept, sends, rate, docs, steps):
+    vmem = pl.BlockSpec(memory_space=pltpu.VMEM)
+    return pl.pallas_call(
+        tables_kernel,
+        out_shape=pltpu.HBM((4, ROWS, ROWS), F32),
+        in_specs=[vmem] * 5,
+        out_specs=vmem,
+        compiler_params=params(),
+        cost_estimate=pl.CostEstimate(flops=0, bytes_accessed=2**19, transcendentals=HEADS * ROWS),
+        name="tables",
+    )(kept, sends, rate, docs, steps)
+
+
+def scan_grad_kernel(skip_ref, tables_ref, g_ref, b_ref, *refs):
     q = pl.program_id(0)
-    proj_refs, (out_ref, totals_scr, source_scr, bias_scr, live_scr) = refs[:MEMBERS], refs[MEMBERS:]
+    proj_refs, (out_ref, source_scr) = refs[:MEMBERS], refs[MEMBERS:]
 
     @pl.when(q == 0)
     def _():
-        totals, source = head_tables(rate_ref, step_ref)
-        keep_tables(totals_scr, source_scr, totals, source)
-        s, t = places((LIVE, ROWS))
-        live = live_count(kept_ref, sends_ref)
-        bias_scr[...] = row_mask(live, doc_ref, t, s)
-        live_scr[...] = jnp.where(s < live, 1.0, 0.0)
-
-    bias = bias_scr[...]
-    totals = totals_scr[group_rows(q), :]
+        source = tables_ref[1]
+        for k in range(GROUPS):
+            source_scr[k] = pltpu.roll(source, HEADS - k * HPG, 1) if k else source
+
+    bias = tables_ref[2, :LIVE, :]
+    alive = tables_ref[3, :LIVE, :]
+    totals = tables_ref[0, group_rows(q), :]
     source_col = source_scr[q]
     half = lax.broadcasted_iota(jnp.int32, (ROWS, 128), 1) < HDIM
     c_proj = proj_refs[0][...].astype(F32)
@@ -257,7 +278,6 @@
     affinity = lax.dot_general(
         b_ref[:LIVE, :], c_proj, (((1,), (1,)), ((), ())), preferred_element_type=F32
     )
-    alive = live_scr[...]
     for p in range(HPG // 2):
         lanes = slice(p * 128, p * 128 + 128)
         g_pair = g_ref[:, lanes]
@@ -276,36 +296,27 @@
     out_ref[LIVE:, :] = jnp.zeros((ROWS - LIVE, HPG * HDIM), BF16)
 
 
-def scan_grad_call(kept, sends, skip, rate, docs, steps, out_grad, b_factors, shares):
+def scan_grad_call(skip, tables, out_grad, b_factors, shares):
     wide = HPG * HDIM
     return pl.pallas_call(
         scan_grad_kernel,
         grid=(GROUPS,),
         out_shape=jax.ShapeDtypeStruct((ROWS, D), BF16),
         in_specs=[
-            pl.BlockSpec((1, 32), lambda q: (0, 0)),
-            pl.BlockSpec((32, 32), lambda q: (0, 0)),
             smem(),
-            row_spec(),
-            row_spec(),
-            pl.BlockSpec((HEADS, ROWS), lambda q: (0, 0)),
+            pl.BlockSpec((4, ROWS, ROWS), lambda q: (0, 0, 0)),
             pl.BlockSpec((ROWS, wide), lambda q: (0, q)),
             pl.BlockSpec((ROWS, STATE), lambda q: (0, q)),
         ]
         + [pl.BlockSpec((LIVE, STATE), lambda q: (0, q))] * MEMBERS,
         out_specs=pl.BlockSpec((ROWS, wide), lambda q: (0, q)),
-        scratch_shapes=[
-            pltpu.VMEM((HEADS, ROWS), F32),
-            pltpu.VMEM((GROUPS, ROWS, HEADS), F32),
-            pltpu.VMEM((LIVE, ROWS), F32),
-            pltpu.VMEM((LIVE, ROWS), F32),
-        ],
+        scratch_shapes=[pltpu.VMEM((GROUPS, ROWS, HEADS), F32)],
         compiler_params=params(),
         cost_estimate=pl.CostEstimate(
             flops=4 * LIVE * ROWS * D, bytes_accessed=4 * ROWS * D, transcendentals=HEADS * LIVE * ROWS
         ),
         name="scan_grad",
-    )(kept, sends, skip, rate, docs, steps, out_grad, b_factors, *shares)
+    )(skip, tables, out_grad, b_factors, *shares)
 
 
 def weight_kernel(s_ref, *refs):
@@ -359,14 +370,45 @@
     )(pieces, *grads)
 
 
-def project_kernel(w_ref, s_ref, grads, *refs):
-    out_refs, (top_ref, held) = refs[:MEMBERS], refs[MEMBERS:]
+def c_proj_kernel(w_ref, s_ref, out_ref):
+    rows = MEMBERS * LIVE
+    part = jnp.dot(s_ref[...].reshape(rows, CHUNK), w_ref[...], preferred_element_type=F32)
+    out_ref[...] = part.astype(BF16).reshape(MEMBERS, LIVE, NARROW)
+
+
+def c_proj_call(weights, pieces):
+    vmem = pl.BlockSpec(memory_space=pltpu.VMEM)
+    return pl.pallas_call(
+        c_proj_kernel,
+        out_shape=jax.ShapeDtypeStruct((MEMBERS, LIVE, NARROW), BF16),
+        in_specs=[vmem] * 2,
+        out_specs=vmem,
+        compiler_params=params(24 * 2**20),
+        cost_estimate=pl.CostEstimate(
+            flops=2 * MEMBERS * LIVE * CHUNK * NARROW, bytes_accessed=4 * 2**20, transcendentals=0
+        ),
+        name="c_proj",
+    )(weights, pieces)
+
+
+def project_kernel(w_ref, proj_ref, grads, *refs):
+    out_refs, (top_ref, held, sems) = refs[:MEMBERS], refs[MEMBERS:]
     rows = MEMBERS * LIVE
     wide = 256
-    proj = jnp.dot(s_ref[...].reshape(rows, CHUNK), w_ref[...], preferred_element_type=F32)
-    held[:, :, :NARROW] = proj.astype(BF16).reshape(MEMBERS, LIVE, NARROW)
+    dests = rows_at(1)
+    copies = []
+    for k, (first, last) in enumerate(((0, NARROW + CHUNK // 2), (NARROW + CHUNK // 2, BOTH))):
+        columns = pl.ds(first, last - first)
+        copies.append(
+            [
+                pltpu.make_async_copy(held.at[f, :, columns], ref.at[:, columns], sems.at[k, i])
+                for i, (ref, f) in enumerate(zip(out_refs, dests))
+            ]
+        )
+    held[:, :, :NARROW] = proj_ref[...]
     top = jnp.zeros((8, wide), F32)
-    for i in range(CHUNK // wide):
+    steps = CHUNK // wide
+    for i in range(steps):
         part = lax.dot_general(
             grads[...].reshape(rows, NARROW),
             w_ref[i * wide : (i + 1) * wide, :],
@@ -377,12 +419,15 @@
             MEMBERS, LIVE, wide
         )
         top = jnp.maximum(top, jnp.max(jnp.abs(part).reshape(rows // 8, 8, wide), axis=0))
-    for out_ref, f in zip(out_refs, rows_at(1)):
-        out_ref[...] = held[f]
+        if i % (steps // 2) == steps // 2 - 1:
+            for copy in copies[i // (steps // 2)]:
+                copy.start()
     top_ref[...] = jnp.broadcast_to(jnp.max(top), (1, 128))
-
-
-def project_call(weights, pieces, grads):
+    for copy in copies[0] + copies[1]:
+        copy.wait()
+
+
+def project_call(weights, proj, grads):
     vmem = pl.BlockSpec(memory_space=pltpu.VMEM)
     out = pl.pallas_call(
         project_kernel,
@@ -390,16 +435,17 @@
         + [pltpu.HBM((LIVE, BOTH), BF16)] * (MEMBERS - 1)
         + [jax.ShapeDtypeStruct((1, 128), F32)],
         in_specs=[vmem] * 3,
-        out_specs=[vmem] * 9,
+        out_specs=[pl.BlockSpec(memory_space=pl.ANY)] * MEMBERS + [vmem],
         scratch_shapes=[
             pltpu.VMEM((MEMBERS, LIVE, BOTH), BF16),
+            pltpu.SemaphoreType.DMA((2, MEMBERS)),
         ],
         compiler_params=params(24 * 2**20),
         cost_estimate=pl.CostEstimate(
-            flops=4 * MEMBERS * LIVE * CHUNK * NARROW, bytes_accessed=6 * 2**20, transcendentals=0
+            flops=2 * MEMBERS * LIVE * CHUNK * NARROW, bytes_accessed=6 * 2**20, transcendentals=0
         ),
         name="project",
-    )(weights, pieces, grads)
+    )(weights, proj, grads)
     return out[:MEMBERS], out[MEMBERS]
 
 
@@ -487,21 +533,25 @@
     c_own = c_grad_call(kept, sends, rate, docs, step_size, out_grad, scan_input, b_factors)
     grads = [c_own] + [lax.ppermute(c_own, ALL, moved(*step)) for step in STEPS[1:]]
 
+    steps, c_own = lax.optimization_barrier((step_size, c_own))
+    tables = tables_call(kept, sends, rate, docs, steps)
+    proj = c_proj_call(c_weight, pieces)
+    grads, tables, proj = lax.optimization_barrier((grads, tables, proj))
     keep, send, grads = weight_call(pieces, grads)
-    both, top = project_call(c_weight, pieces, grads)
+    both, top = project_call(c_weight, proj, grads)
     got = to_core(send)
     got, top = lax.optimization_barrier((got, top))
     parts = (keep + got.astype(F32)).astype(BF16)
     parts = lax.all_to_all(parts, "dp", 0, 0, axis_index_groups=SAME_CORE)
 
-    both = [both[0]] + [lax.ppermute(value, ALL, moved(*step)) for value, step in zip(both[1:], STEPS[1:])]
+    back = [both[0]] + [lax.ppermute(both[i], ALL, moved(*STEPS[i])) for i in range(1, 7)]
     weight_sum, tops = peak_call(parts, top)
+    weight_sum, *late = lax.optimization_barrier((weight_sum, *both[7:]))
     tops = exchange(tops, None)
+    back += [lax.ppermute(value, ALL, moved(*step)) for value, step in zip(late, STEPS[7:])]
     weight_sum = lax.ppermute(weight_sum, ALL, HOME)
-    both = [pltpu.with_memory_space_constraint(value, pltpu.VMEM) for value in both]
-    scan_grad = scan_grad_call(
-        kept, sends, skip_gain, rate, docs, step_size, out_grad, b_factors, both
-    )
+    both = [pltpu.with_memory_space_constraint(value, pltpu.VMEM) for value in back]
+    scan_grad = scan_grad_call(skip_gain, tables, out_grad, b_factors, both)
     input_grad, readout_weight_gradient = finish_call(tops, both, weight_sum)
     return (input_grad, scan_grad, readout_weight_gradient)
 

time: 107 us -> 105 us (0.981)
  waiting for transfers between devices: 18.2 us -> 15.4 us
  Pallas kernels: 23.1 us -> 24.8 us
    ppermute x0 -> x6, starting transfers between devices: none -> 10.8 us  [shards(): lax.ppermute(both[i], ALL, moved(*STEPS[i]))]
    ppermute x7 -> x1, starting transfers between devices: 10.7 us -> 0.16 us  [shards(): lax.ppermute(value, ALL, moved(*step))]
    ppermute x7 -> x1, waiting for transfers between devices: 8.17 us -> 0.01 us  [shards(): lax.ppermute(value, ALL, moved(*step))]
    all_to_all x1, waiting for transfers between devices: 0.01 us -> 4.73 us  [shards(): parts = lax.all_to_all(parts, 'dp', 0, 0, axis_index_groups=SAME_CORE)]
    ppermute x0 -> x6, waiting for transfers between devices: none -> 3.87 us  [shards(): lax.ppermute(both[i], ALL, moved(*STEPS[i]))]
    pallas_call x0 -> x2, Pallas kernels: none -> 3.23 us  [the longest x1 2.26 us: tables_call(): pl.pallas_call(tables_kernel, out_shape=pltpu.HBM((4, ROWS, ROWS), F32),...]
    ppermute x7, waiting for transfers between devices: 10 us -> 6.82 us  [shards(): lax.ppermute(c_own, ALL, moved(*step))]
  transfers between devices with their start and end apart: 19 -> 19, of which waited for: 6 -> 5; matrix products, arithmetic and copies ran while one was open for 0% -> 0% of each run, Pallas kernels for 16% -> 17%
where the time goes in v5:
time: 105 us; the launch traced here: 104 us
  starting transfers between devices  61.5 us (59%)
  Pallas kernels  24.8 us (24%)
  waiting for transfers between devices  15.4 us (15%)
    all_to_all x2, starting transfers between devices, exchange(): return lax.all_to_all(value, ALL, 0, 0, axis_index_groups=groups)  20.2 us
    ppermute x7, starting transfers between devices, shards(): lax.ppermute(c_own, ALL, moved(*step))  12.2 us
    ppermute x6, starting transfers between devices, shards(): lax.ppermute(both[i], ALL, moved(*STEPS[i]))  10.8 us
    all_to_all x1, starting transfers between devices, shards(): parts = lax.all_to_all(parts, 'dp', 0, 0, axis_index_groups=SAME_CORE)  8.29 us
    ppermute x7, waiting for transfers between devices, shards(): lax.ppermute(c_own, ALL, moved(*step))  6.82 us
    pallas_call x1, Pallas kernels, c_grad_call(): pl.pallas_call(c_grad_kernel, grid=(GROUPS,), out_shape=pltpu.VMEM((LIVE,...  5.98 us
    pallas_call x1, Pallas kernels, scan_grad_call(): pl.pallas_call(scan_grad_kernel, grid=(GROUPS,), out_shape=jax.ShapeDtype...  5.69 us
    ppermute x1, starting transfers between devices, shards(): weight_sum = lax.ppermute(weight_sum, ALL, HOME)  5.5 us
  transfers between devices with their start and end apart: 19, of which 5 were waited for; matrix products, arithmetic and copies ran while one was open for 0% of the time, Pallas kernels for 17%

profile of v5, /device:TPU:5, one launch (start us, length us, event | category | flops | bytes accessed | tf_op | source)
XLA Modules:
  0.0 103.7 jit_solution(8036695475932571103)
XLA Ops:
  0.6 2.7 %pack.1 = bf16[8,96,1024]{2,1,0:T(8,128)(2,1)} custom-call(bf16[128,8192]{1,0:T(8,128)(2,1)} %s_ref.1), custom_call_target="tpu_custom_call" | custom-call | bytes 3145728 | tf_op jit(solution)/shard_map/pack/pallas_call | solution.py:107
  3.3 6.7 %all-to-all-start = ((bf16[8,96,1024]{2,1,0:T(8,128)(2,1)}), bf16[8,96,1024]{2,1,0:T(8,128)(2,1)S(1)}, u32[]{:S(2)}, u32[]{:S(2)}) async-start(bf16[8,96,1024]{2,1,0:T(8,128)(2,1)} %pack.1), calls=%async_computation | async-start | bytes 3145728 | tf_op jit(solution)/shard_map/all_to_all | solution.py:72
  10.0 6.0 %c_grad.1.refs_0_ = bf16[96,512]{1,0:T(8,128)(2,1)S(1)} custom-call(s32[1,32]{1,0:T(1,128)} %bitcast.6, s32[32,32]{1,0:T(8,128)} %bitcast.4, f32[1,128]{1,0:T(1,128)} %bitcast.8, s32[1,128]{1,0:T(1,128)} %bitcast.10, f32[128,128]{1,0:T(8,128)} %step_ref.2, bf16[128,8192]{1,0:T(8,128)(2,1)} %g_ref.3, bf16[128,8192]{1,0:T(8,128)(2,1)} %x_ref.1, ...), custom_call_target="tpu_custom_call" | custom-call | flops 402653184 | bytes 4194304 | tf_op jit(solution)/shard_map/c_grad/pallas_call | solution.py:206
  16.0 0.4 collective-permute-start.6
  16.4 1.2 %collective-permute-start.5 = (bf16[96,512]{1,0:T(8,128)(2,1)S(1)}, bf16[96,512]{1,0:T(8,128)(2,1)S(1)}, u32[]{:S(2)}, u32[]{:S(2)}) collective-permute-start(bf16[96,512]{1,0:T(8,128)(2,1)S(1)} %c_grad.1.refs_0_), channel_id=1, source_target_pairs={{0,1},{8,9},{16,17},{24,25},{32,33},{40,41},{48,49},{56,57},{64,65... | collective-permute-start | bytes 294920 | tf_op jit(solution)/shard_map/ppermute | solution.py:534
  17.6 2.4 %collective-permute-start.4 = (bf16[96,512]{1,0:T(8,128)(2,1)S(1)}, bf16[96,512]{1,0:T(8,128)(2,1)S(1)}, u32[]{:S(2)}, u32[]{:S(2)}) collective-permute-start(bf16[96,512]{1,0:T(8,128)(2,1)S(1)} %c_grad.1.refs_0_), channel_id=1, source_target_pairs={{0,132},{8,140},{16,148},{24,156},{32,164},{40,172},{48,180},{56,1... | collective-permute-start | bytes 294920 | tf_op jit(solution)/shard_map/ppermute | solution.py:534
  20.2 3.3 %collective-permute-start.2 = (bf16[96,512]{1,0:T(8,128)(2,1)S(1)}, bf16[96,512]{1,0:T(8,128)(2,1)S(1)}, u32[]{:S(2)}, u32[]{:S(2)}) collective-permute-start(bf16[96,512]{1,0:T(8,128)(2,1)S(1)} %c_grad.1.refs_0_), channel_id=1, source_target_pairs={{0,133},{8,141},{16,149},{24,157},{32,165},{40,173},{48,181},{56,1... | collective-permute-start | bytes 294920 | tf_op jit(solution)/shard_map/ppermute | solution.py:534
  23.5 6.4 %collective-permute-done.6.refs_7_ = bf16[96,512]{1,0:T(8,128)(2,1)S(1)} collective-permute-done((bf16[96,512]{1,0:T(8,128)(2,1)S(1)}, bf16[96,512]{1,0:T(8,128)(2,1)S(1)}, u32[]{:S(2)}, u32[]{:S(2)}) %collective-permute-start.6) | collective-permute-done | bytes 98336 | tf_op jit(solution)/shard_map/ppermute | solution.py:534
  29.9 0.7 collective-permute-start.1
  30.6 0.4 collective-permute-done.5.refs_6_
  31.0 3.9 %collective-permute-start = (bf16[96,512]{1,0:T(8,128)(2,1)S(1)}, bf16[96,512]{1,0:T(8,128)(2,1)S(1)}, u32[]{:S(2)}, u32[]{:S(2)}) collective-permute-start(bf16[96,512]{1,0:T(8,128)(2,1)S(1)} %c_grad.1.refs_0_), channel_id=1, source_target_pairs={{0,134},{8,142},{16,150},{24,158},{32,166},{40,174},{48,182},{56,1... | collective-permute-start | bytes 294920 | tf_op jit(solution)/shard_map/ppermute | solution.py:534
  35.0 2.3 %tables.1.tables_ref = f32[4,128,128]{2,1,0:T(8,128)} custom-call(s32[1,32]{1,0:T(1,128)} %bitcast.7, s32[32,32]{1,0:T(8,128)} %bitcast.5, f32[1,128]{1,0:T(1,128)} %bitcast.9, s32[1,128]{1,0:T(1,128)} %bitcast.11, f32[128,128]{1,0:T(8,128)} %step_ref.2), custom_call_target="tpu_custom_call" | custom-call | bytes 524288 | tf_op jit(solution)/shard_map/tables/pallas_call | solution.py:248
  37.2 1.0 c_proj.1.proj_ref
  38.3 1.9 %weight_part.1 = (f32[16,32,512]{2,1,0:T(8,128)S(1)}, bf16[16,32,512]{2,1,0:T(8,128)(2,1)S(1)}, bf16[8,96,512]{2,1,0:T(8,128)(2,1)S(1)}) custom-call(bf16[8,96,1024]{2,1,0:T(8,128)(2,1)S(1)} %all-to-all-done.s_ref, bf16[96,512]{1,0:T(8,128)(2,1)S(1)} %c_grad.1.refs_0_, bf16[96,512]{1,0:T(8,128)(2,1)S(1)} %collective-permute-done.refs_1_, ...), custom_call_target="tpu_custom_call" | custom-call | flops 805306368 | bytes 5242880 | tf_op jit(solution)/shard_map/weight_part/pallas_call | solution.py:359
  40.2 4.3 %collective-permute-start.7 = (bf16[16,32,512]{2,1,0:T(8,128)(2,1)S(1)}, bf16[16,32,512]{2,1,0:T(8,128)(2,1)S(1)}, u32[]{:S(2)}, u32[]{:S(2)}) collective-permute-start(bf16[16,32,512]{2,1,0:T(8,128)(2,1)S(1)} %get-tuple-element.44), channel_id=1, source_target_pairs={{0,8},{8,0},{16,24},{24,16},{32,40},{40,32},{48,56},{56,48},{64,72... | collective-permute-start | bytes 1572872 | tf_op jit(solution)/shard_map/ppermute | solution.py:76
  44.5 2.3 %project.1 = (bf16[96,1536]{1,0:T(8,128)(2,1)S(1)}, bf16[96,1536]{1,0:T(8,128)(2,1)}, bf16[96,1536]{1,0:T(8,128)(2,1)}, bf16[96,1536]{1,0:T(8,128)(2,1)}, bf16[9...) custom-call(bf16[1024,512]{1,0:T(8,128)(2,1)S(1)} %copy-done, ...), custom_call_target="tpu_custom_call" | custom-call | flops 805306368 | bytes 6291456 | tf_op jit(solution)/shard_map/project/pallas_call | solution.py:432
  46.8 1.0 add_convert_fusion
  47.7 8.3 %all-to-all-start.1 = ((bf16[16,32,512]{2,1,0:T(8,128)(2,1)}), bf16[16,32,512]{2,1,0:T(8,128)(2,1)S(1)}, u32[]{:S(2)}, u32[]{:S(2)}) async-start(bf16[16,32,512]{2,1,0:T(8,128)(2,1)} %add_convert_fusion), calls=%async_computation.1 | async-start | bytes 1048576 | tf_op jit(solution)/shard_map/all_to_all | solution.py:545
  56.1 5.4 %collective-permute-start.9 = (bf16[96,1536]{1,0:T(8,128)(2,1)}, bf16[96,1536]{1,0:T(8,128)(2,1)S(1)}, u32[]{:S(2)}, u32[]{:S(2)}) collective-permute-start(bf16[96,1536]{1,0:T(8,128)(2,1)} %get-tuple-element.55), channel_id=1, source_target_pairs={{0,134},{8,142},{16,150},{24,158},{32,166},{40,174},{48,182},{56,1... | collective-permute-start | bytes 884744 | tf_op jit(solution)/shard_map/ppermute | solution.py:547
  61.4 0.4 collective-permute-start.10
  61.9 0.5 collective-permute-start.11
  62.3 3.1 %collective-permute-start.12 = (bf16[96,1536]{1,0:T(8,128)(2,1)}, bf16[96,1536]{1,0:T(8,128)(2,1)S(1)}, u32[]{:S(2)}, u32[]{:S(2)}) collective-permute-start(bf16[96,1536]{1,0:T(8,128)(2,1)} %get-tuple-element.58), channel_id=1, source_target_pairs={{0,135},{8,143},{16,151},{24,159},{32,167},{40,175},{48,183},{56,1... | collective-permute-start | bytes 884744 | tf_op jit(solution)/shard_map/ppermute | solution.py:547
  65.4 0.3 collective-permute-start.13
  65.8 4.7 %all-to-all-done.1.parts_ref = bf16[16,32,512]{2,1,0:T(8,128)(2,1)S(1)} async-done(((bf16[16,32,512]{2,1,0:T(8,128)(2,1)}), bf16[16,32,512]{2,1,0:T(8,128)(2,1)S(1)}, u32[]{:S(2)}, u32[]{:S(2)}) %all-to-all-start.1) | async-done | bytes 524320 | tf_op jit(solution)/shard_map/all_to_all | solution.py:545
  70.5 0.9 peaks.1
  71.4 1.1 %collective-permute-start.14 = (bf16[96,1536]{1,0:T(8,128)(2,1)S(1)}, bf16[96,1536]{1,0:T(8,128)(2,1)S(1)}, u32[]{:S(2)}, u32[]{:S(2)}) collective-permute-start(bf16[96,1536]{1,0:T(8,128)(2,1)S(1)} %copy-done.2), channel_id=1, source_target_pairs={{0,1},{8,9},{16,17},{24,25},{32,33},{40,41},{48,49},{56,57},{64,65... | collective-permute-start | bytes 884744 | tf_op jit(solution)/shard_map/ppermute | solution.py:547
  72.5 2.4 %collective-permute-done.10.refs_2_ = bf16[96,1536]{1,0:T(8,128)(2,1)S(1)} collective-permute-done((bf16[96,1536]{1,0:T(8,128)(2,1)}, bf16[96,1536]{1,0:T(8,128)(2,1)S(1)}, u32[]{:S(2)}, u32[]{:S(2)}) %collective-permute-start.10) | collective-permute-done | bytes 294944 | tf_op jit(solution)/shard_map/ppermute | solution.py:547
  75.1 13.5 %all-to-all-start.2 = ((f32[256,1,128]{2,1,0:T(1,128)}), f32[256,1,128]{2,1,0:T(1,128)S(1)}, u32[]{:S(2)}, u32[]{:S(2)}) async-start(f32[256,1,128]{2,1,0:T(1,128)} %get-tuple-element.50), calls=%async_computation.2 | async-start | bytes 262144 | tf_op jit(solution)/shard_map/all_to_all | solution.py:72
  88.6 5.5 %collective-permute-start.8 = (f32[32,512]{1,0:T(8,128)S(1)}, f32[32,512]{1,0:T(8,128)S(1)}, u32[]{:S(2)}, u32[]{:S(2)}) collective-permute-start(f32[32,512]{1,0:T(8,128)S(1)} %get-tuple-element.53), channel_id=1, source_target_pairs={{80,0},{88,8},{64,16},{72,24},{96,1},{104,9},{48,17},{56,25},{0,2}... | collective-permute-start | bytes 196616 | tf_op jit(solution)/shard_map/ppermute | solution.py:552
  94.1 1.5 %collective-permute-done.14.refs_6_ = bf16[96,1536]{1,0:T(8,128)(2,1)S(1)} collective-permute-done((bf16[96,1536]{1,0:T(8,128)(2,1)S(1)}, bf16[96,1536]{1,0:T(8,128)(2,1)S(1)}, u32[]{:S(2)}, u32[]{:S(2)}) %collective-permute-start.14) | collective-permute-done | bytes 294944 | tf_op jit(solution)/shard_map/ppermute | solution.py:547
  95.6 5.7 %scan_grad.1 = bf16[128,8192]{1,0:T(8,128)(2,1)} custom-call(f32[128]{0:T(128)} %skip_ref.1, f32[4,128,128]{2,1,0:T(8,128)} %tables.1.tables_ref, bf16[128,8192]{1,0:T(8,128)(2,1)} %g_ref.3, bf16[128,512]{1,0:T(8,128)(2,1)} %b_ref.3, bf16[96,1536]{1,0:T(8,128)(2,1)S(1)} %get-tuple-element.54.refs_0_, bf16[96,1536]{1,0:T(8,128)(2,1)S(1)} %collective-permute-done.9.refs_1_, ...), custom_call_target="tpu_custom_call" | custom-call | flops 402653184 | bytes 4194304 | tf_op jit(solution)/shard_map/scan_grad/pallas_call | solution.py:301
  101.3 2.2 %finish.1 = (bf16[128,8192]{1,0:T(8,128)(2,1)}, f32[32,512]{1,0:T(8,128)}) custom-call(f32[256,1,128]{2,1,0:T(1,128)S(1)} %all-to-all-done.2.tops_ref, f32[32,512]{1,0:T(8,128)S(1)} %collective-permute-done.8.sum_ref, bf16[96,1536]{1,0:T(8,128)(2,1)S(1)} %get-tuple-element.54.refs_0_, bf16[96,1536]{1,0:T(8,128)(2,1)S(1)} %collective-permute-done.9.refs_1_, ...), custom_call_target="tpu_custom_call" | custom-call | flops 786432 | bytes 4194304 | tf_op jit(solution)/shard_map/finish/pallas_call | solution.py:496
  (24 shorter events, 0.5 us)
Async XLA Ops:
  3.3 33.9 %all-to-all-start = ((bf16[8,96,1024]{2,1,0:T(8,128)(2,1)}), bf16[8,96,1024]{2,1,0:T(8,128)(2,1)S(1)}, u32[]{:S(2)}, u32[]{:S(2)}) async-start(bf16[8,96,1024]{2,1,0:T(8,128)(2,1)} %pack.1), calls=%async_computation | async-start | bytes 3145728 | tf_op jit(solution)/shard_map/all_to_all | solution.py:72
  10.0 27.2 %copy-start = (bf16[1024,512]{1,0:T(8,128)(2,1)S(1)}, bf16[1024,512]{1,0:T(8,128)(2,1)}, u32[]{:S(2)}) copy-start(bf16[1024,512]{1,0:T(8,128)(2,1)} %w_ref.3) | copy-start | bytes 3145732
  16.0 13.9 %collective-permute-start.6 = (bf16[96,512]{1,0:T(8,128)(2,1)S(1)}, bf16[96,512]{1,0:T(8,128)(2,1)S(1)}, u32[]{:S(2)}, u32[]{:S(2)}) collective-permute-start(bf16[96,512]{1,0:T(8,128)(2,1)S(1)} %c_grad.1.refs_0_), channel_id=1, source_target_pairs={{0,3},{8,11},{16,19},{24,27},{32,35},{40,43},{48,51},{56,59},{64,6... | collective-permute-start | bytes 294920 | tf_op jit(solution)/shard_map/ppermute | solution.py:534
  16.4 14.7 %collective-permute-start.5 = (bf16[96,512]{1,0:T(8,128)(2,1)S(1)}, bf16[96,512]{1,0:T(8,128)(2,1)S(1)}, u32[]{:S(2)}, u32[]{:S(2)}) collective-permute-start(bf16[96,512]{1,0:T(8,128)(2,1)S(1)} %c_grad.1.refs_0_), channel_id=1, source_target_pairs={{0,1},{8,9},{16,17},{24,25},{32,33},{40,41},{48,49},{56,57},{64,65... | collective-permute-start | bytes 294920 | tf_op jit(solution)/shard_map/ppermute | solution.py:534
  17.6 20.7 %collective-permute-start.4 = (bf16[96,512]{1,0:T(8,128)(2,1)S(1)}, bf16[96,512]{1,0:T(8,128)(2,1)S(1)}, u32[]{:S(2)}, u32[]{:S(2)}) collective-permute-start(bf16[96,512]{1,0:T(8,128)(2,1)S(1)} %c_grad.1.refs_0_), channel_id=1, source_target_pairs={{0,132},{8,140},{16,148},{24,156},{32,164},{40,172},{48,180},{56,1... | collective-permute-start | bytes 294920 | tf_op jit(solution)/shard_map/ppermute | solution.py:534
  19.9 18.3 %collective-permute-start.3 = (bf16[96,512]{1,0:T(8,128)(2,1)S(1)}, bf16[96,512]{1,0:T(8,128)(2,1)S(1)}, u32[]{:S(2)}, u32[]{:S(2)}) collective-permute-start(bf16[96,512]{1,0:T(8,128)(2,1)S(1)} %c_grad.1.refs_0_), channel_id=1, source_target_pairs={{0,135},{8,143},{16,151},{24,159},{32,167},{40,175},{48,183},{56,1... | collective-permute-start | bytes 294920 | tf_op jit(solution)/shard_map/ppermute | solution.py:534
  20.2 18.0 %collective-permute-start.2 = (bf16[96,512]{1,0:T(8,128)(2,1)S(1)}, bf16[96,512]{1,0:T(8,128)(2,1)S(1)}, u32[]{:S(2)}, u32[]{:S(2)}) collective-permute-start(bf16[96,512]{1,0:T(8,128)(2,1)S(1)} %c_grad.1.refs_0_), channel_id=1, source_target_pairs={{0,133},{8,141},{16,149},{24,157},{32,165},{40,173},{48,181},{56,1... | collective-permute-start | bytes 294920 | tf_op jit(solution)/shard_map/ppermute | solution.py:534
  29.9 8.4 %collective-permute-start.1 = (bf16[96,512]{1,0:T(8,128)(2,1)S(1)}, bf16[96,512]{1,0:T(8,128)(2,1)S(1)}, u32[]{:S(2)}, u32[]{:S(2)}) collective-permute-start(bf16[96,512]{1,0:T(8,128)(2,1)S(1)} %c_grad.1.refs_0_), channel_id=1, source_target_pairs={{0,2},{8,10},{16,18},{24,26},{32,34},{40,42},{48,50},{56,58},{64,6... | collective-permute-start | bytes 294920 | tf_op jit(solution)/shard_map/ppermute | solution.py:534
  31.0 7.2 %collective-permute-start = (bf16[96,512]{1,0:T(8,128)(2,1)S(1)}, bf16[96,512]{1,0:T(8,128)(2,1)S(1)}, u32[]{:S(2)}, u32[]{:S(2)}) collective-permute-start(bf16[96,512]{1,0:T(8,128)(2,1)S(1)} %c_grad.1.refs_0_), channel_id=1, source_target_pairs={{0,134},{8,142},{16,150},{24,158},{32,166},{40,174},{48,182},{56,1... | collective-permute-start | bytes 294920 | tf_op jit(solution)/shard_map/ppermute | solution.py:534
  40.2 6.6 %collective-permute-start.7 = (bf16[16,32,512]{2,1,0:T(8,128)(2,1)S(1)}, bf16[16,32,512]{2,1,0:T(8,128)(2,1)S(1)}, u32[]{:S(2)}, u32[]{:S(2)}) collective-permute-start(bf16[16,32,512]{2,1,0:T(8,128)(2,1)S(1)} %get-tuple-element.44), channel_id=1, source_target_pairs={{0,8},{8,0},{16,24},{24,16},{32,40},{40,32},{48,56},{56,48},{64,72... | collective-permute-start | bytes 1572872 | tf_op jit(solution)/shard_map/ppermute | solution.py:76
  46.7 18.7 %copy-start.3 = (bf16[96,1536]{1,0:T(8,128)(2,1)S(1)}, bf16[96,1536]{1,0:T(8,128)(2,1)}, u32[]{:S(2)}) copy-start(bf16[96,1536]{1,0:T(8,128)(2,1)} %get-tuple-element.59) | copy-start | bytes 884740
  46.8 24.6 %copy-start.2 = (bf16[96,1536]{1,0:T(8,128)(2,1)S(1)}, bf16[96,1536]{1,0:T(8,128)(2,1)}, u32[]{:S(2)}) copy-start(bf16[96,1536]{1,0:T(8,128)(2,1)} %get-tuple-element.60) | copy-start | bytes 884740
  46.8 28.2 %copy-start.1 = (bf16[96,1536]{1,0:T(8,128)(2,1)S(1)}, bf16[96,1536]{1,0:T(8,128)(2,1)}, u32[]{:S(2)}) copy-start(bf16[96,1536]{1,0:T(8,128)(2,1)} %get-tuple-element.61) | copy-start | bytes 884740
  47.7 22.7 %all-to-all-start.1 = ((bf16[16,32,512]{2,1,0:T(8,128)(2,1)}), bf16[16,32,512]{2,1,0:T(8,128)(2,1)S(1)}, u32[]{:S(2)}, u32[]{:S(2)}) async-start(bf16[16,32,512]{2,1,0:T(8,128)(2,1)} %add_convert_fusion), calls=%async_computation.1 | async-start | bytes 1048576 | tf_op jit(solution)/shard_map/all_to_all | solution.py:545
  56.1 15.3 %collective-permute-start.9 = (bf16[96,1536]{1,0:T(8,128)(2,1)}, bf16[96,1536]{1,0:T(8,128)(2,1)S(1)}, u32[]{:S(2)}, u32[]{:S(2)}) collective-permute-start(bf16[96,1536]{1,0:T(8,128)(2,1)} %get-tuple-element.55), channel_id=1, source_target_pairs={{0,134},{8,142},{16,150},{24,158},{32,166},{40,174},{48,182},{56,1... | collective-permute-start | bytes 884744 | tf_op jit(solution)/shard_map/ppermute | solution.py:547
  61.4 13.5 %collective-permute-start.10 = (bf16[96,1536]{1,0:T(8,128)(2,1)}, bf16[96,1536]{1,0:T(8,128)(2,1)S(1)}, u32[]{:S(2)}, u32[]{:S(2)}) collective-permute-start(bf16[96,1536]{1,0:T(8,128)(2,1)} %get-tuple-element.56), channel_id=1, source_target_pairs={{0,2},{8,10},{16,18},{24,26},{32,34},{40,42},{48,50},{56,58},{64,6... | collective-permute-start | bytes 884744 | tf_op jit(solution)/shard_map/ppermute | solution.py:547
  61.9 26.8 %collective-permute-start.11 = (bf16[96,1536]{1,0:T(8,128)(2,1)}, bf16[96,1536]{1,0:T(8,128)(2,1)S(1)}, u32[]{:S(2)}, u32[]{:S(2)}) collective-permute-start(bf16[96,1536]{1,0:T(8,128)(2,1)} %get-tuple-element.57), channel_id=1, source_target_pairs={{0,133},{8,141},{16,149},{24,157},{32,165},{40,173},{48,181},{56,1... | collective-permute-start | bytes 884744 | tf_op jit(solution)/shard_map/ppermute | solution.py:547
  62.3 31.8 %collective-permute-start.12 = (bf16[96,1536]{1,0:T(8,128)(2,1)}, bf16[96,1536]{1,0:T(8,128)(2,1)S(1)}, u32[]{:S(2)}, u32[]{:S(2)}) collective-permute-start(bf16[96,1536]{1,0:T(8,128)(2,1)} %get-tuple-element.58), channel_id=1, source_target_pairs={{0,135},{8,143},{16,151},{24,159},{32,167},{40,175},{48,183},{56,1... | collective-permute-start | bytes 884744 | tf_op jit(solution)/shard_map/ppermute | solution.py:547
  65.4 28.7 %collective-permute-start.13 = (bf16[96,1536]{1,0:T(8,128)(2,1)S(1)}, bf16[96,1536]{1,0:T(8,128)(2,1)S(1)}, u32[]{:S(2)}, u32[]{:S(2)}) collective-permute-start(bf16[96,1536]{1,0:T(8,128)(2,1)S(1)} %copy-done.3), channel_id=1, source_target_pairs={{0,132},{8,140},{16,148},{24,156},{32,164},{40,172},{48,180},{56,1... | collective-permute-start | bytes 884744 | tf_op jit(solution)/shard_map/ppermute | solution.py:547
  71.4 24.2 %collective-permute-start.14 = (bf16[96,1536]{1,0:T(8,128)(2,1)S(1)}, bf16[96,1536]{1,0:T(8,128)(2,1)S(1)}, u32[]{:S(2)}, u32[]{:S(2)}) collective-permute-start(bf16[96,1536]{1,0:T(8,128)(2,1)S(1)} %copy-done.2), channel_id=1, source_target_pairs={{0,1},{8,9},{16,17},{24,25},{32,33},{40,41},{48,49},{56,57},{64,65... | collective-permute-start | bytes 884744 | tf_op jit(solution)/shard_map/ppermute | solution.py:547
  74.9 20.6 %collective-permute-start.15 = (bf16[96,1536]{1,0:T(8,128)(2,1)S(1)}, bf16[96,1536]{1,0:T(8,128)(2,1)S(1)}, u32[]{:S(2)}, u32[]{:S(2)}) collective-permute-start(bf16[96,1536]{1,0:T(8,128)(2,1)S(1)} %copy-done.1), channel_id=1, source_target_pairs={{0,3},{8,11},{16,19},{24,27},{32,35},{40,43},{48,51},{56,59},{64,6... | collective-permute-start | bytes 884744 | tf_op jit(solution)/shard_map/ppermute | solution.py:551
  75.1 26.2 %all-to-all-start.2 = ((f32[256,1,128]{2,1,0:T(1,128)}), f32[256,1,128]{2,1,0:T(1,128)S(1)}, u32[]{:S(2)}, u32[]{:S(2)}) async-start(f32[256,1,128]{2,1,0:T(1,128)} %get-tuple-element.50), calls=%async_computation.2 | async-start | bytes 262144 | tf_op jit(solution)/shard_map/all_to_all | solution.py:72
  88.6 12.7 %collective-permute-start.8 = (f32[32,512]{1,0:T(8,128)S(1)}, f32[32,512]{1,0:T(8,128)S(1)}, u32[]{:S(2)}, u32[]{:S(2)}) collective-permute-start(f32[32,512]{1,0:T(8,128)S(1)} %get-tuple-element.53), channel_id=1, source_target_pairs={{80,0},{88,8},{64,16},{72,24},{96,1},{104,9},{48,17},{56,25},{0,2}... | collective-permute-start | bytes 196616 | tf_op jit(solution)/shard_map/ppermute | solution.py:552

commit v6 on v5

--- a/solution.py
+++ b/solution.py
@@ -17,7 +17,10 @@
 MEMBERS = 8
 CHUNK = D // MEMBERS
 BOTH = NARROW + CHUNK
+HALF = BOTH // 2
 VMEM_LIMIT = 60 * 2**20
+C_STEP = 4
+SCAN_STEP = 2
 LOG2E = 1.4426950408889634
 ALL = ("dp", "fsdp")
 peak_eps = 1e-06
@@ -164,9 +167,9 @@
 def c_grad_kernel(
     kept_ref, sends_ref, rate_ref, doc_ref, step_ref, g_ref, x_ref, b_ref, out_ref, source_scr, totals_scr, bias_scr
 ):
-    q = pl.program_id(0)
-
-    @pl.when(q == 0)
+    step = pl.program_id(0)
+
+    @pl.when(step == 0)
     def _():
         totals, source = head_tables(rate_ref, step_ref)
         keep_tables(source_scr, totals_scr, source, totals)
@@ -174,23 +177,27 @@
         bias_scr[...] = row_mask(live_count(kept_ref, sends_ref), doc_ref, t, s)
 
     bias = bias_scr[...]
-    source = source_scr[group_rows(q), :]
-    totals_col = totals_scr[q]
     upper = lax.broadcasted_iota(jnp.int32, (128, ROWS), 0) < HDIM
-    mixing = jnp.zeros((LIVE, ROWS), F32)
-    for p in range(HPG // 2):
-        lanes = slice(p * 128, p * 128 + 128)
-        x_pair = x_ref[:, lanes]
-        zero = jnp.zeros_like(x_pair)
-        x_turned = jnp.transpose(x_pair)
-        both = jnp.concatenate([jnp.where(upper, x_turned, zero), jnp.where(upper, zero, x_turned)], axis=1)
-        inner = jnp.dot(g_ref[:, lanes], both, preferred_element_type=F32)
-        for k in range(2):
-            h = 2 * p + k
-            gap = (source[h : h + 1, :] - totals_col[:LIVE, h : h + 1]) + bias
-            mixing = mixing + jnp.exp2(gap) * inner[:, k * 128 : k * 128 + 128]
-    c_grad = jnp.dot(mixing.astype(BF16), b_ref[...], preferred_element_type=F32).astype(BF16)
-    out_ref[...] = c_grad
+    for k in range(C_STEP):
+        q = step * C_STEP + k
+        source = source_scr[group_rows(q), :]
+        totals_col = totals_scr[q]
+        mixing = jnp.zeros((LIVE, ROWS), F32)
+        for p in range(HPG // 2):
+            lanes = slice(k * HPG * HDIM + p * 128, k * HPG * HDIM + p * 128 + 128)
+            x_pair = x_ref[:, lanes]
+            zero = jnp.zeros_like(x_pair)
+            x_turned = jnp.transpose(x_pair)
+            both = jnp.concatenate([jnp.where(upper, x_turned, zero), jnp.where(upper, zero, x_turned)], axis=1)
+            inner = jnp.dot(g_ref[:, lanes], both, preferred_element_type=F32)
+            for i in range(2):
+                h = 2 * p + i
+                gap = (source[h : h + 1, :] - totals_col[:LIVE, h : h + 1]) + bias
+                mixing = mixing + jnp.exp2(gap) * inner[:, i * 128 : i * 128 + 128]
+        columns = slice(k * STATE, (k + 1) * STATE)
+        out_ref[:, columns] = jnp.dot(
+            mixing.astype(BF16), b_ref[:, columns], preferred_element_type=F32
+        ).astype(BF16)
 
 
 def smem():
@@ -202,10 +209,10 @@
 
 
 def c_grad_call(kept, sends, rate, docs, steps, out_grad, scan_input, b_factors):
-    wide = HPG * HDIM
+    wide, narrow = C_STEP * HPG * HDIM, C_STEP * STATE
     return pl.pallas_call(
         c_grad_kernel,
-        grid=(GROUPS,),
+        grid=(GROUPS // C_STEP,),
         out_shape=pltpu.VMEM((LIVE, NARROW), BF16),
         in_specs=[
             pl.BlockSpec((1, 32), lambda q: (0, 0)),
@@ -215,9 +222,9 @@
             pl.BlockSpec((HEADS, ROWS), lambda q: (0, 0)),
             pl.BlockSpec((LIVE, wide), lambda q: (0, q)),
             pl.BlockSpec((ROWS, wide), lambda q: (0, q)),
-            pl.BlockSpec((ROWS, STATE), lambda q: (0, q)),
+            pl.BlockSpec((ROWS, narrow), lambda q: (0, q)),
         ],
-        out_specs=pl.BlockSpec((LIVE, STATE), lambda q: (0, q)),
+        out_specs=pl.BlockSpec((LIVE, narrow), lambda q: (0, q)),
         scratch_shapes=[
             pltpu.VMEM((HEADS, ROWS), F32),
             pltpu.VMEM((GROUPS, ROWS, HEADS), F32),
@@ -257,10 +264,10 @@
 
 
 def scan_grad_kernel(skip_ref, tables_ref, g_ref, b_ref, *refs):
-    q = pl.program_id(0)
+    step = pl.program_id(0)
     proj_refs, (out_ref, source_scr) = refs[:MEMBERS], refs[MEMBERS:]
 
-    @pl.when(q == 0)
+    @pl.when(step == 0)
     def _():
         source = tables_ref[1]
         for k in range(GROUPS):
@@ -268,47 +275,50 @@
 
     bias = tables_ref[2, :LIVE, :]
     alive = tables_ref[3, :LIVE, :]
-    totals = tables_ref[0, group_rows(q), :]
-    source_col = source_scr[q]
     half = lax.broadcasted_iota(jnp.int32, (ROWS, 128), 1) < HDIM
-    c_proj = proj_refs[0][...].astype(F32)
-    for proj_ref in proj_refs[1:]:
-        c_proj = c_proj + proj_ref[...].astype(F32)
-    c_proj = jnp.concatenate([c_proj.astype(BF16), jnp.zeros((ROWS - LIVE, STATE), BF16)], axis=0)
-    affinity = lax.dot_general(
-        b_ref[:LIVE, :], c_proj, (((1,), (1,)), ((), ())), preferred_element_type=F32
-    )
-    for p in range(HPG // 2):
-        lanes = slice(p * 128, p * 128 + 128)
-        g_pair = g_ref[:, lanes]
-        zero = jnp.zeros_like(g_pair)
-        both = jnp.concatenate([jnp.where(half, g_pair, zero), jnp.where(half, zero, g_pair)], axis=0)
-        kernels = []
-        for k in range(2):
-            h = 2 * p + k
-            gap = (source_col[:LIVE, h : h + 1] - totals[h : h + 1, :]) + bias
-            kernels.append((jnp.exp2(gap) * affinity).astype(BF16))
-        grads = jnp.dot(jnp.concatenate(kernels, axis=1), both, preferred_element_type=F32)
-        first = q * HPG + 2 * p
-        gain = jnp.where(half[:LIVE], skip_ref[first], skip_ref[first + 1]) * alive
-        grads = grads + gain * g_pair[:LIVE].astype(F32)
-        out_ref[:LIVE, lanes] = grads.astype(BF16)
-    out_ref[LIVE:, :] = jnp.zeros((ROWS - LIVE, HPG * HDIM), BF16)
+    out_ref[LIVE:, :] = jnp.zeros((ROWS - LIVE, SCAN_STEP * HPG * HDIM), BF16)
+    for k in range(SCAN_STEP):
+        q = step * SCAN_STEP + k
+        totals = tables_ref[0, group_rows(q), :]
+        source_col = source_scr[q]
+        columns = slice(k * STATE, (k + 1) * STATE)
+        c_proj = proj_refs[0][:, columns].astype(F32)
+        for proj_ref in proj_refs[1:]:
+            c_proj = c_proj + proj_ref[:, columns].astype(F32)
+        c_proj = jnp.concatenate([c_proj.astype(BF16), jnp.zeros((ROWS - LIVE, STATE), BF16)], axis=0)
+        affinity = lax.dot_general(
+            b_ref[:LIVE, columns], c_proj, (((1,), (1,)), ((), ())), preferred_element_type=F32
+        )
+        for p in range(HPG // 2):
+            lanes = slice(k * HPG * HDIM + p * 128, k * HPG * HDIM + p * 128 + 128)
+            g_pair = g_ref[:, lanes]
+            zero = jnp.zeros_like(g_pair)
+            both = jnp.concatenate([jnp.where(half, g_pair, zero), jnp.where(half, zero, g_pair)], axis=0)
+            kernels = []
+            for i in range(2):
+                h = 2 * p + i
+                gap = (source_col[:LIVE, h : h + 1] - totals[h : h + 1, :]) + bias
+                kernels.append((jnp.exp2(gap) * affinity).astype(BF16))
+            grads = jnp.dot(jnp.concatenate(kernels, axis=1), both, preferred_element_type=F32)
+            first = q * HPG + 2 * p
+            gain = jnp.where(half[:LIVE], skip_ref[first], skip_ref[first + 1]) * alive
+            grads = grads + gain * g_pair[:LIVE].astype(F32)
+            out_ref[:LIVE, lanes] = grads.astype(BF16)
 
 
 def scan_grad_call(skip, tables, out_grad, b_factors, shares):
-    wide = HPG * HDIM
+    wide, narrow = SCAN_STEP * HPG * HDIM, SCAN_STEP * STATE
     return pl.pallas_call(
         scan_grad_kernel,
-        grid=(GROUPS,),
+        grid=(GROUPS // SCAN_STEP,),
         out_shape=jax.ShapeDtypeStruct((ROWS, D), BF16),
         in_specs=[
             smem(),
             pl.BlockSpec((4, ROWS, ROWS), lambda q: (0, 0, 0)),
             pl.BlockSpec((ROWS, wide), lambda q: (0, q)),
-            pl.BlockSpec((ROWS, STATE), lambda q: (0, q)),
+            pl.BlockSpec((ROWS, narrow), lambda q: (0, q)),
         ]
-        + [pl.BlockSpec((LIVE, STATE), lambda q: (0, q))] * MEMBERS,
+        + [pl.BlockSpec((LIVE, narrow), lambda q: (0, q))] * MEMBERS,
         out_specs=pl.BlockSpec((ROWS, wide), lambda q: (0, q)),
         scratch_shapes=[pltpu.VMEM((GROUPS, ROWS, HEADS), F32)],
         compiler_params=params(),
@@ -392,10 +402,17 @@
 
 
 def project_kernel(w_ref, proj_ref, grads, *refs):
-    out_refs, (top_ref, held, sems) = refs[:MEMBERS], refs[MEMBERS:]
+    out_refs, half_refs, (top_ref, held, sems) = refs[: MEMBERS - 1], refs[MEMBERS - 1 : MEMBERS + 1], refs[MEMBERS + 1 :]
     rows = MEMBERS * LIVE
     wide = 256
     dests = rows_at(1)
+    last_sems = [sems.at[k, MEMBERS - 1] for k in range(2)]
+    halves = [
+        pltpu.make_async_copy(
+            held.at[dests[-1], :, pl.ds(k * HALF, HALF)], half_refs[k], last_sems[k]
+        )
+        for k in range(2)
+    ]
     copies = []
     for k, (first, last) in enumerate(((0, NARROW + CHUNK // 2), (NARROW + CHUNK // 2, BOTH))):
         columns = pl.ds(first, last - first)
@@ -404,6 +421,7 @@
                 pltpu.make_async_copy(held.at[f, :, columns], ref.at[:, columns], sems.at[k, i])
                 for i, (ref, f) in enumerate(zip(out_refs, dests))
             ]
+            + halves[k : k + 1]
         )
     held[:, :, :NARROW] = proj_ref[...]
     top = jnp.zeros((8, wide), F32)
@@ -432,10 +450,11 @@
     out = pl.pallas_call(
         project_kernel,
         out_shape=[pltpu.VMEM((LIVE, BOTH), BF16)]
-        + [pltpu.HBM((LIVE, BOTH), BF16)] * (MEMBERS - 1)
+        + [pltpu.HBM((LIVE, BOTH), BF16)] * (MEMBERS - 2)
+        + [pltpu.HBM((LIVE, HALF), BF16)] * 2
         + [jax.ShapeDtypeStruct((1, 128), F32)],
         in_specs=[vmem] * 3,
-        out_specs=[pl.BlockSpec(memory_space=pl.ANY)] * MEMBERS + [vmem],
+        out_specs=[pl.BlockSpec(memory_space=pl.ANY)] * (MEMBERS + 1) + [vmem],
         scratch_shapes=[
             pltpu.VMEM((MEMBERS, LIVE, BOTH), BF16),
             pltpu.SemaphoreType.DMA((2, MEMBERS)),
@@ -446,7 +465,7 @@
         ),
         name="project",
     )(weights, proj, grads)
-    return out[:MEMBERS], out[MEMBERS]
+    return out[: MEMBERS + 1], out[MEMBERS + 1]
 
 
 def peak_kernel(parts_ref, top_ref, sum_ref, tops_ref):
@@ -476,13 +495,18 @@
 
 
 def finish_kernel(tops_ref, sum_ref, *refs):
-    back_refs, (input_ref, weight_ref, held, sems) = refs[:MEMBERS], refs[MEMBERS:]
+    back_refs, (input_ref, weight_ref, held, sems) = refs[: MEMBERS + 1], refs[MEMBERS + 1 :]
+    split = HALF - NARROW
     tops = jnp.max(tops_ref[...], axis=0)
     scale = 1.0 / (tops[:, :1] + peak_eps)
     held[:, LIVE:, :] = jnp.zeros((MEMBERS, ROWS - LIVE, CHUNK), BF16)
     copies = []
     for i, (ref, f) in enumerate(zip(back_refs, rows_at(-1))):
-        held[i, :LIVE] = (ref[:, NARROW:].astype(F32) * scale).astype(BF16)
+        if i < MEMBERS - 1:
+            held[i, :LIVE] = (ref[:, NARROW:].astype(F32) * scale).astype(BF16)
+        else:
+            held[i, :LIVE, :split] = (ref[:, NARROW:].astype(F32) * scale).astype(BF16)
+            held[i, :LIVE, split:] = (back_refs[MEMBERS][...].astype(F32) * scale).astype(BF16)
         columns = pl.ds(pl.multiple_of(f * CHUNK, CHUNK), CHUNK)
         copies.append(pltpu.make_async_copy(held.at[i], input_ref.at[:, columns], sems.at[i]))
         copies[-1].start()
@@ -499,7 +523,7 @@
             jax.ShapeDtypeStruct((ROWS, D), BF16),
             jax.ShapeDtypeStruct((32, NARROW), F32),
         ],
-        in_specs=[vmem] * (2 + MEMBERS),
+        in_specs=[vmem] * (3 + MEMBERS),
         out_specs=[pl.BlockSpec(memory_space=pl.ANY), vmem],
         scratch_shapes=[
             pltpu.VMEM((MEMBERS, ROWS, CHUNK), BF16),
@@ -548,10 +572,10 @@
     weight_sum, tops = peak_call(parts, top)
     weight_sum, *late = lax.optimization_barrier((weight_sum, *both[7:]))
     tops = exchange(tops, None)
-    back += [lax.ppermute(value, ALL, moved(*step)) for value, step in zip(late, STEPS[7:])]
+    back += [lax.ppermute(value, ALL, moved(*STEPS[7])) for value in late]
     weight_sum = lax.ppermute(weight_sum, ALL, HOME)
     both = [pltpu.with_memory_space_constraint(value, pltpu.VMEM) for value in back]
-    scan_grad = scan_grad_call(skip_gain, tables, out_grad, b_factors, both)
+    scan_grad = scan_grad_call(skip_gain, tables, out_grad, b_factors, both[:MEMBERS])
     input_grad, readout_weight_gradient = finish_call(tops, both, weight_sum)
     return (input_grad, scan_grad, readout_weight_gradient)
 

time: 105 us -> 104 us (level)
  starting transfers between devices: 61.5 us -> 63.2 us
  Pallas kernels: 24.8 us -> 23.7 us
  waiting for transfers between devices: 15.4 us -> 14.3 us
    all_to_all x1, waiting for transfers between devices: 4.73 us -> 1.29 us  [shards(): parts = lax.all_to_all(parts, 'dp', 0, 0, axis_index_groups=SAME_CORE)]
    ppermute x6, waiting for transfers between devices: 3.87 us -> 5.63 us  [shards(): lax.ppermute(both[i], ALL, moved(*STEPS[i]))]
    all_to_all x2, starting transfers between devices: 20.2 us -> 21.8 us  [exchange(): return lax.all_to_all(value, ALL, 0, 0, axis_index_groups=groups)]
    pallas_call x2, Pallas kernels: 11.7 us -> 10.5 us  [the longest x1 5.45 us: c_grad_call(): pl.pallas_call(c_grad_kernel, grid=(GROUPS // C_STEP,), out_shape=pltpu.V...]
  transfers between devices with their start and end apart: 19 -> 20, of which waited for: 5 -> 5; matrix products, arithmetic and copies ran while one was open for 0% -> 0% of each run, Pallas kernels for 17% -> 16%
where the time goes in v6:
time: 104 us; the launch traced here: 103 us
  starting transfers between devices  63.2 us (61%)
  Pallas kernels  23.7 us (23%)
  waiting for transfers between devices  14.3 us (14%)
    all_to_all x2, starting transfers between devices, exchange(): return lax.all_to_all(value, ALL, 0, 0, axis_index_groups=groups)  21.8 us
    ppermute x7, starting transfers between devices, shards(): lax.ppermute(c_own, ALL, moved(*step))  12.2 us
    ppermute x6, starting transfers between devices, shards(): lax.ppermute(both[i], ALL, moved(*STEPS[i]))  10.6 us
    all_to_all x1, starting transfers between devices, shards(): parts = lax.all_to_all(parts, 'dp', 0, 0, axis_index_groups=SAME_CORE)  8.29 us
    ppermute x7, waiting for transfers between devices, shards(): lax.ppermute(c_own, ALL, moved(*step))  7.37 us
    ppermute x6, waiting for transfers between devices, shards(): lax.ppermute(both[i], ALL, moved(*STEPS[i]))  5.63 us
    ppermute x1, starting transfers between devices, shards(): weight_sum = lax.ppermute(weight_sum, ALL, HOME)  5.58 us
    pallas_call x1, Pallas kernels, c_grad_call(): pl.pallas_call(c_grad_kernel, grid=(GROUPS // C_STEP,), out_shape=pltpu.V...  5.45 us
  transfers between devices with their start and end apart: 20, of which 5 were waited for; matrix products, arithmetic and copies ran while one was open for 0% of the time, Pallas kernels for 16%

profile of v6, /device:TPU:5, one launch (start us, length us, event | category | flops | bytes accessed | tf_op | source)
XLA Modules:
  0.0 103.1 jit_solution(7365550726239103834)
XLA Ops:
  0.6 2.7 %pack.1 = bf16[8,96,1024]{2,1,0:T(8,128)(2,1)} custom-call(bf16[128,8192]{1,0:T(8,128)(2,1)} %s_ref.1), custom_call_target="tpu_custom_call" | custom-call | bytes 3145728 | tf_op jit(solution)/shard_map/pack/pallas_call | solution.py:110
  3.3 6.7 %all-to-all-start = ((bf16[8,96,1024]{2,1,0:T(8,128)(2,1)}), bf16[8,96,1024]{2,1,0:T(8,128)(2,1)S(1)}, u32[]{:S(2)}, u32[]{:S(2)}) async-start(bf16[8,96,1024]{2,1,0:T(8,128)(2,1)} %pack.1), calls=%async_computation | async-start | bytes 3145728 | tf_op jit(solution)/shard_map/all_to_all | solution.py:75
  10.0 5.4 %c_grad.1.refs_0_ = bf16[96,512]{1,0:T(8,128)(2,1)S(1)} custom-call(s32[1,32]{1,0:T(1,128)} %bitcast.6, s32[32,32]{1,0:T(8,128)} %bitcast.4, f32[1,128]{1,0:T(1,128)} %bitcast.8, s32[1,128]{1,0:T(1,128)} %bitcast.10, f32[128,128]{1,0:T(8,128)} %step_ref.2, bf16[128,8192]{1,0:T(8,128)(2,1)} %g_ref.3, bf16[128,8192]{1,0:T(8,128)(2,1)} %x_ref.1, ...), custom_call_target="tpu_custom_call" | custom-call | flops 402653184 | bytes 4194304 | tf_op jit(solution)/shard_map/c_grad/pallas_call | solution.py:213
  15.5 0.3 collective-permute-start.6
  15.8 1.2 %collective-permute-start.5 = (bf16[96,512]{1,0:T(8,128)(2,1)S(1)}, bf16[96,512]{1,0:T(8,128)(2,1)S(1)}, u32[]{:S(2)}, u32[]{:S(2)}) collective-permute-start(bf16[96,512]{1,0:T(8,128)(2,1)S(1)} %c_grad.1.refs_0_), channel_id=1, source_target_pairs={{0,1},{8,9},{16,17},{24,25},{32,33},{40,41},{48,49},{56,57},{64,65... | collective-permute-start | bytes 294920 | tf_op jit(solution)/shard_map/ppermute | solution.py:558
  17.0 2.4 %collective-permute-start.4 = (bf16[96,512]{1,0:T(8,128)(2,1)S(1)}, bf16[96,512]{1,0:T(8,128)(2,1)S(1)}, u32[]{:S(2)}, u32[]{:S(2)}) collective-permute-start(bf16[96,512]{1,0:T(8,128)(2,1)S(1)} %c_grad.1.refs_0_), channel_id=1, source_target_pairs={{0,132},{8,140},{16,148},{24,156},{32,164},{40,172},{48,180},{56,1... | collective-permute-start | bytes 294920 | tf_op jit(solution)/shard_map/ppermute | solution.py:558
  19.7 3.3 %collective-permute-start.2 = (bf16[96,512]{1,0:T(8,128)(2,1)S(1)}, bf16[96,512]{1,0:T(8,128)(2,1)S(1)}, u32[]{:S(2)}, u32[]{:S(2)}) collective-permute-start(bf16[96,512]{1,0:T(8,128)(2,1)S(1)} %c_grad.1.refs_0_), channel_id=1, source_target_pairs={{0,133},{8,141},{16,149},{24,157},{32,165},{40,173},{48,181},{56,1... | collective-permute-start | bytes 294920 | tf_op jit(solution)/shard_map/ppermute | solution.py:558
  23.0 6.9 %collective-permute-done.6.refs_7_ = bf16[96,512]{1,0:T(8,128)(2,1)S(1)} collective-permute-done((bf16[96,512]{1,0:T(8,128)(2,1)S(1)}, bf16[96,512]{1,0:T(8,128)(2,1)S(1)}, u32[]{:S(2)}, u32[]{:S(2)}) %collective-permute-start.6) | collective-permute-done | bytes 98336 | tf_op jit(solution)/shard_map/ppermute | solution.py:558
  29.9 0.7 collective-permute-start.1
  30.6 0.4 collective-permute-done.5.refs_6_
  31.0 3.9 %collective-permute-start = (bf16[96,512]{1,0:T(8,128)(2,1)S(1)}, bf16[96,512]{1,0:T(8,128)(2,1)S(1)}, u32[]{:S(2)}, u32[]{:S(2)}) collective-permute-start(bf16[96,512]{1,0:T(8,128)(2,1)S(1)} %c_grad.1.refs_0_), channel_id=1, source_target_pairs={{0,134},{8,142},{16,150},{24,158},{32,166},{40,174},{48,182},{56,1... | collective-permute-start | bytes 294920 | tf_op jit(solution)/shard_map/ppermute | solution.py:558
  35.0 2.3 %tables.1.tables_ref = f32[4,128,128]{2,1,0:T(8,128)} custom-call(s32[1,32]{1,0:T(1,128)} %bitcast.7, s32[32,32]{1,0:T(8,128)} %bitcast.5, f32[1,128]{1,0:T(1,128)} %bitcast.9, s32[1,128]{1,0:T(1,128)} %bitcast.11, f32[128,128]{1,0:T(8,128)} %step_ref.2), custom_call_target="tpu_custom_call" | custom-call | bytes 524288 | tf_op jit(solution)/shard_map/tables/pallas_call | solution.py:255
  37.3 1.0 c_proj.1.proj_ref
  38.3 1.9 %weight_part.1 = (f32[16,32,512]{2,1,0:T(8,128)S(1)}, bf16[16,32,512]{2,1,0:T(8,128)(2,1)S(1)}, bf16[8,96,512]{2,1,0:T(8,128)(2,1)S(1)}) custom-call(bf16[8,96,1024]{2,1,0:T(8,128)(2,1)S(1)} %all-to-all-done.s_ref, bf16[96,512]{1,0:T(8,128)(2,1)S(1)} %c_grad.1.refs_0_, bf16[96,512]{1,0:T(8,128)(2,1)S(1)} %collective-permute-done.refs_1_, ...), custom_call_target="tpu_custom_call" | custom-call | flops 805306368 | bytes 5242880 | tf_op jit(solution)/shard_map/weight_part/pallas_call | solution.py:369
  40.2 4.3 %collective-permute-start.7 = (bf16[16,32,512]{2,1,0:T(8,128)(2,1)S(1)}, bf16[16,32,512]{2,1,0:T(8,128)(2,1)S(1)}, u32[]{:S(2)}, u32[]{:S(2)}) collective-permute-start(bf16[16,32,512]{2,1,0:T(8,128)(2,1)S(1)} %get-tuple-element.46), channel_id=1, source_target_pairs={{0,8},{8,0},{16,24},{24,16},{32,40},{40,32},{48,56},{56,48},{64,72... | collective-permute-start | bytes 1572872 | tf_op jit(solution)/shard_map/ppermute | solution.py:79
  44.5 2.3 %project.1 = (bf16[96,1536]{1,0:T(8,128)(2,1)S(1)}, bf16[96,1536]{1,0:T(8,128)(2,1)}, bf16[96,1536]{1,0:T(8,128)(2,1)}, bf16[96,1536]{1,0:T(8,128)(2,1)}, bf16[9...) custom-call(bf16[1024,512]{1,0:T(8,128)(2,1)S(1)} %copy-done, ...), custom_call_target="tpu_custom_call" | custom-call | flops 805306368 | bytes 6291456 | tf_op jit(solution)/shard_map/project/pallas_call | solution.py:450
  46.8 1.0 add_convert_fusion
  47.8 8.3 %all-to-all-start.1 = ((bf16[16,32,512]{2,1,0:T(8,128)(2,1)}), bf16[16,32,512]{2,1,0:T(8,128)(2,1)S(1)}, u32[]{:S(2)}, u32[]{:S(2)}) async-start(bf16[16,32,512]{2,1,0:T(8,128)(2,1)} %add_convert_fusion), calls=%async_computation.1 | async-start | bytes 1048576 | tf_op jit(solution)/shard_map/all_to_all | solution.py:569
  56.1 5.5 %collective-permute-start.9 = (bf16[96,1536]{1,0:T(8,128)(2,1)S(1)}, bf16[96,1536]{1,0:T(8,128)(2,1)S(1)}, u32[]{:S(2)}, u32[]{:S(2)}) collective-permute-start(bf16[96,1536]{1,0:T(8,128)(2,1)S(1)} %copy-done.3), channel_id=1, source_target_pairs={{0,134},{8,142},{16,150},{24,158},{32,166},{40,174},{48,182},{56,1... | collective-permute-start | bytes 884744 | tf_op jit(solution)/shard_map/ppermute | solution.py:571
  61.6 0.4 collective-permute-start.10
  62.0 0.4 collective-permute-start.11
  62.4 3.2 %collective-permute-start.12 = (bf16[96,1536]{1,0:T(8,128)(2,1)}, bf16[96,1536]{1,0:T(8,128)(2,1)S(1)}, u32[]{:S(2)}, u32[]{:S(2)}) collective-permute-start(bf16[96,1536]{1,0:T(8,128)(2,1)} %get-tuple-element.61), channel_id=1, source_target_pairs={{0,135},{8,143},{16,151},{24,159},{32,167},{40,175},{48,183},{56,1... | collective-permute-start | bytes 884744 | tf_op jit(solution)/shard_map/ppermute | solution.py:571
  65.9 2.5 %collective-permute-done.9.refs_1_ = bf16[96,1536]{1,0:T(8,128)(2,1)S(1)} collective-permute-done((bf16[96,1536]{1,0:T(8,128)(2,1)S(1)}, bf16[96,1536]{1,0:T(8,128)(2,1)S(1)}, u32[]{:S(2)}, u32[]{:S(2)}) %collective-permute-start.9) | collective-permute-done | bytes 294944 | tf_op jit(solution)/shard_map/ppermute | solution.py:571
  68.4 0.8 collective-permute-start.14
  69.2 1.3 %all-to-all-done.1.parts_ref = bf16[16,32,512]{2,1,0:T(8,128)(2,1)S(1)} async-done(((bf16[16,32,512]{2,1,0:T(8,128)(2,1)}), bf16[16,32,512]{2,1,0:T(8,128)(2,1)S(1)}, u32[]{:S(2)}, u32[]{:S(2)}) %all-to-all-start.1) | async-done | bytes 524320 | tf_op jit(solution)/shard_map/all_to_all | solution.py:569
  70.5 0.9 peaks.1
  71.4 15.1 %all-to-all-start.2 = ((f32[256,1,128]{2,1,0:T(1,128)}), f32[256,1,128]{2,1,0:T(1,128)S(1)}, u32[]{:S(2)}, u32[]{:S(2)}) async-start(f32[256,1,128]{2,1,0:T(1,128)} %get-tuple-element.52), calls=%async_computation.2 | async-start | bytes 262144 | tf_op jit(solution)/shard_map/all_to_all | solution.py:75
  86.5 0.4 collective-permute-start.15
  87.0 5.6 %collective-permute-start.8 = (f32[32,512]{1,0:T(8,128)S(1)}, f32[32,512]{1,0:T(8,128)S(1)}, u32[]{:S(2)}, u32[]{:S(2)}) collective-permute-start(f32[32,512]{1,0:T(8,128)S(1)} %get-tuple-element.56), channel_id=1, source_target_pairs={{80,0},{88,8},{64,16},{72,24},{96,1},{104,9},{48,17},{56,25},{0,2}... | collective-permute-start | bytes 196616 | tf_op jit(solution)/shard_map/ppermute | solution.py:576
  92.6 3.1 %collective-permute-done.14.refs_6_ = bf16[96,1536]{1,0:T(8,128)(2,1)S(1)} collective-permute-done((bf16[96,1536]{1,0:T(8,128)(2,1)S(1)}, bf16[96,1536]{1,0:T(8,128)(2,1)S(1)}, u32[]{:S(2)}, u32[]{:S(2)}) %collective-permute-start.14) | collective-permute-done | bytes 294944 | tf_op jit(solution)/shard_map/ppermute | solution.py:571
  95.7 5.0 %scan_grad.1 = bf16[128,8192]{1,0:T(8,128)(2,1)} custom-call(f32[128]{0:T(128)} %skip_ref.1, f32[4,128,128]{2,1,0:T(8,128)} %tables.1.tables_ref, bf16[128,8192]{1,0:T(8,128)(2,1)} %g_ref.3, bf16[128,512]{1,0:T(8,128)(2,1)} %b_ref.3, bf16[96,1536]{1,0:T(8,128)(2,1)S(1)} %get-tuple-element.57.refs_0_, bf16[96,1536]{1,0:T(8,128)(2,1)S(1)} %collective-permute-done.9.refs_1_, ...), custom_call_target="tpu_custom_call" | custom-call | flops 402653184 | bytes 4194304 | tf_op jit(solution)/shard_map/scan_grad/pallas_call | solution.py:311
  100.7 2.2 %finish.1 = (bf16[128,8192]{1,0:T(8,128)(2,1)}, f32[32,512]{1,0:T(8,128)}) custom-call(f32[256,1,128]{2,1,0:T(1,128)S(1)} %all-to-all-done.2.tops_ref, f32[32,512]{1,0:T(8,128)S(1)} %collective-permute-done.8.sum_ref, bf16[96,1536]{1,0:T(8,128)(2,1)S(1)} %get-tuple-element.57.refs_0_, bf16[96,1536]{1,0:T(8,128)(2,1)S(1)} %collective-permute-done.9.refs_1_, ...), custom_call_target="tpu_custom_call" | custom-call | flops 786432 | bytes 4194304 | tf_op jit(solution)/shard_map/finish/pallas_call | solution.py:520
  (30 shorter events, 0.8 us)
Async XLA Ops:
  3.3 33.9 %all-to-all-start = ((bf16[8,96,1024]{2,1,0:T(8,128)(2,1)}), bf16[8,96,1024]{2,1,0:T(8,128)(2,1)S(1)}, u32[]{:S(2)}, u32[]{:S(2)}) async-start(bf16[8,96,1024]{2,1,0:T(8,128)(2,1)} %pack.1), calls=%async_computation | async-start | bytes 3145728 | tf_op jit(solution)/shard_map/all_to_all | solution.py:75
  10.0 27.2 %copy-start = (bf16[1024,512]{1,0:T(8,128)(2,1)S(1)}, bf16[1024,512]{1,0:T(8,128)(2,1)}, u32[]{:S(2)}) copy-start(bf16[1024,512]{1,0:T(8,128)(2,1)} %w_ref.3) | copy-start | bytes 3145732
  15.5 14.4 %collective-permute-start.6 = (bf16[96,512]{1,0:T(8,128)(2,1)S(1)}, bf16[96,512]{1,0:T(8,128)(2,1)S(1)}, u32[]{:S(2)}, u32[]{:S(2)}) collective-permute-start(bf16[96,512]{1,0:T(8,128)(2,1)S(1)} %c_grad.1.refs_0_), channel_id=1, source_target_pairs={{0,3},{8,11},{16,19},{24,27},{32,35},{40,43},{48,51},{56,59},{64,6... | collective-permute-start | bytes 294920 | tf_op jit(solution)/shard_map/ppermute | solution.py:558
  15.8 15.2 %collective-permute-start.5 = (bf16[96,512]{1,0:T(8,128)(2,1)S(1)}, bf16[96,512]{1,0:T(8,128)(2,1)S(1)}, u32[]{:S(2)}, u32[]{:S(2)}) collective-permute-start(bf16[96,512]{1,0:T(8,128)(2,1)S(1)} %c_grad.1.refs_0_), channel_id=1, source_target_pairs={{0,1},{8,9},{16,17},{24,25},{32,33},{40,41},{48,49},{56,57},{64,65... | collective-permute-start | bytes 294920 | tf_op jit(solution)/shard_map/ppermute | solution.py:558
  17.0 21.3 %collective-permute-start.4 = (bf16[96,512]{1,0:T(8,128)(2,1)S(1)}, bf16[96,512]{1,0:T(8,128)(2,1)S(1)}, u32[]{:S(2)}, u32[]{:S(2)}) collective-permute-start(bf16[96,512]{1,0:T(8,128)(2,1)S(1)} %c_grad.1.refs_0_), channel_id=1, source_target_pairs={{0,132},{8,140},{16,148},{24,156},{32,164},{40,172},{48,180},{56,1... | collective-permute-start | bytes 294920 | tf_op jit(solution)/shard_map/ppermute | solution.py:558
  19.4 18.9 %collective-permute-start.3 = (bf16[96,512]{1,0:T(8,128)(2,1)S(1)}, bf16[96,512]{1,0:T(8,128)(2,1)S(1)}, u32[]{:S(2)}, u32[]{:S(2)}) collective-permute-start(bf16[96,512]{1,0:T(8,128)(2,1)S(1)} %c_grad.1.refs_0_), channel_id=1, source_target_pairs={{0,135},{8,143},{16,151},{24,159},{32,167},{40,175},{48,183},{56,1... | collective-permute-start | bytes 294920 | tf_op jit(solution)/shard_map/ppermute | solution.py:558
  19.7 18.6 %collective-permute-start.2 = (bf16[96,512]{1,0:T(8,128)(2,1)S(1)}, bf16[96,512]{1,0:T(8,128)(2,1)S(1)}, u32[]{:S(2)}, u32[]{:S(2)}) collective-permute-start(bf16[96,512]{1,0:T(8,128)(2,1)S(1)} %c_grad.1.refs_0_), channel_id=1, source_target_pairs={{0,133},{8,141},{16,149},{24,157},{32,165},{40,173},{48,181},{56,1... | collective-permute-start | bytes 294920 | tf_op jit(solution)/shard_map/ppermute | solution.py:558
  29.9 8.4 %collective-permute-start.1 = (bf16[96,512]{1,0:T(8,128)(2,1)S(1)}, bf16[96,512]{1,0:T(8,128)(2,1)S(1)}, u32[]{:S(2)}, u32[]{:S(2)}) collective-permute-start(bf16[96,512]{1,0:T(8,128)(2,1)S(1)} %c_grad.1.refs_0_), channel_id=1, source_target_pairs={{0,2},{8,10},{16,18},{24,26},{32,34},{40,42},{48,50},{56,58},{64,6... | collective-permute-start | bytes 294920 | tf_op jit(solution)/shard_map/ppermute | solution.py:558
  31.0 7.2 %collective-permute-start = (bf16[96,512]{1,0:T(8,128)(2,1)S(1)}, bf16[96,512]{1,0:T(8,128)(2,1)S(1)}, u32[]{:S(2)}, u32[]{:S(2)}) collective-permute-start(bf16[96,512]{1,0:T(8,128)(2,1)S(1)} %c_grad.1.refs_0_), channel_id=1, source_target_pairs={{0,134},{8,142},{16,150},{24,158},{32,166},{40,174},{48,182},{56,1... | collective-permute-start | bytes 294920 | tf_op jit(solution)/shard_map/ppermute | solution.py:558
  40.2 6.6 %collective-permute-start.7 = (bf16[16,32,512]{2,1,0:T(8,128)(2,1)S(1)}, bf16[16,32,512]{2,1,0:T(8,128)(2,1)S(1)}, u32[]{:S(2)}, u32[]{:S(2)}) collective-permute-start(bf16[16,32,512]{2,1,0:T(8,128)(2,1)S(1)} %get-tuple-element.46), channel_id=1, source_target_pairs={{0,8},{8,0},{16,24},{24,16},{32,40},{40,32},{48,56},{56,48},{64,72... | collective-permute-start | bytes 1572872 | tf_op jit(solution)/shard_map/ppermute | solution.py:79
  46.8 9.3 %copy-start.3 = (bf16[96,1536]{1,0:T(8,128)(2,1)S(1)}, bf16[96,1536]{1,0:T(8,128)(2,1)}, u32[]{:S(2)}) copy-start(bf16[96,1536]{1,0:T(8,128)(2,1)} %get-tuple-element.58) | copy-start | bytes 884740
  46.8 14.8 %copy-start.2 = (bf16[96,1536]{1,0:T(8,128)(2,1)S(1)}, bf16[96,1536]{1,0:T(8,128)(2,1)}, u32[]{:S(2)}) copy-start(bf16[96,1536]{1,0:T(8,128)(2,1)} %get-tuple-element.59) | copy-start | bytes 884740
  46.8 21.6 %copy-start.1 = (bf16[96,1536]{1,0:T(8,128)(2,1)S(1)}, bf16[96,1536]{1,0:T(8,128)(2,1)}, u32[]{:S(2)}) copy-start(bf16[96,1536]{1,0:T(8,128)(2,1)} %get-tuple-element.63) | copy-start | bytes 884740
  46.8 39.7 %copy-start.5 = (bf16[96,768]{1,0:T(8,128)(2,1)S(1)}, bf16[96,768]{1,0:T(8,128)(2,1)}, u32[]{:S(2)}) copy-start(bf16[96,768]{1,0:T(8,128)(2,1)} %get-tuple-element.64) | copy-start | bytes 442372
  46.8 40.1 %copy-start.4 = (bf16[96,768]{1,0:T(8,128)(2,1)S(1)}, bf16[96,768]{1,0:T(8,128)(2,1)}, u32[]{:S(2)}) copy-start(bf16[96,768]{1,0:T(8,128)(2,1)} %get-tuple-element.65) | copy-start | bytes 442372
  47.8 22.7 %all-to-all-start.1 = ((bf16[16,32,512]{2,1,0:T(8,128)(2,1)}), bf16[16,32,512]{2,1,0:T(8,128)(2,1)S(1)}, u32[]{:S(2)}, u32[]{:S(2)}) async-start(bf16[16,32,512]{2,1,0:T(8,128)(2,1)} %add_convert_fusion), calls=%async_computation.1 | async-start | bytes 1048576 | tf_op jit(solution)/shard_map/all_to_all | solution.py:569
  56.1 12.3 %collective-permute-start.9 = (bf16[96,1536]{1,0:T(8,128)(2,1)S(1)}, bf16[96,1536]{1,0:T(8,128)(2,1)S(1)}, u32[]{:S(2)}, u32[]{:S(2)}) collective-permute-start(bf16[96,1536]{1,0:T(8,128)(2,1)S(1)} %copy-done.3), channel_id=1, source_target_pairs={{0,134},{8,142},{16,150},{24,158},{32,166},{40,174},{48,182},{56,1... | collective-permute-start | bytes 884744 | tf_op jit(solution)/shard_map/ppermute | solution.py:571
  61.6 24.9 %collective-permute-start.10 = (bf16[96,1536]{1,0:T(8,128)(2,1)S(1)}, bf16[96,1536]{1,0:T(8,128)(2,1)S(1)}, u32[]{:S(2)}, u32[]{:S(2)}) collective-permute-start(bf16[96,1536]{1,0:T(8,128)(2,1)S(1)} %copy-done.2), channel_id=1, source_target_pairs={{0,2},{8,10},{16,18},{24,26},{32,34},{40,42},{48,50},{56,58},{64,6... | collective-permute-start | bytes 884744 | tf_op jit(solution)/shard_map/ppermute | solution.py:571
  62.0 24.9 %collective-permute-start.11 = (bf16[96,1536]{1,0:T(8,128)(2,1)}, bf16[96,1536]{1,0:T(8,128)(2,1)S(1)}, u32[]{:S(2)}, u32[]{:S(2)}) collective-permute-start(bf16[96,1536]{1,0:T(8,128)(2,1)} %get-tuple-element.60), channel_id=1, source_target_pairs={{0,133},{8,141},{16,149},{24,157},{32,165},{40,173},{48,181},{56,1... | collective-permute-start | bytes 884744 | tf_op jit(solution)/shard_map/ppermute | solution.py:571
  62.4 24.6 %collective-permute-start.12 = (bf16[96,1536]{1,0:T(8,128)(2,1)}, bf16[96,1536]{1,0:T(8,128)(2,1)S(1)}, u32[]{:S(2)}, u32[]{:S(2)}) collective-permute-start(bf16[96,1536]{1,0:T(8,128)(2,1)} %get-tuple-element.61), channel_id=1, source_target_pairs={{0,135},{8,143},{16,151},{24,159},{32,167},{40,175},{48,183},{56,1... | collective-permute-start | bytes 884744 | tf_op jit(solution)/shard_map/ppermute | solution.py:571
  65.6 27.0 %collective-permute-start.13 = (bf16[96,1536]{1,0:T(8,128)(2,1)}, bf16[96,1536]{1,0:T(8,128)(2,1)S(1)}, u32[]{:S(2)}, u32[]{:S(2)}) collective-permute-start(bf16[96,1536]{1,0:T(8,128)(2,1)} %get-tuple-element.62), channel_id=1, source_target_pairs={{0,132},{8,140},{16,148},{24,156},{32,164},{40,172},{48,180},{56,1... | collective-permute-start | bytes 884744 | tf_op jit(solution)/shard_map/ppermute | solution.py:571
  68.4 27.3 %collective-permute-start.14 = (bf16[96,1536]{1,0:T(8,128)(2,1)S(1)}, bf16[96,1536]{1,0:T(8,128)(2,1)S(1)}, u32[]{:S(2)}, u32[]{:S(2)}) collective-permute-start(bf16[96,1536]{1,0:T(8,128)(2,1)S(1)} %copy-done.1), channel_id=1, source_target_pairs={{0,1},{8,9},{16,17},{24,25},{32,33},{40,41},{48,49},{56,57},{64,65... | collective-permute-start | bytes 884744 | tf_op jit(solution)/shard_map/ppermute | solution.py:571
  71.4 29.3 %all-to-all-start.2 = ((f32[256,1,128]{2,1,0:T(1,128)}), f32[256,1,128]{2,1,0:T(1,128)S(1)}, u32[]{:S(2)}, u32[]{:S(2)}) async-start(f32[256,1,128]{2,1,0:T(1,128)} %get-tuple-element.52), calls=%async_computation.2 | async-start | bytes 262144 | tf_op jit(solution)/shard_map/all_to_all | solution.py:75
  86.5 9.2 %collective-permute-start.15 = (bf16[96,768]{1,0:T(8,128)(2,1)S(1)}, bf16[96,768]{1,0:T(8,128)(2,1)S(1)}, u32[]{:S(2)}, u32[]{:S(2)}) collective-permute-start(bf16[96,768]{1,0:T(8,128)(2,1)S(1)} %copy-done.5), channel_id=1, source_target_pairs={{0,3},{8,11},{16,19},{24,27},{32,35},{40,43},{48,51},{56,59},{64,6... | collective-permute-start | bytes 442376 | tf_op jit(solution)/shard_map/ppermute | solution.py:575
  86.9 13.8 %collective-permute-start.16 = (bf16[96,768]{1,0:T(8,128)(2,1)S(1)}, bf16[96,768]{1,0:T(8,128)(2,1)S(1)}, u32[]{:S(2)}, u32[]{:S(2)}) collective-permute-start(bf16[96,768]{1,0:T(8,128)(2,1)S(1)} %copy-done.4), channel_id=1, source_target_pairs={{0,3},{8,11},{16,19},{24,27},{32,35},{40,43},{48,51},{56,59},{64,6... | collective-permute-start | bytes 442376 | tf_op jit(solution)/shard_map/ppermute | solution.py:575
  87.0 13.7 %collective-permute-start.8 = (f32[32,512]{1,0:T(8,128)S(1)}, f32[32,512]{1,0:T(8,128)S(1)}, u32[]{:S(2)}, u32[]{:S(2)}) collective-permute-start(f32[32,512]{1,0:T(8,128)S(1)} %get-tuple-element.56), channel_id=1, source_target_pairs={{80,0},{88,8},{64,16},{72,24},{96,1},{104,9},{48,17},{56,25},{0,2}... | collective-permute-start | bytes 196616 | tf_op jit(solution)/shard_map/ppermute | solution.py:576

commit v7 on v6

--- a/solution.py
+++ b/solution.py
@@ -50,6 +50,7 @@
 
 
 STEPS = [(0, 0), (2, 1), (2, 0), (1, 1), (3, 1), (0, 1), (1, 0), (3, 0)]
+C_ORDER = (0, 5, 2, 1, 3, 4, 6, 7)
 CORE_SWAP = [(i, i ^ 1) for i in range(32)]
 SAME_CORE = [[l * 16 + z * 2 + c for l in (0, 1) for z in range(8)] for c in (0, 1)]
 AWAY = (3, 2, 0, 1)
@@ -331,8 +332,9 @@
 
 def weight_kernel(s_ref, *refs):
     c_refs, (keep_ref, send_ref, grads) = refs[:MEMBERS], refs[MEMBERS:]
-    for c_ref, f in zip(c_refs, rows_at(-1)):
-        grads[f] = c_ref[...]
+    rows = rows_at(-1)
+    for c_ref, i in zip(c_refs, C_ORDER):
+        grads[rows[i]] = c_ref[...]
     at = coordinates()
     first_core = at["core"] == 0
 
@@ -556,6 +558,7 @@
 
     c_own = c_grad_call(kept, sends, rate, docs, step_size, out_grad, scan_input, b_factors)
     grads = [c_own] + [lax.ppermute(c_own, ALL, moved(*step)) for step in STEPS[1:]]
+    grads = [grads[i] for i in C_ORDER]
 
     steps, c_own = lax.optimization_barrier((step_size, c_own))
     tables = tables_call(kept, sends, rate, docs, steps)

time: 104 us -> 101 us (0.971)
  starting transfers between devices: 63.2 us -> 55.7 us
  waiting for transfers between devices: 14.3 us -> 19.8 us
    ppermute x1, starting transfers between devices: 4.29 us -> 0.59 us  [to_core(): return lax.ppermute(value, 'dp', CORE_SWAP)]
    ppermute x7, waiting for transfers between devices: 7.37 us -> 10.6 us  [shards(): lax.ppermute(c_own, ALL, moved(*step))]
    ppermute x6, waiting for transfers between devices: 5.63 us -> 7.22 us  [shards(): lax.ppermute(both[i], ALL, moved(*STEPS[i]))]
    all_to_all x2, starting transfers between devices: 21.8 us -> 20.5 us  [exchange(): return lax.all_to_all(value, ALL, 0, 0, axis_index_groups=groups)]
    ppermute x6, starting transfers between devices: 10.6 us -> 9.49 us  [shards(): lax.ppermute(both[i], ALL, moved(*STEPS[i]))]
  transfers between devices with their start and end apart: 20 -> 20, of which waited for: 5 -> 8; matrix products, arithmetic and copies ran while one was open for 0% -> 0% of each run, Pallas kernels for 16% -> 17%
where the time goes in v7:
time: 101 us
  starting transfers between devices  55.7 us (55%)
  Pallas kernels  23.7 us (23%)
  waiting for transfers between devices  19.8 us (20%)
    all_to_all x2, starting transfers between devices, exchange(): return lax.all_to_all(value, ALL, 0, 0, axis_index_groups=groups)  20.5 us
    ppermute x7, starting transfers between devices, shards(): lax.ppermute(c_own, ALL, moved(*step))  11.6 us
    ppermute x7, waiting for transfers between devices, shards(): lax.ppermute(c_own, ALL, moved(*step))  10.6 us
    ppermute x6, starting transfers between devices, shards(): lax.ppermute(both[i], ALL, moved(*STEPS[i]))  9.49 us
    all_to_all x1, starting transfers between devices, shards(): parts = lax.all_to_all(parts, 'dp', 0, 0, axis_index_groups=SAME_CORE)  8.29 us
    ppermute x6, waiting for transfers between devices, shards(): lax.ppermute(both[i], ALL, moved(*STEPS[i]))  7.22 us
    pallas_call x1, Pallas kernels, c_grad_call(): pl.pallas_call(c_grad_kernel, grid=(GROUPS // C_STEP,), out_shape=pltpu.V...  5.45 us
    pallas_call x1, Pallas kernels, scan_grad_call(): pl.pallas_call(scan_grad_kernel, grid=(GROUPS // SCAN_STEP,), out_shape=j...  5.05 us
  transfers between devices with their start and end apart: 20, of which 8 were waited for; matrix products, arithmetic and copies ran while one was open for 0% of the time, Pallas kernels for 17%

profile of v7, /device:TPU:5, one launch (start us, length us, event | category | flops | bytes accessed | tf_op | source)
XLA Modules:
  0.0 101.1 jit_solution(1423605713384673023)
XLA Ops:
  0.6 2.7 %pack.1 = bf16[8,96,1024]{2,1,0:T(8,128)(2,1)} custom-call(bf16[128,8192]{1,0:T(8,128)(2,1)} %s_ref.1), custom_call_target="tpu_custom_call" | custom-call | bytes 3145728 | tf_op jit(solution)/shard_map/pack/pallas_call | solution.py:111
  3.3 6.7 %all-to-all-start = ((bf16[8,96,1024]{2,1,0:T(8,128)(2,1)}), bf16[8,96,1024]{2,1,0:T(8,128)(2,1)S(1)}, u32[]{:S(2)}, u32[]{:S(2)}) async-start(bf16[8,96,1024]{2,1,0:T(8,128)(2,1)} %pack.1), calls=%async_computation | async-start | bytes 3145728 | tf_op jit(solution)/shard_map/all_to_all | solution.py:76
  10.0 5.4 %c_grad.1.refs_0_ = bf16[96,512]{1,0:T(8,128)(2,1)S(1)} custom-call(s32[1,32]{1,0:T(1,128)} %bitcast.6, s32[32,32]{1,0:T(8,128)} %bitcast.4, f32[1,128]{1,0:T(1,128)} %bitcast.8, s32[1,128]{1,0:T(1,128)} %bitcast.10, f32[128,128]{1,0:T(8,128)} %step_ref.2, bf16[128,8192]{1,0:T(8,128)(2,1)} %g_ref.3, bf16[128,8192]{1,0:T(8,128)(2,1)} %x_ref.1, ...), custom_call_target="tpu_custom_call" | custom-call | flops 402653184 | bytes 4194304 | tf_op jit(solution)/shard_map/c_grad/pallas_call | solution.py:214
  15.8 1.2 %collective-permute-start.5 = (bf16[96,512]{1,0:T(8,128)(2,1)S(1)}, bf16[96,512]{1,0:T(8,128)(2,1)S(1)}, u32[]{:S(2)}, u32[]{:S(2)}) collective-permute-start(bf16[96,512]{1,0:T(8,128)(2,1)S(1)} %c_grad.1.refs_0_), channel_id=1, source_target_pairs={{0,1},{8,9},{16,17},{24,25},{32,33},{40,41},{48,49},{56,57},{64,65... | collective-permute-start | bytes 294920 | tf_op jit(solution)/shard_map/ppermute | solution.py:560
  17.0 2.4 %collective-permute-start.4 = (bf16[96,512]{1,0:T(8,128)(2,1)S(1)}, bf16[96,512]{1,0:T(8,128)(2,1)S(1)}, u32[]{:S(2)}, u32[]{:S(2)}) collective-permute-start(bf16[96,512]{1,0:T(8,128)(2,1)S(1)} %c_grad.1.refs_0_), channel_id=1, source_target_pairs={{0,135},{8,143},{16,151},{24,159},{32,167},{40,175},{48,183},{56,1... | collective-permute-start | bytes 294920 | tf_op jit(solution)/shard_map/ppermute | solution.py:560
  19.4 1.8 %collective-permute-start.3 = (bf16[96,512]{1,0:T(8,128)(2,1)S(1)}, bf16[96,512]{1,0:T(8,128)(2,1)S(1)}, u32[]{:S(2)}, u32[]{:S(2)}) collective-permute-start(bf16[96,512]{1,0:T(8,128)(2,1)S(1)} %c_grad.1.refs_0_), channel_id=1, source_target_pairs={{0,133},{8,141},{16,149},{24,157},{32,165},{40,173},{48,181},{56,1... | collective-permute-start | bytes 294920 | tf_op jit(solution)/shard_map/ppermute | solution.py:560
  21.2 2.7 %collective-permute-start.2 = (bf16[96,512]{1,0:T(8,128)(2,1)S(1)}, bf16[96,512]{1,0:T(8,128)(2,1)S(1)}, u32[]{:S(2)}, u32[]{:S(2)}) collective-permute-start(bf16[96,512]{1,0:T(8,128)(2,1)S(1)} %c_grad.1.refs_0_), channel_id=1, source_target_pairs={{0,134},{8,142},{16,150},{24,158},{32,166},{40,174},{48,182},{56,1... | collective-permute-start | bytes 294920 | tf_op jit(solution)/shard_map/ppermute | solution.py:560
  23.9 6.0 %collective-permute-done.6.refs_7_ = bf16[96,512]{1,0:T(8,128)(2,1)S(1)} collective-permute-done((bf16[96,512]{1,0:T(8,128)(2,1)S(1)}, bf16[96,512]{1,0:T(8,128)(2,1)S(1)}, u32[]{:S(2)}, u32[]{:S(2)}) %collective-permute-start.6) | collective-permute-done | bytes 98336 | tf_op jit(solution)/shard_map/ppermute | solution.py:560
  29.9 0.7 collective-permute-start.1
  31.0 2.4 %collective-permute-start = (bf16[96,512]{1,0:T(8,128)(2,1)S(1)}, bf16[96,512]{1,0:T(8,128)(2,1)S(1)}, u32[]{:S(2)}, u32[]{:S(2)}) collective-permute-start(bf16[96,512]{1,0:T(8,128)(2,1)S(1)} %c_grad.1.refs_0_), channel_id=1, source_target_pairs={{0,132},{8,140},{16,148},{24,156},{32,164},{40,172},{48,180},{56,1... | collective-permute-start | bytes 294920 | tf_op jit(solution)/shard_map/ppermute | solution.py:560
  33.4 2.3 %tables.1.tables_ref = f32[4,128,128]{2,1,0:T(8,128)} custom-call(s32[1,32]{1,0:T(1,128)} %bitcast.7, s32[32,32]{1,0:T(8,128)} %bitcast.5, f32[1,128]{1,0:T(1,128)} %bitcast.9, s32[1,128]{1,0:T(1,128)} %bitcast.11, f32[128,128]{1,0:T(8,128)} %step_ref.2), custom_call_target="tpu_custom_call" | custom-call | bytes 524288 | tf_op jit(solution)/shard_map/tables/pallas_call | solution.py:256
  35.7 1.0 c_proj.1.proj_ref
  36.7 1.8 %collective-permute-done.3.refs_4_ = bf16[96,512]{1,0:T(8,128)(2,1)S(1)} collective-permute-done((bf16[96,512]{1,0:T(8,128)(2,1)S(1)}, bf16[96,512]{1,0:T(8,128)(2,1)S(1)}, u32[]{:S(2)}, u32[]{:S(2)}) %collective-permute-start.3) | collective-permute-done | bytes 98336 | tf_op jit(solution)/shard_map/ppermute | solution.py:560
  38.5 2.4 %collective-permute-done.refs_1_ = bf16[96,512]{1,0:T(8,128)(2,1)S(1)} collective-permute-done((bf16[96,512]{1,0:T(8,128)(2,1)S(1)}, bf16[96,512]{1,0:T(8,128)(2,1)S(1)}, u32[]{:S(2)}, u32[]{:S(2)}) %collective-permute-start) | collective-permute-done | bytes 98336 | tf_op jit(solution)/shard_map/ppermute | solution.py:560
  40.9 1.9 %weight_part.1 = (f32[16,32,512]{2,1,0:T(8,128)S(1)}, bf16[16,32,512]{2,1,0:T(8,128)(2,1)S(1)}, bf16[8,96,512]{2,1,0:T(8,128)(2,1)S(1)}) custom-call(bf16[8,96,1024]{2,1,0:T(8,128)(2,1)S(1)} %all-to-all-done.s_ref, bf16[96,512]{1,0:T(8,128)(2,1)S(1)} %c_grad.1.refs_0_, bf16[96,512]{1,0:T(8,128)(2,1)S(1)} %collective-permute-done.refs_1_, ...), custom_call_target="tpu_custom_call" | custom-call | flops 805306368 | bytes 5242880 | tf_op jit(solution)/shard_map/weight_part/pallas_call | solution.py:371
  42.8 0.6 collective-permute-start.7
  43.4 2.3 %project.1 = (bf16[96,1536]{1,0:T(8,128)(2,1)S(1)}, bf16[96,1536]{1,0:T(8,128)(2,1)}, bf16[96,1536]{1,0:T(8,128)(2,1)}, bf16[96,1536]{1,0:T(8,128)(2,1)}, bf16[9...) custom-call(bf16[1024,512]{1,0:T(8,128)(2,1)S(1)} %copy-done, ...), custom_call_target="tpu_custom_call" | custom-call | flops 805306368 | bytes 6291456 | tf_op jit(solution)/shard_map/project/pallas_call | solution.py:452
  45.7 1.0 add_convert_fusion
  46.7 8.3 %all-to-all-start.1 = ((bf16[16,32,512]{2,1,0:T(8,128)(2,1)}), bf16[16,32,512]{2,1,0:T(8,128)(2,1)S(1)}, u32[]{:S(2)}, u32[]{:S(2)}) async-start(bf16[16,32,512]{2,1,0:T(8,128)(2,1)} %add_convert_fusion), calls=%async_computation.1 | async-start | bytes 1048576 | tf_op jit(solution)/shard_map/all_to_all | solution.py:572
  55.0 4.2 %collective-permute-start.9 = (bf16[96,1536]{1,0:T(8,128)(2,1)S(1)}, bf16[96,1536]{1,0:T(8,128)(2,1)S(1)}, u32[]{:S(2)}, u32[]{:S(2)}) collective-permute-start(bf16[96,1536]{1,0:T(8,128)(2,1)S(1)} %copy-done.3), channel_id=1, source_target_pairs={{0,134},{8,142},{16,150},{24,158},{32,166},{40,174},{48,182},{56,1... | collective-permute-start | bytes 884744 | tf_op jit(solution)/shard_map/ppermute | solution.py:574
  59.2 0.7 collective-permute-start.10
  59.9 0.8 collective-permute-start.11
  60.7 2.8 %collective-permute-start.12 = (bf16[96,1536]{1,0:T(8,128)(2,1)}, bf16[96,1536]{1,0:T(8,128)(2,1)S(1)}, u32[]{:S(2)}, u32[]{:S(2)}) collective-permute-start(bf16[96,1536]{1,0:T(8,128)(2,1)} %get-tuple-element.61), channel_id=1, source_target_pairs={{0,135},{8,143},{16,151},{24,159},{32,167},{40,175},{48,183},{56,1... | collective-permute-start | bytes 884744 | tf_op jit(solution)/shard_map/ppermute | solution.py:574
  64.0 3.0 %collective-permute-done.9.refs_1_ = bf16[96,1536]{1,0:T(8,128)(2,1)S(1)} collective-permute-done((bf16[96,1536]{1,0:T(8,128)(2,1)S(1)}, bf16[96,1536]{1,0:T(8,128)(2,1)S(1)}, u32[]{:S(2)}, u32[]{:S(2)}) %collective-permute-start.9) | collective-permute-done | bytes 294944 | tf_op jit(solution)/shard_map/ppermute | solution.py:574
  67.5 1.9 %all-to-all-done.1.parts_ref = bf16[16,32,512]{2,1,0:T(8,128)(2,1)S(1)} async-done(((bf16[16,32,512]{2,1,0:T(8,128)(2,1)}), bf16[16,32,512]{2,1,0:T(8,128)(2,1)S(1)}, u32[]{:S(2)}, u32[]{:S(2)}) %all-to-all-start.1) | async-done | bytes 524320 | tf_op jit(solution)/shard_map/all_to_all | solution.py:572
  69.4 0.9 peaks.1
  70.3 13.8 %all-to-all-start.2 = ((f32[256,1,128]{2,1,0:T(1,128)}), f32[256,1,128]{2,1,0:T(1,128)S(1)}, u32[]{:S(2)}, u32[]{:S(2)}) async-start(f32[256,1,128]{2,1,0:T(1,128)} %get-tuple-element.52), calls=%async_computation.2 | async-start | bytes 262144 | tf_op jit(solution)/shard_map/all_to_all | solution.py:76
  84.5 0.8 collective-permute-done.11.refs_3_
  85.3 4.9 %collective-permute-start.8 = (f32[32,512]{1,0:T(8,128)S(1)}, f32[32,512]{1,0:T(8,128)S(1)}, u32[]{:S(2)}, u32[]{:S(2)}) collective-permute-start(f32[32,512]{1,0:T(8,128)S(1)} %get-tuple-element.56), channel_id=1, source_target_pairs={{80,0},{88,8},{64,16},{72,24},{96,1},{104,9},{48,17},{56,25},{0,2}... | collective-permute-start | bytes 196616 | tf_op jit(solution)/shard_map/ppermute | solution.py:579
  90.2 3.4 %collective-permute-done.14.refs_6_ = bf16[96,1536]{1,0:T(8,128)(2,1)S(1)} collective-permute-done((bf16[96,1536]{1,0:T(8,128)(2,1)S(1)}, bf16[96,1536]{1,0:T(8,128)(2,1)S(1)}, u32[]{:S(2)}, u32[]{:S(2)}) %collective-permute-start.14) | collective-permute-done | bytes 294944 | tf_op jit(solution)/shard_map/ppermute | solution.py:574
  93.6 5.0 %scan_grad.1 = bf16[128,8192]{1,0:T(8,128)(2,1)} custom-call(f32[128]{0:T(128)} %skip_ref.1, f32[4,128,128]{2,1,0:T(8,128)} %tables.1.tables_ref, bf16[128,8192]{1,0:T(8,128)(2,1)} %g_ref.3, bf16[128,512]{1,0:T(8,128)(2,1)} %b_ref.3, bf16[96,1536]{1,0:T(8,128)(2,1)S(1)} %get-tuple-element.57.refs_0_, bf16[96,1536]{1,0:T(8,128)(2,1)S(1)} %collective-permute-done.9.refs_1_, ...), custom_call_target="tpu_custom_call" | custom-call | flops 402653184 | bytes 4194304 | tf_op jit(solution)/shard_map/scan_grad/pallas_call | solution.py:312
  98.7 2.2 %finish.1 = (bf16[128,8192]{1,0:T(8,128)(2,1)}, f32[32,512]{1,0:T(8,128)}) custom-call(f32[256,1,128]{2,1,0:T(1,128)S(1)} %all-to-all-done.2.tops_ref, f32[32,512]{1,0:T(8,128)S(1)} %collective-permute-done.8.sum_ref, bf16[96,1536]{1,0:T(8,128)(2,1)S(1)} %get-tuple-element.57.refs_0_, bf16[96,1536]{1,0:T(8,128)(2,1)S(1)} %collective-permute-done.9.refs_1_, ...), custom_call_target="tpu_custom_call" | custom-call | flops 786432 | bytes 4194304 | tf_op jit(solution)/shard_map/finish/pallas_call | solution.py:522
  (30 shorter events, 2.2 us)
Async XLA Ops:
  3.3 32.4 %all-to-all-start = ((bf16[8,96,1024]{2,1,0:T(8,128)(2,1)}), bf16[8,96,1024]{2,1,0:T(8,128)(2,1)S(1)}, u32[]{:S(2)}, u32[]{:S(2)}) async-start(bf16[8,96,1024]{2,1,0:T(8,128)(2,1)} %pack.1), calls=%async_computation | async-start | bytes 3145728 | tf_op jit(solution)/shard_map/all_to_all | solution.py:76
  10.0 25.7 %copy-start = (bf16[1024,512]{1,0:T(8,128)(2,1)S(1)}, bf16[1024,512]{1,0:T(8,128)(2,1)}, u32[]{:S(2)}) copy-start(bf16[1024,512]{1,0:T(8,128)(2,1)} %w_ref.3) | copy-start | bytes 3145732
  15.5 14.4 %collective-permute-start.6 = (bf16[96,512]{1,0:T(8,128)(2,1)S(1)}, bf16[96,512]{1,0:T(8,128)(2,1)S(1)}, u32[]{:S(2)}, u32[]{:S(2)}) collective-permute-start(bf16[96,512]{1,0:T(8,128)(2,1)S(1)} %c_grad.1.refs_0_), channel_id=1, source_target_pairs={{0,3},{8,11},{16,19},{24,27},{32,35},{40,43},{48,51},{56,59},{64,6... | collective-permute-start | bytes 294920 | tf_op jit(solution)/shard_map/ppermute | solution.py:560
  15.8 15.2 %collective-permute-start.5 = (bf16[96,512]{1,0:T(8,128)(2,1)S(1)}, bf16[96,512]{1,0:T(8,128)(2,1)S(1)}, u32[]{:S(2)}, u32[]{:S(2)}) collective-permute-start(bf16[96,512]{1,0:T(8,128)(2,1)S(1)} %c_grad.1.refs_0_), channel_id=1, source_target_pairs={{0,1},{8,9},{16,17},{24,25},{32,33},{40,41},{48,49},{56,57},{64,65... | collective-permute-start | bytes 294920 | tf_op jit(solution)/shard_map/ppermute | solution.py:560
  17.0 19.7 %collective-permute-start.4 = (bf16[96,512]{1,0:T(8,128)(2,1)S(1)}, bf16[96,512]{1,0:T(8,128)(2,1)S(1)}, u32[]{:S(2)}, u32[]{:S(2)}) collective-permute-start(bf16[96,512]{1,0:T(8,128)(2,1)S(1)} %c_grad.1.refs_0_), channel_id=1, source_target_pairs={{0,135},{8,143},{16,151},{24,159},{32,167},{40,175},{48,183},{56,1... | collective-permute-start | bytes 294920 | tf_op jit(solution)/shard_map/ppermute | solution.py:560
  19.4 19.1 %collective-permute-start.3 = (bf16[96,512]{1,0:T(8,128)(2,1)S(1)}, bf16[96,512]{1,0:T(8,128)(2,1)S(1)}, u32[]{:S(2)}, u32[]{:S(2)}) collective-permute-start(bf16[96,512]{1,0:T(8,128)(2,1)S(1)} %c_grad.1.refs_0_), channel_id=1, source_target_pairs={{0,133},{8,141},{16,149},{24,157},{32,165},{40,173},{48,181},{56,1... | collective-permute-start | bytes 294920 | tf_op jit(solution)/shard_map/ppermute | solution.py:560
  21.2 17.3 %collective-permute-start.2 = (bf16[96,512]{1,0:T(8,128)(2,1)S(1)}, bf16[96,512]{1,0:T(8,128)(2,1)S(1)}, u32[]{:S(2)}, u32[]{:S(2)}) collective-permute-start(bf16[96,512]{1,0:T(8,128)(2,1)S(1)} %c_grad.1.refs_0_), channel_id=1, source_target_pairs={{0,134},{8,142},{16,150},{24,158},{32,166},{40,174},{48,182},{56,1... | collective-permute-start | bytes 294920 | tf_op jit(solution)/shard_map/ppermute | solution.py:560
  29.9 8.6 %collective-permute-start.1 = (bf16[96,512]{1,0:T(8,128)(2,1)S(1)}, bf16[96,512]{1,0:T(8,128)(2,1)S(1)}, u32[]{:S(2)}, u32[]{:S(2)}) collective-permute-start(bf16[96,512]{1,0:T(8,128)(2,1)S(1)} %c_grad.1.refs_0_), channel_id=1, source_target_pairs={{0,2},{8,10},{16,18},{24,26},{32,34},{40,42},{48,50},{56,58},{64,6... | collective-permute-start | bytes 294920 | tf_op jit(solution)/shard_map/ppermute | solution.py:560
  31.0 9.9 %collective-permute-start = (bf16[96,512]{1,0:T(8,128)(2,1)S(1)}, bf16[96,512]{1,0:T(8,128)(2,1)S(1)}, u32[]{:S(2)}, u32[]{:S(2)}) collective-permute-start(bf16[96,512]{1,0:T(8,128)(2,1)S(1)} %c_grad.1.refs_0_), channel_id=1, source_target_pairs={{0,132},{8,140},{16,148},{24,156},{32,164},{40,172},{48,180},{56,1... | collective-permute-start | bytes 294920 | tf_op jit(solution)/shard_map/ppermute | solution.py:560
  42.8 2.9 %collective-permute-start.7 = (bf16[16,32,512]{2,1,0:T(8,128)(2,1)S(1)}, bf16[16,32,512]{2,1,0:T(8,128)(2,1)S(1)}, u32[]{:S(2)}, u32[]{:S(2)}) collective-permute-start(bf16[16,32,512]{2,1,0:T(8,128)(2,1)S(1)} %get-tuple-element.46), channel_id=1, source_target_pairs={{0,8},{8,0},{16,24},{24,16},{32,40},{40,32},{48,56},{56,48},{64,72... | collective-permute-start | bytes 1572872 | tf_op jit(solution)/shard_map/ppermute | solution.py:80
  45.7 9.3 %copy-start.3 = (bf16[96,1536]{1,0:T(8,128)(2,1)S(1)}, bf16[96,1536]{1,0:T(8,128)(2,1)}, u32[]{:S(2)}) copy-start(bf16[96,1536]{1,0:T(8,128)(2,1)} %get-tuple-element.58) | copy-start | bytes 884740
  45.7 13.5 %copy-start.2 = (bf16[96,1536]{1,0:T(8,128)(2,1)S(1)}, bf16[96,1536]{1,0:T(8,128)(2,1)}, u32[]{:S(2)}) copy-start(bf16[96,1536]{1,0:T(8,128)(2,1)} %get-tuple-element.59) | copy-start | bytes 884740
  45.7 21.4 %copy-start.1 = (bf16[96,1536]{1,0:T(8,128)(2,1)S(1)}, bf16[96,1536]{1,0:T(8,128)(2,1)}, u32[]{:S(2)}) copy-start(bf16[96,1536]{1,0:T(8,128)(2,1)} %get-tuple-element.63) | copy-start | bytes 884740
  45.7 38.4 %copy-start.5 = (bf16[96,768]{1,0:T(8,128)(2,1)S(1)}, bf16[96,768]{1,0:T(8,128)(2,1)}, u32[]{:S(2)}) copy-start(bf16[96,768]{1,0:T(8,128)(2,1)} %get-tuple-element.64) | copy-start | bytes 442372
  45.7 39.6 %copy-start.4 = (bf16[96,768]{1,0:T(8,128)(2,1)S(1)}, bf16[96,768]{1,0:T(8,128)(2,1)}, u32[]{:S(2)}) copy-start(bf16[96,768]{1,0:T(8,128)(2,1)} %get-tuple-element.65) | copy-start | bytes 442372
  46.7 22.7 %all-to-all-start.1 = ((bf16[16,32,512]{2,1,0:T(8,128)(2,1)}), bf16[16,32,512]{2,1,0:T(8,128)(2,1)S(1)}, u32[]{:S(2)}, u32[]{:S(2)}) async-start(bf16[16,32,512]{2,1,0:T(8,128)(2,1)} %add_convert_fusion), calls=%async_computation.1 | async-start | bytes 1048576 | tf_op jit(solution)/shard_map/all_to_all | solution.py:572
  55.0 12.0 %collective-permute-start.9 = (bf16[96,1536]{1,0:T(8,128)(2,1)S(1)}, bf16[96,1536]{1,0:T(8,128)(2,1)S(1)}, u32[]{:S(2)}, u32[]{:S(2)}) collective-permute-start(bf16[96,1536]{1,0:T(8,128)(2,1)S(1)} %copy-done.3), channel_id=1, source_target_pairs={{0,134},{8,142},{16,150},{24,158},{32,166},{40,174},{48,182},{56,1... | collective-permute-start | bytes 884744 | tf_op jit(solution)/shard_map/ppermute | solution.py:574
  59.2 24.9 %collective-permute-start.10 = (bf16[96,1536]{1,0:T(8,128)(2,1)S(1)}, bf16[96,1536]{1,0:T(8,128)(2,1)S(1)}, u32[]{:S(2)}, u32[]{:S(2)}) collective-permute-start(bf16[96,1536]{1,0:T(8,128)(2,1)S(1)} %copy-done.2), channel_id=1, source_target_pairs={{0,2},{8,10},{16,18},{24,26},{32,34},{40,42},{48,50},{56,58},{64,6... | collective-permute-start | bytes 884744 | tf_op jit(solution)/shard_map/ppermute | solution.py:574
  59.9 25.4 %collective-permute-start.11 = (bf16[96,1536]{1,0:T(8,128)(2,1)}, bf16[96,1536]{1,0:T(8,128)(2,1)S(1)}, u32[]{:S(2)}, u32[]{:S(2)}) collective-permute-start(bf16[96,1536]{1,0:T(8,128)(2,1)} %get-tuple-element.60), channel_id=1, source_target_pairs={{0,133},{8,141},{16,149},{24,157},{32,165},{40,173},{48,181},{56,1... | collective-permute-start | bytes 884744 | tf_op jit(solution)/shard_map/ppermute | solution.py:574
  60.7 24.6 %collective-permute-start.12 = (bf16[96,1536]{1,0:T(8,128)(2,1)}, bf16[96,1536]{1,0:T(8,128)(2,1)S(1)}, u32[]{:S(2)}, u32[]{:S(2)}) collective-permute-start(bf16[96,1536]{1,0:T(8,128)(2,1)} %get-tuple-element.61), channel_id=1, source_target_pairs={{0,135},{8,143},{16,151},{24,159},{32,167},{40,175},{48,183},{56,1... | collective-permute-start | bytes 884744 | tf_op jit(solution)/shard_map/ppermute | solution.py:574
  63.5 26.7 %collective-permute-start.13 = (bf16[96,1536]{1,0:T(8,128)(2,1)}, bf16[96,1536]{1,0:T(8,128)(2,1)S(1)}, u32[]{:S(2)}, u32[]{:S(2)}) collective-permute-start(bf16[96,1536]{1,0:T(8,128)(2,1)} %get-tuple-element.62), channel_id=1, source_target_pairs={{0,132},{8,140},{16,148},{24,156},{32,164},{40,172},{48,180},{56,1... | collective-permute-start | bytes 884744 | tf_op jit(solution)/shard_map/ppermute | solution.py:574
  67.0 26.6 %collective-permute-start.14 = (bf16[96,1536]{1,0:T(8,128)(2,1)S(1)}, bf16[96,1536]{1,0:T(8,128)(2,1)S(1)}, u32[]{:S(2)}, u32[]{:S(2)}) collective-permute-start(bf16[96,1536]{1,0:T(8,128)(2,1)S(1)} %copy-done.1), channel_id=1, source_target_pairs={{0,1},{8,9},{16,17},{24,25},{32,33},{40,41},{48,49},{56,57},{64,65... | collective-permute-start | bytes 884744 | tf_op jit(solution)/shard_map/ppermute | solution.py:574
  70.3 28.4 %all-to-all-start.2 = ((f32[256,1,128]{2,1,0:T(1,128)}), f32[256,1,128]{2,1,0:T(1,128)S(1)}, u32[]{:S(2)}, u32[]{:S(2)}) async-start(f32[256,1,128]{2,1,0:T(1,128)} %get-tuple-element.52), calls=%async_computation.2 | async-start | bytes 262144 | tf_op jit(solution)/shard_map/all_to_all | solution.py:76
  84.1 9.5 %collective-permute-start.15 = (bf16[96,768]{1,0:T(8,128)(2,1)S(1)}, bf16[96,768]{1,0:T(8,128)(2,1)S(1)}, u32[]{:S(2)}, u32[]{:S(2)}) collective-permute-start(bf16[96,768]{1,0:T(8,128)(2,1)S(1)} %copy-done.5), channel_id=1, source_target_pairs={{0,3},{8,11},{16,19},{24,27},{32,35},{40,43},{48,51},{56,59},{64,6... | collective-permute-start | bytes 442376 | tf_op jit(solution)/shard_map/ppermute | solution.py:578
  85.3 13.4 %collective-permute-start.16 = (bf16[96,768]{1,0:T(8,128)(2,1)S(1)}, bf16[96,768]{1,0:T(8,128)(2,1)S(1)}, u32[]{:S(2)}, u32[]{:S(2)}) collective-permute-start(bf16[96,768]{1,0:T(8,128)(2,1)S(1)} %copy-done.4), channel_id=1, source_target_pairs={{0,3},{8,11},{16,19},{24,27},{32,35},{40,43},{48,51},{56,59},{64,6... | collective-permute-start | bytes 442376 | tf_op jit(solution)/shard_map/ppermute | solution.py:578
  85.3 13.4 %collective-permute-start.8 = (f32[32,512]{1,0:T(8,128)S(1)}, f32[32,512]{1,0:T(8,128)S(1)}, u32[]{:S(2)}, u32[]{:S(2)}) collective-permute-start(f32[32,512]{1,0:T(8,128)S(1)} %get-tuple-element.56), channel_id=1, source_target_pairs={{80,0},{88,8},{64,16},{72,24},{96,1},{104,9},{48,17},{56,25},{0,2}... | collective-permute-start | bytes 196616 | tf_op jit(solution)/shard_map/ppermute | solution.py:579
